TPU v7x, 32 devices: a whole 2x2x4 slice. The times are simulated.
32 devices in a mesh: seq: 4 (over y, x), frame: 8 (over z, core).
Axes of the slice: x: 2, y: 2, z: 4, core: 2. Of those that a mesh axis runs over, the one named last changes fastest.
Arguments:
- value_grad: bfloat16 [8, 4096, 512], P('frame', 'seq'), may hold values from -6 to 6
- w_value: bfloat16 [8192, 512], P('seq'), may hold values from -0.25 to 0.25
- norm_gain: float32 [8192], P('seq'), may hold values from 0.1 to 1.9
- vis_pos: int32 [8, 128], P('frame'), may hold values from 0 to 4095, as said below
- frame_owner: int32 [8, 128, 1], P('frame'), may hold values from 0 to 7; in each aligned block of 128 rows (0 to 127, 128 to 255, ..., all dimensions but the last counted through in order) at most 32 rows name the same one
- ques_span: int32 [8, 2], P('frame'), may hold values from 0 to 32, as said below
- vis_proj: bfloat16 [8, 128, 8192], P('frame', None, 'seq')
- vis_resid: bfloat16 [8, 128, 8192], P('frame', None, 'seq'), may hold values from -6 to 6
- ques_hidden: bfloat16 [8, 32, 8192], P('frame', None, 'seq'), may hold values from -6 to 6
- w_down: bfloat16 [8192, 8192], P(None, 'seq'), may hold values from -0.0625 to 0.0625
- pre_owned: bfloat16 [8, 8192, 256], P('frame', 'seq'), may hold values from -6 to 6
Outputs:
- pre_grad: bfloat16 [8, 8192, 256], P('frame', 'seq')
- ques_grad: bfloat16 [8, 32, 8192], P('frame', None, 'seq')
Inputs may be any that keep to these rules, and one draw needn't show every extreme that they name: `vis_pos`: each row is distinct and increasing. `frame_owner`: in each sequence at most 32 visual tokens name the same owner. `ques_span`: column 1 is at least 1, and column 0 plus column 1 is at most 32.
All inputs are finite; a program needn't handle non-finite values.
Results may differ from a plain program's by a relative error of at most 0.015.
Values may be sent and summed in bfloat16 or wider, within the bound.
No kernel may reach another device: no remote copies, remote signals or barrier semaphores. Data moves between devices by JAX's collectives and lax.ppermute only.
A program may use at most 128 MiB of HBM per device.

v0:
```python
import functools
import math

import jax
import jax.numpy as jnp
from jax import lax
from jax.experimental import pallas as pl
from jax.experimental.pallas import tpu as pltpu
from jax.sharding import PartitionSpec as P

EPSILON = 1e-06
F32 = jnp.float32
BF16 = jnp.bfloat16
LANES = 128
MIB = 1024 * 1024
GRANT, LOAD_GRANT, PICK_GRANT = 40, 40, 63
HBM = pl.BlockSpec(memory_space=pltpu.HBM)
VMEM = pl.BlockSpec(memory_space=pltpu.VMEM)
ANY = pl.BlockSpec(memory_space=pl.ANY)


def call(
    kernel, out_shape, in_specs, scratch=(), aliases=None, out_specs=None, grant=GRANT, cost=1024
):
    return pl.pallas_call(
        kernel,
        out_shape=out_shape,
        in_specs=in_specs,
        out_specs=jax.tree.map(lambda _: VMEM, out_shape) if out_specs is None else out_specs,
        scratch_shapes=list(scratch),
        input_output_aliases=aliases or {},
        compiler_params=pltpu.CompilerParams(vmem_limit_bytes=grant * MIB),
        cost_estimate=pl.CostEstimate(flops=256 * cost, bytes_accessed=cost, transcendentals=0),
    )


class Chain:
    def __init__(self):
        self.last = []

    def call(
        self, kernel, out_shape, in_specs, scratch=(), aliases=None, out_specs=None, cost=1024
    ):
        given, made, linked = len(in_specs), len(out_shape), len(self.last)

        def run(*refs):
            outs = refs[given + linked :]
            outs[made][...] = jnp.zeros(outs[made].shape, F32)
            kernel(*refs[:given], *outs[:made], *outs[made + 1 :])

        out_specs = [VMEM] * made if out_specs is None else out_specs
        run_call = call(
            run,
            [*out_shape, shape((8, LANES), F32)],
            [*in_specs, *[VMEM] * linked],
            scratch,
            aliases,
            [*out_specs, VMEM],
            cost=cost,
        )

        def apply(*args):
            *results, token = run_call(*args, *self.last)
            self.last = [token]
            return results

        return apply


def shape(dims, dtype):
    return jax.ShapeDtypeStruct(dims, dtype)


def swap(value, axis, count, step):
    return lax.ppermute(value, axis, [(i, i ^ step) for i in range(count)])


def to_column(row):
    return jnp.transpose(jnp.broadcast_to(row, (LANES, row.shape[1])), (1, 0))


def pick_kernel(pieces, pos_hbm, rows_hbm, own_ref, pos, rows, sems):
    tokens, shard_len = pos.shape[1], rows.shape[0]
    size = shard_len // pieces
    head = pltpu.make_async_copy(pos_hbm, pos, sems.at[pieces])
    head.start()
    copies = []
    for piece in range(pieces):
        cut = pl.ds(piece * size, size)
        copies.append(
            pltpu.make_async_copy(rows_hbm.at[0, cut], rows.at[cut], sems.at[piece])
        )
        copies[-1].start()
    offset = lax.axis_index("seq") * shard_len
    head.wait()
    column = to_column(pos[...] - offset)
    lanes = lax.broadcasted_iota(jnp.int32, (tokens, LANES), 1)
    total = None
    for piece in range(pieces):
        select = jnp.concatenate(
            [
                jnp.where(column == lanes + at, 1.0, 0.0).astype(BF16)
                for at in range(piece * size, (piece + 1) * size, LANES)
            ],
            axis=1,
        )
        copies[piece].wait()
        part = jnp.dot(
            select, rows[piece * size : (piece + 1) * size, :], preferred_element_type=F32
        )
        total = part if total is None else total + part
    own_ref[...] = total.astype(BF16)


def load_kernel(
    span_hbm, hidden_hbm, gain_hbm, proj_hbm, resid_hbm, weight_hbm,
    stats_ref, projt_ref, residt_ref, gaint_ref, meant_ref, weight_ref,
    span, hidden, gain, proj, resid, sems,
):
    copies = [
        pltpu.make_async_copy(source, target, sems.at[index])
        for index, (source, target) in enumerate(
            [
                (span_hbm, span),
                (hidden_hbm.at[0], hidden),
                (gain_hbm, gain),
                (proj_hbm.at[0], proj),
                (resid_hbm.at[0], resid),
                (weight_hbm, weight_ref),
            ]
        )
    ]
    for copy in copies:
        copy.start()
    for copy in copies[:5]:
        copy.wait()
    start, count = span[0, 0], span[0, 1]
    tokens, width = proj.shape
    places = lax.broadcasted_iota(jnp.int32, (hidden.shape[0], 1), 0)
    mask = ((places >= start) & (places < start + count)).astype(F32)
    query = square = cross = jnp.zeros((LANES, tokens), F32)
    for at in range(0, width, LANES):
        cut = slice(at, at + LANES)
        mean = jnp.sum(hidden[:, cut].astype(F32) * mask, axis=0, keepdims=True)
        meant = to_column(mean / count.astype(F32))
        projt = jnp.transpose(proj[:, cut].astype(F32), (1, 0))
        residt = jnp.transpose(resid[:, cut].astype(F32), (1, 0))
        meant_ref[cut, :] = meant
        projt_ref[cut, :] = projt
        residt_ref[cut, :] = residt
        gaint_ref[cut, :] = to_column(gain[:, cut])
        query = query + projt * meant
        square = square + projt * projt
        cross = cross + projt * residt
    stats_ref[...] = jnp.zeros(stats_ref.shape, F32)
    for row, value in enumerate((query, square, cross)):
        stats_ref[row : row + 1, :] = jnp.sum(value, axis=0, keepdims=True)
    copies[5].wait()


def norm_kernel(peers, *refs):
    own_refs = refs[:peers]
    stats_ref, weight_ref, gaint_ref, projt_ref, scaledt_ref, sums_ref, pickedt = refs[peers:]
    key_width = own_refs[0].shape[1]
    for at in range(0, key_width, LANES):
        cut = slice(at, at + LANES)
        picked = own_refs[0][:, cut].astype(F32)
        for ref in own_refs[1:]:
            picked = picked + ref[:, cut].astype(F32)
        pickedt[cut, :] = jnp.transpose(picked, (1, 0)).astype(BF16)
    width, tokens = projt_ref.shape
    total = jnp.zeros((LANES, tokens), F32)
    for at in range(0, width, 256):
        cut = slice(at, at + 256)
        normed = jnp.dot(weight_ref[cut, :], pickedt[...], preferred_element_type=F32)
        scaled = normed * gaint_ref[cut, :]
        scaledt_ref[cut, :] = scaled
        terms = scaled * projt_ref[cut, :]
        total = total + terms[:LANES] + terms[LANES:]
    sums_ref[...] = stats_ref[...]
    sums_ref[3:4, :] = jnp.sum(total, axis=0, keepdims=True)


def start_weights(weight_hbm, weights, sems, peers, share, base, rows):
    quarter = weight_hbm.shape[0] // peers
    block = min(rows, 256)
    part = lax.rem(lax.axis_index("frame"), share) * (quarter // share)
    copies = []
    for peer in range(peers):
        first = (lax.axis_index("seq") ^ peer) * quarter + part + base
        for at in range(0, rows, block):
            index = len(copies)
            copies.append(
                pltpu.make_async_copy(
                    weight_hbm.at[pl.ds(pl.multiple_of(first + at, block), block)],
                    weights.at[pl.ds(peer * rows + at, block)],
                    sems.at[index],
                )
            )
            copies[-1].start()
    return copies


def preload_kernel(peers, share, rows, weight_hbm, after_ref, weights_ref, sems):
    del after_ref
    for copy in start_weights(weight_hbm, weights_ref, sems, peers, share, 0, rows):
        copy.wait()


def gate_kernel(features, peers, *refs):
    sums_refs = refs[:peers]
    projt_ref, residt_ref, scaledt_ref, meant_ref, owner_ref, after_ref = refs[peers : peers + 6]
    del after_ref
    gradt_ref, logit_ref = refs[peers + 6 :]
    sums = sums_refs[0][...]
    for ref in sums_refs[1:]:
        sums = sums + ref[...]
    sum_query, sum_square, sum_resid, sum_norm = (sums[i : i + 1] for i in range(4))
    gate_scale = 4.0 / math.sqrt(features)
    gate = jax.nn.sigmoid(gate_scale * sum_query)
    inv_rms = lax.rsqrt(gate * gate * sum_square / features + EPSILON)
    coef = gate * inv_rms * inv_rms * inv_rms * (gate * sum_norm) / features
    gate_grad = sum_resid + inv_rms * sum_norm - coef * sum_square
    logit = gate_grad * gate * (1.0 - gate) * gate_scale
    logit_ref[...] = jnp.broadcast_to(logit, logit_ref.shape)
    width = projt_ref.shape[0]
    for at in range(0, width, LANES):
        cut = slice(at, at + LANES)
        grad = residt_ref[cut, :] + inv_rms * scaledt_ref[cut, :] - coef * projt_ref[cut, :]
        gradt_ref[cut, :] = (gate * grad + logit * meant_ref[cut, :]).astype(BF16)
    tail = gradt_ref.shape[0] - width
    owner = owner_ref[...].astype(F32)
    gradt_ref[width:, :] = jnp.broadcast_to(owner, (tail, owner.shape[1])).astype(BF16)


def down_kernel(peers, share, base, rows, held, *refs):
    weight_ref = refs[0]
    gradt_refs = refs[1 : 1 + share]
    out_refs = refs[1 + share : 1 + share + peers]
    scratch = list(refs[1 + share + peers :])
    joined = scratch.pop(0)
    copies = None
    if held:
        weights = weight_ref
    else:
        weights, sems = scratch
        copies = start_weights(weight_ref, weights, sems, peers, share, base, rows)
    width, tokens = joined.shape[0], gradt_refs[0].shape[1]
    for index, ref in enumerate(gradt_refs):
        joined[:, index * tokens : (index + 1) * tokens] = ref[:width, :]
    block = min(rows, 256)
    inner = rows // block
    for index in range(peers * inner):
        peer, part = index // inner, index % inner
        if copies is not None:
            copies[index].wait()
        value = jnp.dot(
            weights[index * block : (index + 1) * block, :],
            joined[...],
            preferred_element_type=F32,
        )
        out_refs[peer][part * block : (part + 1) * block, :] = value.astype(BF16)


def ques_kernel(span_hbm, logit_ref, proj_hbm, out_ref, span, proj, sems):
    head = pltpu.make_async_copy(span_hbm, span, sems.at[0])
    load = pltpu.make_async_copy(proj_hbm.at[0], proj, sems.at[1])
    head.start()
    load.start()
    head.wait()
    start, count = span[0, 0], span[0, 1]
    length, width = out_ref.shape[1], out_ref.shape[2]
    places = lax.broadcasted_iota(jnp.int32, (length, LANES), 0)
    mask = ((places >= start) & (places < start + count)).astype(F32)
    column = to_column(logit_ref[0:1, :])
    load.wait()
    for at in range(0, width, LANES):
        cut = slice(at, at + LANES)
        total = jnp.sum(column * proj[:, cut].astype(F32), axis=0, keepdims=True)
        out_ref[0, :, cut] = (mask * total / count.astype(F32)).astype(BF16)


def targets(owner, capacity, share, source):
    tokens = owner.shape[1]
    above = lax.broadcasted_iota(jnp.int32, (tokens, tokens), 0)
    below = lax.broadcasted_iota(jnp.int32, (tokens, tokens), 1)
    earlier = jnp.where((to_column(owner) == owner) & (above < below), 1.0, 0.0)
    rank = jnp.sum(earlier, axis=0, keepdims=True).astype(jnp.int32)
    away = owner ^ lax.axis_index("frame")
    return (away * share + source) * capacity + rank


def place_kernel(capacity, share, pieces, mine, *refs):
    gradt_refs = refs[:share]
    part_refs = refs[share : share + mine]
    out_refs = refs[-pieces:]
    target = jnp.concatenate(
        [
            targets(ref[-16:-15, :].astype(F32).astype(jnp.int32), capacity, share, source)
            for source, ref in enumerate(gradt_refs)
        ],
        axis=1,
    )
    size = out_refs[0].shape[0]
    places = lax.broadcasted_iota(jnp.int32, (size * pieces, target.shape[1]), 0)
    placing = jnp.where(places == target, 1.0, 0.0).astype(BF16)
    total = part_refs[0][...].astype(F32)
    for ref in part_refs[1:]:
        total = total + ref[...].astype(F32)
    placed = lax.dot_general(
        placing, total.astype(BF16), (((1,), (1,)), ((), ())), preferred_element_type=F32
    ).astype(BF16)
    for index, ref in enumerate(out_refs):
        ref[...] = placed[index * size : (index + 1) * size, :]


def group_kernel(*refs):
    *part_refs, keep_ref, send_ref = refs
    size = part_refs[0].shape[0] // 2
    for index, ref in enumerate(part_refs):
        cut = slice(index * size, (index + 1) * size)
        keep_ref[cut, :] = ref[:size, :]
        send_ref[cut, :] = ref[size:, :]


def slope(pre_act):
    normal_cdf = 0.5 * (1.0 + lax.erf(pre_act * 0.7071067811865476))
    density = jnp.exp(-0.5 * pre_act * pre_act) * 0.3989422804014327
    return normal_cdf + pre_act * density


def final_kernel(capacity, share, turn, base, *refs):
    part_ref, pre_hbm = refs[:2]
    out_hbm, pre, out, sems = refs[-4:]
    rows, slots = pre.shape
    part = lax.rem(lax.axis_index("frame") + turn, share) * (pre_hbm.shape[1] // share)
    cut = pl.ds(pl.multiple_of(part + base, rows), rows)
    load = pltpu.make_async_copy(pre_hbm.at[0, cut], pre, sems.at[0])
    load.start()
    source = lax.broadcasted_iota(jnp.int32, (slots, slots), 0)
    goal = lax.broadcasted_iota(jnp.int32, (slots, slots), 1)
    moved = (goal ^ ((lax.axis_index("frame") ^ turn) * capacity)) == source
    hidden = lax.dot_general(
        part_ref[...],
        jnp.where(moved, 1.0, 0.0).astype(BF16),
        (((0,), (0,)), ((), ())),
        preferred_element_type=F32,
    )
    load.wait()
    out[...] = (hidden * slope(pre[...].astype(F32))).astype(BF16)
    store = pltpu.make_async_copy(out, out_hbm.at[0, cut], sems.at[1])
    store.start()
    store.wait()


def chunk_rows(quarter):
    return [quarter // 2] * 2


def body(
    peers,
    owners_count,
    value_grad,
    w_value,
    norm_gain,
    vis_pos,
    frame_owner,
    ques_span,
    vis_proj,
    vis_resid,
    ques_hidden,
    w_down,
    pre_owned,
):
    _, tokens, width = vis_proj.shape
    shard_len, key_width = value_grad.shape[1:]
    length = ques_hidden.shape[1]
    features = peers * width
    slots = pre_owned.shape[2]
    capacity = slots // owners_count
    gain = norm_gain.reshape(1, width)
    owner = frame_owner.reshape(1, tokens)
    row = shape((8, tokens), F32)
    tall = shape((width, tokens), F32)
    dma = pltpu.SemaphoreType.DMA

    pieces = max(1, shard_len // 256)
    own = call(
        functools.partial(pick_kernel, pieces),
        shape((tokens, key_width), BF16),
        [HBM, HBM],
        [
            pltpu.VMEM((1, tokens), jnp.int32),
            pltpu.VMEM((shard_len, key_width), BF16),
            dma((pieces + 1,)),
        ],
        grant=PICK_GRANT,
    )(vis_pos, value_grad)
    own_all = [own] + [swap(own, "seq", peers, k) for k in range(1, peers)]

    stats, projt, residt, gaint, meant, weight = call(
        load_kernel,
        [row, tall, tall, tall, tall, shape(w_value.shape, BF16)],
        [HBM] * 6,
        [
            pltpu.SMEM((1, 2), jnp.int32),
            pltpu.VMEM((length, width), BF16),
            pltpu.VMEM((1, width), F32),
            pltpu.VMEM((tokens, width), BF16),
            pltpu.VMEM((tokens, width), BF16),
            dma((6,)),
        ],
        grant=LOAD_GRANT,
    )(ques_span, ques_hidden, gain, vis_proj, vis_resid, w_value)

    scaledt, sums = call(
        functools.partial(norm_kernel, peers),
        [tall, row],
        [VMEM] * (peers + 4),
        [pltpu.VMEM((key_width, tokens), BF16)],
    )(*own_all, stats, weight, gaint, projt)
    sums_all = [sums] + [swap(sums, "seq", peers, k) for k in range(1, peers)]

    paired = capacity % 16 == 0 and owners_count % 2 == 0
    share = 2 if paired else 1
    pieces = owners_count // 2 if paired else 1
    chunks = chunk_rows(w_down.shape[0] // peers // share)
    bases = [sum(chunks[:i]) for i in range(len(chunks))]
    chain = Chain()

    def sems(rows):
        return dma((peers * (rows // min(rows, 256)),))

    preloaded = call(
        functools.partial(preload_kernel, peers, share, chunks[0]),
        shape((peers * chunks[0], width), BF16),
        [HBM, VMEM],
        [sems(chunks[0])],
    )(w_down, sums)

    gradt, logit = chain.call(
        functools.partial(gate_kernel, features, peers),
        [shape((width + 16, tokens), BF16), row],
        [VMEM] * (peers + 5) + [ANY],
    )(*sums_all, projt, residt, scaledt, meant, owner, preloaded)
    gradts = [gradt] + [swap(gradt, "frame", owners_count, k) for k in range(1, share)]

    def down(index):
        rows = chunks[index]
        weights = [pltpu.VMEM((peers * rows, width), BF16), sems(rows)]
        partial = chain.call(
            functools.partial(down_kernel, peers, share, bases[index], rows, index == 0),
            [shape((rows, share * tokens), BF16)] * peers,
            [VMEM if index == 0 else HBM] + [VMEM] * share,
            [pltpu.VMEM((width, share * tokens), BF16)] + (weights if index else []),
            cost=2 * peers * rows * width,
        )(w_down if index else preloaded, *gradts)
        return [partial[0]] + [swap(partial[k], "seq", peers, k) for k in range(1, peers)]

    def place(parts):
        rows = parts[0].shape[0]
        placed = chain.call(
            functools.partial(place_kernel, capacity, share, pieces, len(parts)),
            [shape((slots * share // pieces, rows), BF16)] * pieces,
            [VMEM] * (share + len(parts)),
        )(*gradts, *parts)
        if paired:
            return [placed[0]] + [
                swap(placed[k], "frame", owners_count, 2 * k) for k in range(1, pieces)
            ]
        order = jnp.arange(owners_count) ^ lax.axis_index("frame")
        split = placed[0].reshape(owners_count, capacity, rows)[order]
        split = lax.all_to_all(split, "frame", split_axis=0, concat_axis=0, tiled=True)
        return [split[order].reshape(slots, rows)]

    def group(parts):
        if not paired:
            return parts
        keep, send = chain.call(
            group_kernel,
            [shape((slots, parts[0].shape[1]), BF16)] * 2,
            [VMEM] * pieces,
        )(*parts)
        return [keep, swap(send, "frame", owners_count, 1)]

    def finish(parts, index, held):
        rows = chunks[index]
        for turn, part in enumerate(parts):
            held = chain.call(
                functools.partial(final_kernel, capacity, share, turn, bases[index]),
                [shape(pre_owned.shape, BF16)],
                [VMEM, HBM] + [HBM] * len(held),
                [pltpu.VMEM((rows, slots), BF16), pltpu.VMEM((rows, slots), BF16), dma((2,))],
                {2: 0} if held else None,
                [HBM],
            )(part, pre_owned, *held)
        return held

    waiting = [down(0), down(1)]
    placed = place(waiting[0])
    (ques_grad,) = chain.call(
        ques_kernel,
        [shape(ques_hidden.shape, BF16)],
        [HBM, VMEM, HBM],
        [pltpu.SMEM((1, 2), jnp.int32), pltpu.VMEM((tokens, width), BF16), dma((2,))],
    )(ques_span, logit, vis_proj)
    held = []
    for index in range(len(chunks)):
        parts = group(placed)
        if index + 1 < len(chunks):
            placed = place(waiting[index + 1])
            if index + 2 < len(chunks):
                waiting.append(down(index + 2))
        held = finish(parts, index, held)
    return (held[0], ques_grad)


def solution(mesh):
    in_specs = (
        P("frame", "seq", None),
        P("seq", None),
        P("seq"),
        P("frame", None),
        P("frame", None, None),
        P("frame", None),
        P("frame", None, "seq"),
        P("frame", None, "seq"),
        P("frame", None, "seq"),
        P(None, "seq"),
        P("frame", "seq", None),
    )
    out_specs = (P("frame", "seq", None), P("frame", None, "seq"))
    run = functools.partial(body, mesh.shape["seq"], mesh.shape["frame"])
    return jax.shard_map(run, mesh=mesh, in_specs=in_specs, out_specs=out_specs, check_vma=False)
```

profile of v0, /device:TPU:0, one launch (start us, length us, event | category | flops | bytes accessed | tf_op | source)
XLA Modules:
  0.0 78.6 jit_solution(2552391042444407862)
XLA Ops:
  0.6 2.1 %shard_map.122.refs_0_ = bf16[128,512]{1,0:T(8,128)(2,1)} custom-call(s32[1,128]{1,0:T(1,128)} %pos_hbm.1, bf16[1,1024,512]{2,1,0:T(8,128)(2,1)} %rows_hbm.1), custom_call_target="tpu_custom_call" | custom-call | flops 262144 | bytes 1024 | tf_op jit(solution)/shard_map/pallas_call | solution.py:388
  2.8 4.0 %collective-permute-start.2 = (bf16[128,512]{1,0:T(8,128)(2,1)}, bf16[128,512]{1,0:T(8,128)(2,1)S(1)}, u32[]{:S(2)}, u32[]{:S(2)}) collective-permute-start(bf16[128,512]{1,0:T(8,128)(2,1)} %shard_map.122.refs_0_), channel_id=1, source_target_pairs={{0,24},{8,16},{16,8},{24,0},{1,25},{9,17},{17,9},{25,1},{2,26},{10... | collective-permute-start | bytes 393224 | tf_op jit(solution)/shard_map/ppermute | solution.py:75
  7.4 1.6 %copy-done.1 = bf16[2048,512]{1,0:T(8,128)(2,1)S(1)} copy-done((bf16[2048,512]{1,0:T(8,128)(2,1)S(1)}, bf16[2048,512]{1,0:T(8,128)(2,1)}, u32[]{:S(2)}) %copy-start.1) | copy-done | bytes 2097176
  13.3 1.5 %shard_map.123 = (f32[8,128]{1,0:T(8,128)S(1)}, f32[2048,128]{1,0:T(8,128)S(1)}, f32[2048,128]{1,0:T(8,128)S(1)}, f32[2048,128]{1,0:T(8,128)S(1)}, f32[2048,128]...) custom-call(s32[1,2]{1,0:T(1,128)S(1)} %copy-done.8, bf16[1,32,2048]{2,1,0:T(8,128)(2,1)S(1)} %copy-done.6, ...), custom_call_target="tpu_custom_call" | custom-call | flops 262144 | bytes 1024 | tf_op jit(solution)/shard_map/pallas_call | solution.py:401
  16.7 2.9 %collective-permute-start.5 = (f32[8,128]{1,0:T(8,128)S(1)}, f32[8,128]{1,0:T(8,128)S(1)}, u32[]{:S(2)}, u32[]{:S(2)}) collective-permute-start(f32[8,128]{1,0:T(8,128)S(1)} %get-tuple-element.52.after_ref.refs_0_), channel_id=1, source_target_pairs={{0,24},{8,16},{16,8},{24,0},{1,25},{9,17},{17,9},{25,1},{2,26},{10... | collective-permute-start | bytes 12296 | tf_op jit(solution)/shard_map/ppermute | solution.py:75
  20.2 3.5 %shard_map.125.refs_9_.refs_0_ = bf16[2048,2048]{1,0:T(8,128)(2,1)S(1)} custom-call(bf16[8192,2048]{1,0:T(8,128)(2,1)} %refs_0_.2, f32[8,128]{1,0:T(8,128)S(1)} %get-tuple-element.52.after_ref.refs_0_), custom_call_target="tpu_custom_call" | custom-call | flops 262144 | bytes 1024 | tf_op jit(solution)/shard_map/pallas_call | solution.py:434
  24.1 1.9 %collective-permute-done.6.refs_2_.refs_1_ = bf16[2064,128]{1,0:T(8,128)(2,1)S(1)} collective-permute-done((bf16[2064,128]{1,0:T(8,128)(2,1)S(1)}, bf16[2064,128]{1,0:T(8,128)(2,1)S(1)}, u32[]{:S(2)}, u32[]{:S(2)}) %collective-permute-start.6) | collective-permute-done | bytes 528416 | tf_op jit(solution)/shard_map/ppermute | solution.py:75
  26.0 2.4 %shard_map.127 = (bf16[512,256]{1,0:T(8,128)(2,1)S(1)}, bf16[512,256]{1,0:T(8,128)(2,1)S(1)}, bf16[512,256]{1,0:T(8,128)(2,1)S(1)}, bf16[512,256]{1,0:T(8,128)(2,1)S(1)}, f32[8,128]{1,0:T(8,128)S(1)}) custom-call(bf16[2048,2048]{1,0:T(8,128)(2,1)S(1)} %shard_map.125.refs_9_.refs_0_, bf16[2064,128]{1,0:T(8,128)(2,1)S(1)} %get-tuple-element.56.refs_1_.refs_0_, ...), custom_call_target="tpu_custom_call" | custom-call | flops 2147483648 | bytes 8388608 | tf_op jit(solution)/shard_map/pallas_call | solution.py:63
  28.5 2.0 %collective-permute-start.10 = (bf16[512,256]{1,0:T(8,128)(2,1)S(1)}, bf16[512,256]{1,0:T(8,128)(2,1)S(1)}, u32[]{:S(2)}, u32[]{:S(2)}) collective-permute-start(bf16[512,256]{1,0:T(8,128)(2,1)S(1)} %get-tuple-element.64), channel_id=1, source_target_pairs={{0,8},{8,0},{16,24},{24,16},{1,9},{9,1},{17,25},{25,17},{2,10},{10... | collective-permute-start | bytes 786440 | tf_op jit(solution)/shard_map/ppermute | solution.py:75
  30.4 1.5 %collective-permute-start.11 = (bf16[512,256]{1,0:T(8,128)(2,1)S(1)}, bf16[512,256]{1,0:T(8,128)(2,1)S(1)}, u32[]{:S(2)}, u32[]{:S(2)}) collective-permute-start(bf16[512,256]{1,0:T(8,128)(2,1)S(1)} %get-tuple-element.65), channel_id=1, source_target_pairs={{0,16},{8,24},{16,0},{24,8},{1,17},{9,25},{17,1},{25,9},{2,18},{10... | collective-permute-start | bytes 786440 | tf_op jit(solution)/shard_map/ppermute | solution.py:75
  32.0 7.0 %shard_map.128 = (bf16[512,256]{1,0:T(8,128)(2,1)S(1)}, bf16[512,256]{1,0:T(8,128)(2,1)S(1)}, bf16[512,256]{1,0:T(8,128)(2,1)S(1)}, bf16[512,256]{1,0:T(8,128)(2,1)S(1)}, f32[8,128]{1,0:T(8,128)S(1)}) custom-call(bf16[8192,2048]{1,0:T(8,128)(2,1)} %refs_0_.2, bf16[2064,128]{1,0:T(8,128)(2,1)S(1)} %get-tuple-element.56.refs_1_.refs_0_, ...), custom_call_target="tpu_custom_call" | custom-call | flops 2147483648 | bytes 8388608 | tf_op jit(solution)/shard_map/pallas_call | solution.py:63
  39.0 5.1 %collective-permute-done.11.refs_4_ = bf16[512,256]{1,0:T(8,128)(2,1)S(1)} collective-permute-done((bf16[512,256]{1,0:T(8,128)(2,1)S(1)}, bf16[512,256]{1,0:T(8,128)(2,1)S(1)}, u32[]{:S(2)}, u32[]{:S(2)}) %collective-permute-start.11) | collective-permute-done | bytes 262176 | tf_op jit(solution)/shard_map/ppermute | solution.py:75
  44.5 1.7 %collective-permute-start.13 = (bf16[128,512]{1,0:T(8,128)(2,1)S(1)}, bf16[128,512]{1,0:T(8,128)(2,1)S(1)}, u32[]{:S(2)}, u32[]{:S(2)}) collective-permute-start(bf16[128,512]{1,0:T(8,128)(2,1)S(1)} %get-tuple-element.69), channel_id=1, source_target_pairs={{0,2},{1,3},{2,0},{3,1},{4,6},{5,7},{6,4},{7,5},{8,10},{9,11},{10,... | collective-permute-start | bytes 393224 | tf_op jit(solution)/shard_map/ppermute | solution.py:75
  48.2 2.6 %collective-permute-start.14 = (bf16[128,512]{1,0:T(8,128)(2,1)S(1)}, bf16[128,512]{1,0:T(8,128)(2,1)S(1)}, u32[]{:S(2)}, u32[]{:S(2)}) collective-permute-start(bf16[128,512]{1,0:T(8,128)(2,1)S(1)} %get-tuple-element.70), channel_id=1, source_target_pairs={{0,4},{1,5},{2,6},{3,7},{4,0},{5,1},{6,2},{7,3},{8,12},{9,13},{10,... | collective-permute-start | bytes 393224 | tf_op jit(solution)/shard_map/ppermute | solution.py:75
  51.0 1.4 %collective-permute-start.9 = (bf16[512,256]{1,0:T(8,128)(2,1)S(1)}, bf16[512,256]{1,0:T(8,128)(2,1)S(1)}, u32[]{:S(2)}, u32[]{:S(2)}) collective-permute-start(bf16[512,256]{1,0:T(8,128)(2,1)S(1)} %get-tuple-element.62), channel_id=1, source_target_pairs={{0,24},{8,16},{16,8},{24,0},{1,25},{9,17},{17,9},{25,1},{2,26},{10... | collective-permute-start | bytes 786440 | tf_op jit(solution)/shard_map/ppermute | solution.py:75
  52.5 1.5 %shard_map.130 = (bf16[1,32,2048]{2,1,0:T(8,128)(2,1)}, f32[8,128]{1,0:T(8,128)S(1)}) custom-call(s32[1,2]{1,0:T(1,128)S(1)} %copy-done.9, f32[8,128]{1,0:T(8,128)S(1)} %get-tuple-element.72.refs_1_, bf16[1,128,2048]{2,1,0:T(8,128)(2,1)S(1)} %copy-done.3, f32[8,128]{1,0:T(8,128)S(1)} %get-tuple-element.73.refs_3_), custom_call_target="tpu_custom_call" | custom-call | flops 262144 | bytes 1024 | tf_op jit(solution)/shard_map/pallas_call | solution.py:63
  53.9 5.7 %collective-permute-done.14.refs_2_ = bf16[128,512]{1,0:T(8,128)(2,1)S(1)} collective-permute-done((bf16[128,512]{1,0:T(8,128)(2,1)S(1)}, bf16[128,512]{1,0:T(8,128)(2,1)S(1)}, u32[]{:S(2)}, u32[]{:S(2)}) %collective-permute-start.14) | collective-permute-done | bytes 131104 | tf_op jit(solution)/shard_map/ppermute | solution.py:75
  60.4 1.8 %collective-permute-start.16 = (bf16[128,512]{1,0:T(8,128)(2,1)S(1)}, bf16[128,512]{1,0:T(8,128)(2,1)S(1)}, u32[]{:S(2)}, u32[]{:S(2)}) collective-permute-start(bf16[128,512]{1,0:T(8,128)(2,1)S(1)} %get-tuple-element.77), channel_id=1, source_target_pairs={{0,2},{1,3},{2,0},{3,1},{4,6},{5,7},{6,4},{7,5},{8,10},{9,11},{10,... | collective-permute-start | bytes 393224 | tf_op jit(solution)/shard_map/ppermute | solution.py:75
  62.2 1.3 %collective-permute-start.17 = (bf16[128,512]{1,0:T(8,128)(2,1)S(1)}, bf16[128,512]{1,0:T(8,128)(2,1)S(1)}, u32[]{:S(2)}, u32[]{:S(2)}) collective-permute-start(bf16[128,512]{1,0:T(8,128)(2,1)S(1)} %get-tuple-element.78), channel_id=1, source_target_pairs={{0,4},{1,5},{2,6},{3,7},{4,0},{5,1},{6,2},{7,3},{8,12},{9,13},{10,... | collective-permute-start | bytes 393224 | tf_op jit(solution)/shard_map/ppermute | solution.py:75
  63.5 1.3 %collective-permute-start.18 = (bf16[128,512]{1,0:T(8,128)(2,1)S(1)}, bf16[128,512]{1,0:T(8,128)(2,1)S(1)}, u32[]{:S(2)}, u32[]{:S(2)}) collective-permute-start(bf16[128,512]{1,0:T(8,128)(2,1)S(1)} %get-tuple-element.79), channel_id=1, source_target_pairs={{0,6},{1,7},{2,4},{3,5},{4,2},{5,3},{6,0},{7,1},{8,14},{9,15},{10,... | collective-permute-start | bytes 393224 | tf_op jit(solution)/shard_map/ppermute | solution.py:75
  66.1 1.3 %shard_map.134 = (bf16[1,2048,256]{2,1,0:T(8,128)(2,1)}, f32[8,128]{1,0:T(8,128)S(1)}) custom-call(bf16[256,512]{1,0:T(8,128)(2,1)S(1)} %collective-permute-done.19.refs_0_, bf16[1,2048,256]{2,1,0:T(8,128)(2,1)S(1)} %copy-done, bf16[1,2048,256]{2,1,0:T(8,128)(2,1)} %get-tuple-element.83.refs_2_, ...), custom_call_target="tpu_custom_call", output_to_operand_aliasing={{0}: (2, {})} | custom-call | flops 262144 | bytes 1024 | tf_op jit(solution)/shard_map/pallas_call | solution.py:63
  68.7 6.5 %collective-permute-done.17.refs_2_ = bf16[128,512]{1,0:T(8,128)(2,1)S(1)} collective-permute-done((bf16[128,512]{1,0:T(8,128)(2,1)S(1)}, bf16[128,512]{1,0:T(8,128)(2,1)S(1)}, u32[]{:S(2)}, u32[]{:S(2)}) %collective-permute-start.17) | collective-permute-done | bytes 131104 | tf_op jit(solution)/shard_map/ppermute | solution.py:75
  75.2 1.3 %shard_map.136 = (bf16[1,2048,256]{2,1,0:T(8,128)(2,1)}, f32[8,128]{1,0:T(8,128)S(1)}) custom-call(bf16[256,512]{1,0:T(8,128)(2,1)S(1)} %get-tuple-element.87.refs_0_, bf16[1,2048,256]{2,1,0:T(8,128)(2,1)S(1)} %copy-done, bf16[1,2048,256]{2,1,0:T(8,128)(2,1)} %get-tuple-element.88.refs_2_, ...), custom_call_target="tpu_custom_call", output_to_operand_aliasing={{0}: (2, {})} | custom-call | flops 262144 | bytes 1024 | tf_op jit(solution)/shard_map/pallas_call | solution.py:63
  76.8 1.8 %shard_map.137 = (bf16[1,2048,256]{2,1,0:T(8,128)(2,1)}, f32[8,128]{1,0:T(8,128)}) custom-call(bf16[256,512]{1,0:T(8,128)(2,1)S(1)} %collective-permute-done.20.refs_0_, bf16[1,2048,256]{2,1,0:T(8,128)(2,1)S(1)} %copy-done, bf16[1,2048,256]{2,1,0:T(8,128)(2,1)} %get-tuple-element.90.refs_2_, ...), custom_call_target="tpu_custom_call", output_to_operand_aliasing={{0}: (2, {})} | custom-call | flops 262144 | bytes 1024 | tf_op jit(solution)/shard_map/pallas_call | solution.py:63
  (56 shorter events, 14.2 us)
Async XLA Ops:
  2.8 12.1 %collective-permute-start.2 = (bf16[128,512]{1,0:T(8,128)(2,1)}, bf16[128,512]{1,0:T(8,128)(2,1)S(1)}, u32[]{:S(2)}, u32[]{:S(2)}) collective-permute-start(bf16[128,512]{1,0:T(8,128)(2,1)} %shard_map.122.refs_0_), channel_id=1, source_target_pairs={{0,24},{8,16},{16,8},{24,0},{1,25},{9,17},{17,9},{25,1},{2,26},{10... | collective-permute-start | bytes 393224 | tf_op jit(solution)/shard_map/ppermute | solution.py:75
  6.7 8.1 %collective-permute-start.1 = (bf16[128,512]{1,0:T(8,128)(2,1)}, bf16[128,512]{1,0:T(8,128)(2,1)S(1)}, u32[]{:S(2)}, u32[]{:S(2)}) collective-permute-start(bf16[128,512]{1,0:T(8,128)(2,1)} %shard_map.122.refs_0_), channel_id=1, source_target_pairs={{0,16},{8,24},{16,0},{24,8},{1,17},{9,25},{17,1},{25,9},{2,18},{10... | collective-permute-start | bytes 393224 | tf_op jit(solution)/shard_map/ppermute | solution.py:75
  7.2 7.6 %collective-permute-start = (bf16[128,512]{1,0:T(8,128)(2,1)}, bf16[128,512]{1,0:T(8,128)(2,1)S(1)}, u32[]{:S(2)}, u32[]{:S(2)}) collective-permute-start(bf16[128,512]{1,0:T(8,128)(2,1)} %shard_map.122.refs_0_), channel_id=1, source_target_pairs={{0,8},{8,0},{16,24},{24,16},{1,9},{9,1},{17,25},{25,17},{2,10},{10... | collective-permute-start | bytes 393224 | tf_op jit(solution)/shard_map/ppermute | solution.py:75
  16.7 7.0 %collective-permute-start.5 = (f32[8,128]{1,0:T(8,128)S(1)}, f32[8,128]{1,0:T(8,128)S(1)}, u32[]{:S(2)}, u32[]{:S(2)}) collective-permute-start(f32[8,128]{1,0:T(8,128)S(1)} %get-tuple-element.52.after_ref.refs_0_), channel_id=1, source_target_pairs={{0,24},{8,16},{16,8},{24,0},{1,25},{9,17},{17,9},{25,1},{2,26},{10... | collective-permute-start | bytes 12296 | tf_op jit(solution)/shard_map/ppermute | solution.py:75
  19.6 4.1 %collective-permute-start.4 = (f32[8,128]{1,0:T(8,128)S(1)}, f32[8,128]{1,0:T(8,128)S(1)}, u32[]{:S(2)}, u32[]{:S(2)}) collective-permute-start(f32[8,128]{1,0:T(8,128)S(1)} %get-tuple-element.52.after_ref.refs_0_), channel_id=1, source_target_pairs={{0,16},{8,24},{16,0},{24,8},{1,17},{9,25},{17,1},{25,9},{2,18},{10... | collective-permute-start | bytes 12296 | tf_op jit(solution)/shard_map/ppermute | solution.py:75
  20.1 3.6 %collective-permute-start.3 = (f32[8,128]{1,0:T(8,128)S(1)}, f32[8,128]{1,0:T(8,128)S(1)}, u32[]{:S(2)}, u32[]{:S(2)}) collective-permute-start(f32[8,128]{1,0:T(8,128)S(1)} %get-tuple-element.52.after_ref.refs_0_), channel_id=1, source_target_pairs={{0,8},{8,0},{16,24},{24,16},{1,9},{9,1},{17,25},{25,17},{2,10},{10... | collective-permute-start | bytes 12296 | tf_op jit(solution)/shard_map/ppermute | solution.py:75
  24.0 2.0 %collective-permute-start.6 = (bf16[2064,128]{1,0:T(8,128)(2,1)S(1)}, bf16[2064,128]{1,0:T(8,128)(2,1)S(1)}, u32[]{:S(2)}, u32[]{:S(2)}) collective-permute-start(bf16[2064,128]{1,0:T(8,128)(2,1)S(1)} %get-tuple-element.56.refs_1_.refs_0_), channel_id=1, source_target_pairs={{0,1},{1,0},{2,3},{3,2},{4,5},{5,4},{6,7},{7,6},{8,9},{9,8},{10,11... | collective-permute-start | bytes 1585160 | tf_op jit(solution)/shard_map/ppermute | solution.py:75
  28.5 10.5 %collective-permute-start.10 = (bf16[512,256]{1,0:T(8,128)(2,1)S(1)}, bf16[512,256]{1,0:T(8,128)(2,1)S(1)}, u32[]{:S(2)}, u32[]{:S(2)}) collective-permute-start(bf16[512,256]{1,0:T(8,128)(2,1)S(1)} %get-tuple-element.64), channel_id=1, source_target_pairs={{0,8},{8,0},{16,24},{24,16},{1,9},{9,1},{17,25},{25,17},{2,10},{10... | collective-permute-start | bytes 786440 | tf_op jit(solution)/shard_map/ppermute | solution.py:75
  30.4 13.7 %collective-permute-start.11 = (bf16[512,256]{1,0:T(8,128)(2,1)S(1)}, bf16[512,256]{1,0:T(8,128)(2,1)S(1)}, u32[]{:S(2)}, u32[]{:S(2)}) collective-permute-start(bf16[512,256]{1,0:T(8,128)(2,1)S(1)} %get-tuple-element.65), channel_id=1, source_target_pairs={{0,16},{8,24},{16,0},{24,8},{1,17},{9,25},{17,1},{25,9},{2,18},{10... | collective-permute-start | bytes 786440 | tf_op jit(solution)/shard_map/ppermute | solution.py:75
  31.9 12.2 %collective-permute-start.12 = (bf16[512,256]{1,0:T(8,128)(2,1)S(1)}, bf16[512,256]{1,0:T(8,128)(2,1)S(1)}, u32[]{:S(2)}, u32[]{:S(2)}) collective-permute-start(bf16[512,256]{1,0:T(8,128)(2,1)S(1)} %get-tuple-element.66), channel_id=1, source_target_pairs={{0,24},{8,16},{16,8},{24,0},{1,25},{9,17},{17,9},{25,1},{2,26},{10... | collective-permute-start | bytes 786440 | tf_op jit(solution)/shard_map/ppermute | solution.py:75
  32.0 20.5 %copy-start.3 = (bf16[1,128,2048]{2,1,0:T(8,128)(2,1)S(1)}, bf16[1,128,2048]{2,1,0:T(8,128)(2,1)}, u32[]{:S(2)}) copy-start(bf16[1,128,2048]{2,1,0:T(8,128)(2,1)} %refs_2_.1) | copy-start | bytes 1572868
  32.0 20.5 %copy-start.9 = (s32[1,2]{1,0:T(1,128)S(1)}, s32[1,2]{1,0:T(1,128)}, u32[]{:S(2)}) copy-start(s32[1,2]{1,0:T(1,128)} %refs_0_.3) | copy-start | bytes 28
  32.0 32.9 %copy-start = (bf16[1,2048,256]{2,1,0:T(8,128)(2,1)S(1)}, bf16[1,2048,256]{2,1,0:T(8,128)(2,1)}, u32[]{:S(2)}) copy-start(bf16[1,2048,256]{2,1,0:T(8,128)(2,1)} %refs_1_.7) | copy-start | bytes 3145732
  44.5 6.5 %collective-permute-start.13 = (bf16[128,512]{1,0:T(8,128)(2,1)S(1)}, bf16[128,512]{1,0:T(8,128)(2,1)S(1)}, u32[]{:S(2)}, u32[]{:S(2)}) collective-permute-start(bf16[128,512]{1,0:T(8,128)(2,1)S(1)} %get-tuple-element.69), channel_id=1, source_target_pairs={{0,2},{1,3},{2,0},{3,1},{4,6},{5,7},{6,4},{7,5},{8,10},{9,11},{10,... | collective-permute-start | bytes 393224 | tf_op jit(solution)/shard_map/ppermute | solution.py:75
  46.2 13.6 %collective-permute-start.7 = (bf16[512,256]{1,0:T(8,128)(2,1)S(1)}, bf16[512,256]{1,0:T(8,128)(2,1)S(1)}, u32[]{:S(2)}, u32[]{:S(2)}) collective-permute-start(bf16[512,256]{1,0:T(8,128)(2,1)S(1)} %get-tuple-element.60), channel_id=1, source_target_pairs={{0,8},{8,0},{16,24},{24,16},{1,9},{9,1},{17,25},{25,17},{2,10},{10... | collective-permute-start | bytes 786440 | tf_op jit(solution)/shard_map/ppermute | solution.py:75
  47.4 12.6 %collective-permute-start.8 = (bf16[512,256]{1,0:T(8,128)(2,1)S(1)}, bf16[512,256]{1,0:T(8,128)(2,1)S(1)}, u32[]{:S(2)}, u32[]{:S(2)}) collective-permute-start(bf16[512,256]{1,0:T(8,128)(2,1)S(1)} %get-tuple-element.61), channel_id=1, source_target_pairs={{0,16},{8,24},{16,0},{24,8},{1,17},{9,25},{17,1},{25,9},{2,18},{10... | collective-permute-start | bytes 786440 | tf_op jit(solution)/shard_map/ppermute | solution.py:75
  48.2 11.4 %collective-permute-start.14 = (bf16[128,512]{1,0:T(8,128)(2,1)S(1)}, bf16[128,512]{1,0:T(8,128)(2,1)S(1)}, u32[]{:S(2)}, u32[]{:S(2)}) collective-permute-start(bf16[128,512]{1,0:T(8,128)(2,1)S(1)} %get-tuple-element.70), channel_id=1, source_target_pairs={{0,4},{1,5},{2,6},{3,7},{4,0},{5,1},{6,2},{7,3},{8,12},{9,13},{10,... | collective-permute-start | bytes 393224 | tf_op jit(solution)/shard_map/ppermute | solution.py:75
  50.8 8.8 %collective-permute-start.15 = (bf16[128,512]{1,0:T(8,128)(2,1)S(1)}, bf16[128,512]{1,0:T(8,128)(2,1)S(1)}, u32[]{:S(2)}, u32[]{:S(2)}) collective-permute-start(bf16[128,512]{1,0:T(8,128)(2,1)S(1)} %get-tuple-element.71), channel_id=1, source_target_pairs={{0,6},{1,7},{2,4},{3,5},{4,2},{5,3},{6,0},{7,1},{8,14},{9,15},{10,... | collective-permute-start | bytes 393224 | tf_op jit(solution)/shard_map/ppermute | solution.py:75
  51.0 8.9 %collective-permute-start.9 = (bf16[512,256]{1,0:T(8,128)(2,1)S(1)}, bf16[512,256]{1,0:T(8,128)(2,1)S(1)}, u32[]{:S(2)}, u32[]{:S(2)}) collective-permute-start(bf16[512,256]{1,0:T(8,128)(2,1)S(1)} %get-tuple-element.62), channel_id=1, source_target_pairs={{0,24},{8,16},{16,8},{24,0},{1,25},{9,17},{17,9},{25,1},{2,26},{10... | collective-permute-start | bytes 786440 | tf_op jit(solution)/shard_map/ppermute | solution.py:75
  59.6 6.5 %collective-permute-start.19 = (bf16[256,512]{1,0:T(8,128)(2,1)S(1)}, bf16[256,512]{1,0:T(8,128)(2,1)S(1)}, u32[]{:S(2)}, u32[]{:S(2)}) collective-permute-start(bf16[256,512]{1,0:T(8,128)(2,1)S(1)} %get-tuple-element.80), channel_id=1, source_target_pairs={{0,1},{1,0},{2,3},{3,2},{4,5},{5,4},{6,7},{7,6},{8,9},{9,8},{10,11... | collective-permute-start | bytes 786440 | tf_op jit(solution)/shard_map/ppermute | solution.py:75
  60.4 8.3 %collective-permute-start.16 = (bf16[128,512]{1,0:T(8,128)(2,1)S(1)}, bf16[128,512]{1,0:T(8,128)(2,1)S(1)}, u32[]{:S(2)}, u32[]{:S(2)}) collective-permute-start(bf16[128,512]{1,0:T(8,128)(2,1)S(1)} %get-tuple-element.77), channel_id=1, source_target_pairs={{0,2},{1,3},{2,0},{3,1},{4,6},{5,7},{6,4},{7,5},{8,10},{9,11},{10,... | collective-permute-start | bytes 393224 | tf_op jit(solution)/shard_map/ppermute | solution.py:75
  62.2 12.9 %collective-permute-start.17 = (bf16[128,512]{1,0:T(8,128)(2,1)S(1)}, bf16[128,512]{1,0:T(8,128)(2,1)S(1)}, u32[]{:S(2)}, u32[]{:S(2)}) collective-permute-start(bf16[128,512]{1,0:T(8,128)(2,1)S(1)} %get-tuple-element.78), channel_id=1, source_target_pairs={{0,4},{1,5},{2,6},{3,7},{4,0},{5,1},{6,2},{7,3},{8,12},{9,13},{10,... | collective-permute-start | bytes 393224 | tf_op jit(solution)/shard_map/ppermute | solution.py:75
  63.5 11.6 %collective-permute-start.18 = (bf16[128,512]{1,0:T(8,128)(2,1)S(1)}, bf16[128,512]{1,0:T(8,128)(2,1)S(1)}, u32[]{:S(2)}, u32[]{:S(2)}) collective-permute-start(bf16[128,512]{1,0:T(8,128)(2,1)S(1)} %get-tuple-element.79), channel_id=1, source_target_pairs={{0,6},{1,7},{2,4},{3,5},{4,2},{5,3},{6,0},{7,1},{8,14},{9,15},{10,... | collective-permute-start | bytes 393224 | tf_op jit(solution)/shard_map/ppermute | solution.py:75
  75.2 1.6 %collective-permute-start.20 = (bf16[256,512]{1,0:T(8,128)(2,1)S(1)}, bf16[256,512]{1,0:T(8,128)(2,1)S(1)}, u32[]{:S(2)}, u32[]{:S(2)}) collective-permute-start(bf16[256,512]{1,0:T(8,128)(2,1)S(1)} %get-tuple-element.86), channel_id=1, source_target_pairs={{0,1},{1,0},{2,3},{3,2},{4,5},{5,4},{6,7},{7,6},{8,9},{9,8},{10,11... | collective-permute-start | bytes 786440 | tf_op jit(solution)/shard_map/ppermute | solution.py:75
  (8 other events, 13.9 us)
where the time goes:
time: 79.1 us; the launch traced here: 78.6 us
  Pallas kernels  25.6 us (32%)
  starting transfers between devices  24.3 us (31%)
  waiting for transfers between devices  20.9 us (26%)
  local copies, waits for them, and re-layouts  6.84 us (9%)
  between operations  0.88 us (1%)
    ppermute x21, starting transfers between devices, swap(): return lax.ppermute(value, axis, [(i, i ^ step) for i in range(count)])  24.3 us
    ppermute x21, waiting for transfers between devices, swap(): return lax.ppermute(value, axis, [(i, i ^ step) for i in range(count)])  20.9 us
    pallas_call x12, Pallas kernels, apply(): *results, token = run_call(*args, *self.last)  17.6 us
    unnamed x22, local copies, waits for them, and re-layouts  6.84 us
    pallas_call x1, Pallas kernels, body(): call(functools.partial(preload_kernel, peers, share, chunks[0]), shape((p...  3.47 us
    pallas_call x1, Pallas kernels, body(): call(functools.partial(pick_kernel, pieces), shape((tokens, key_width), B...  2.15 us
  transfers between devices with their start and end apart: 21, of which 7 were waited for; matrix products, arithmetic and copies ran while one was open for 0% of the time, Pallas kernels for 22%

commit v1 on v0

--- a/solution.py
+++ b/solution.py
@@ -12,8 +12,9 @@
 F32 = jnp.float32
 BF16 = jnp.bfloat16
 LANES = 128
+AHEAD = 3
 MIB = 1024 * 1024
-GRANT, LOAD_GRANT, PICK_GRANT = 40, 40, 63
+GRANT, LOAD_GRANT, PICK_GRANT = 40, 46, 54
 HBM = pl.BlockSpec(memory_space=pltpu.HBM)
 VMEM = pl.BlockSpec(memory_space=pltpu.VMEM)
 ANY = pl.BlockSpec(memory_space=pl.ANY)
@@ -73,6 +74,17 @@
 
 def swap(value, axis, count, step):
     return lax.ppermute(value, axis, [(i, i ^ step) for i in range(count)])
+
+
+def far_first(count):
+    return [0, *reversed(range(1, count))]
+
+
+def swaps(values, axis, count, stride=1):
+    return [
+        swap(value, axis, count, step * stride) if step else value
+        for value, step in zip(values, far_first(len(values)))
+    ]
 
 
 def to_column(row):
@@ -181,13 +193,13 @@
     sums_ref[3:4, :] = jnp.sum(total, axis=0, keepdims=True)
 
 
-def start_weights(weight_hbm, weights, sems, peers, share, base, rows):
+def weight_copies(weight_hbm, weights, sems, peers, share, base, rows):
     quarter = weight_hbm.shape[0] // peers
     block = min(rows, 256)
     part = lax.rem(lax.axis_index("frame"), share) * (quarter // share)
     copies = []
-    for peer in range(peers):
-        first = (lax.axis_index("seq") ^ peer) * quarter + part + base
+    for peer, step in enumerate(far_first(peers)):
+        first = (lax.axis_index("seq") ^ step) * quarter + part + base
         for at in range(0, rows, block):
             index = len(copies)
             copies.append(
@@ -197,13 +209,15 @@
                     sems.at[index],
                 )
             )
-            copies[-1].start()
     return copies
 
 
 def preload_kernel(peers, share, rows, weight_hbm, after_ref, weights_ref, sems):
     del after_ref
-    for copy in start_weights(weight_hbm, weights_ref, sems, peers, share, 0, rows):
+    copies = weight_copies(weight_hbm, weights_ref, sems, peers, share, 0, rows)
+    for copy in copies:
+        copy.start()
+    for copy in copies:
         copy.wait()
 
 
@@ -239,12 +253,14 @@
     out_refs = refs[1 + share : 1 + share + peers]
     scratch = list(refs[1 + share + peers :])
     joined = scratch.pop(0)
-    copies = None
+    copies = []
     if held:
         weights = weight_ref
     else:
         weights, sems = scratch
-        copies = start_weights(weight_ref, weights, sems, peers, share, base, rows)
+        copies = weight_copies(weight_ref, weights, sems, peers, share, base, rows)
+    for copy in copies[:AHEAD]:
+        copy.start()
     width, tokens = joined.shape[0], gradt_refs[0].shape[1]
     for index, ref in enumerate(gradt_refs):
         joined[:, index * tokens : (index + 1) * tokens] = ref[:width, :]
@@ -252,8 +268,10 @@
     inner = rows // block
     for index in range(peers * inner):
         peer, part = index // inner, index % inner
-        if copies is not None:
+        if copies:
             copies[index].wait()
+        if index + AHEAD < len(copies):
+            copies[index + AHEAD].start()
         value = jnp.dot(
             weights[index * block : (index + 1) * block, :],
             joined[...],
@@ -310,15 +328,15 @@
     placed = lax.dot_general(
         placing, total.astype(BF16), (((1,), (1,)), ((), ())), preferred_element_type=F32
     ).astype(BF16)
-    for index, ref in enumerate(out_refs):
-        ref[...] = placed[index * size : (index + 1) * size, :]
+    for ref, step in zip(out_refs, far_first(pieces)):
+        ref[...] = placed[step * size : (step + 1) * size, :]
 
 
 def group_kernel(*refs):
     *part_refs, keep_ref, send_ref = refs
     size = part_refs[0].shape[0] // 2
-    for index, ref in enumerate(part_refs):
-        cut = slice(index * size, (index + 1) * size)
+    for ref, step in zip(part_refs, far_first(len(part_refs))):
+        cut = slice(step * size, (step + 1) * size)
         keep_ref[cut, :] = ref[:size, :]
         send_ref[cut, :] = ref[size:, :]
 
@@ -329,14 +347,25 @@
     return normal_cdf + pre_act * density
 
 
+def slope_kernel(pieces, pre_hbm, slope_ref, pre, sems):
+    rows = pre.shape[0] // pieces
+    copies = []
+    for piece in range(pieces):
+        cut = pl.ds(piece * rows, rows)
+        copies.append(pltpu.make_async_copy(pre_hbm.at[0, cut], pre.at[cut], sems.at[piece]))
+        copies[-1].start()
+    for piece, copy in enumerate(copies):
+        copy.wait()
+        cut = slice(piece * rows, (piece + 1) * rows)
+        slope_ref[cut, :] = slope(pre[cut, :].astype(F32))
+
+
 def final_kernel(capacity, share, turn, base, *refs):
-    part_ref, pre_hbm = refs[:2]
-    out_hbm, pre, out, sems = refs[-4:]
-    rows, slots = pre.shape
-    part = lax.rem(lax.axis_index("frame") + turn, share) * (pre_hbm.shape[1] // share)
+    part_ref, slope_ref = refs[:2]
+    out_hbm, out, sem = refs[-3:]
+    rows, slots = out.shape
+    part = lax.rem(lax.axis_index("frame") + turn, share) * (slope_ref.shape[0] // share)
     cut = pl.ds(pl.multiple_of(part + base, rows), rows)
-    load = pltpu.make_async_copy(pre_hbm.at[0, cut], pre, sems.at[0])
-    load.start()
     source = lax.broadcasted_iota(jnp.int32, (slots, slots), 0)
     goal = lax.broadcasted_iota(jnp.int32, (slots, slots), 1)
     moved = (goal ^ ((lax.axis_index("frame") ^ turn) * capacity)) == source
@@ -346,9 +375,8 @@
         (((0,), (0,)), ((), ())),
         preferred_element_type=F32,
     )
-    load.wait()
-    out[...] = (hidden * slope(pre[...].astype(F32))).astype(BF16)
-    store = pltpu.make_async_copy(out, out_hbm.at[0, cut], sems.at[1])
+    out[...] = (hidden * slope_ref[cut, :]).astype(BF16)
+    store = pltpu.make_async_copy(out, out_hbm.at[0, cut], sem.at[0])
     store.start()
     store.wait()
 
@@ -455,19 +483,17 @@
             [pltpu.VMEM((width, share * tokens), BF16)] + (weights if index else []),
             cost=2 * peers * rows * width,
         )(w_down if index else preloaded, *gradts)
-        return [partial[0]] + [swap(partial[k], "seq", peers, k) for k in range(1, peers)]
-
-    def place(parts):
+        return swaps(partial, "seq", peers)
+
+    def place(parts, after=()):
         rows = parts[0].shape[0]
         placed = chain.call(
             functools.partial(place_kernel, capacity, share, pieces, len(parts)),
             [shape((slots * share // pieces, rows), BF16)] * pieces,
-            [VMEM] * (share + len(parts)),
-        )(*gradts, *parts)
+            [VMEM] * (share + len(parts)) + [ANY] * len(after),
+        )(*gradts, *parts, *after)
         if paired:
-            return [placed[0]] + [
-                swap(placed[k], "frame", owners_count, 2 * k) for k in range(1, pieces)
-            ]
+            return swaps(placed, "frame", owners_count, 2)
         order = jnp.arange(owners_count) ^ lax.axis_index("frame")
         split = placed[0].reshape(owners_count, capacity, rows)[order]
         split = lax.all_to_all(split, "frame", split_axis=0, concat_axis=0, tiled=True)
@@ -489,20 +515,27 @@
             held = chain.call(
                 functools.partial(final_kernel, capacity, share, turn, bases[index]),
                 [shape(pre_owned.shape, BF16)],
-                [VMEM, HBM] + [HBM] * len(held),
-                [pltpu.VMEM((rows, slots), BF16), pltpu.VMEM((rows, slots), BF16), dma((2,))],
+                [VMEM, VMEM] + [HBM] * len(held),
+                [pltpu.VMEM((rows, slots), BF16), dma((1,))],
                 {2: 0} if held else None,
                 [HBM],
-            )(part, pre_owned, *held)
+            )(part, slopes, *held)
         return held
 
     waiting = [down(0), down(1)]
-    placed = place(waiting[0])
+    (slopes,) = chain.call(
+        functools.partial(slope_kernel, 4),
+        [shape(pre_owned.shape[1:], F32)],
+        [HBM],
+        [pltpu.VMEM(pre_owned.shape[1:], BF16), dma((4,))],
+    )(pre_owned)
+    placed = place(waiting[0], waiting[1][-1:])
     (ques_grad,) = chain.call(
         ques_kernel,
         [shape(ques_hidden.shape, BF16)],
         [HBM, VMEM, HBM],
         [pltpu.SMEM((1, 2), jnp.int32), pltpu.VMEM((tokens, width), BF16), dma((2,))],
+        cost=400000000,
     )(ques_span, logit, vis_proj)
     held = []
     for index in range(len(chunks)):

time: 79.1 us -> 79.7 us (level)
  waiting for transfers between devices: 20.9 us -> 23.9 us
  local copies, waits for them, and re-layouts: 6.84 us -> 4.37 us
    ppermute x21, waiting for transfers between devices: 20.9 us -> 23.9 us  [swap(): return lax.ppermute(value, axis, [(i, i ^ step) for i in range(count)])]
    unnamed x22 -> x20, local copies, waits for them, and re-layouts: 6.84 us -> 4.37 us
    pallas_call x12 -> x13, Pallas kernels: 17.6 us -> 17.4 us  [apply(): *results, token = run_call(*args, *self.last)]
  transfers between devices with their start and end apart: 21 -> 21, of which waited for: 7 -> 8; matrix products, arithmetic and copies ran while one was open for 0% -> 0% of each run, Pallas kernels for 22% -> 23%
where the time goes in v1:
time: 79.7 us; the launch traced here: 79.4 us
  Pallas kernels  25.8 us (32%)
  starting transfers between devices  24.4 us (31%)
  waiting for transfers between devices  23.9 us (30%)
  local copies, waits for them, and re-layouts  4.37 us (5%)
  between operations  0.91 us (1%)
    ppermute x21, starting transfers between devices, swap(): return lax.ppermute(value, axis, [(i, i ^ step) for i in range(count)])  24.4 us
    ppermute x21, waiting for transfers between devices, swap(): return lax.ppermute(value, axis, [(i, i ^ step) for i in range(count)])  23.9 us
    pallas_call x13, Pallas kernels, apply(): *results, token = run_call(*args, *self.last)  17.4 us
    unnamed x20, local copies, waits for them, and re-layouts  4.37 us
    pallas_call x1, Pallas kernels, body(): call(functools.partial(preload_kernel, peers, share, chunks[0]), shape((p...  3.47 us
    pallas_call x1, Pallas kernels, body(): call(functools.partial(pick_kernel, pieces), shape((tokens, key_width), B...  2.15 us
    pallas_call x1, Pallas kernels, body(): call(load_kernel, [row, tall, tall, tall, tall, shape(w_value.shape, BF16...  1.86 us
  transfers between devices with their start and end apart: 21, of which 8 were waited for; matrix products, arithmetic and copies ran while one was open for 0% of the time, Pallas kernels for 23%

profile of v1, /device:TPU:0, one launch (start us, length us, event | category | flops | bytes accessed | tf_op | source)
XLA Modules:
  0.0 79.4 jit_solution(15970985919852245641)
XLA Ops:
  0.6 2.1 %shard_map.122.refs_0_ = bf16[128,512]{1,0:T(8,128)(2,1)} custom-call(s32[1,128]{1,0:T(1,128)} %pos_hbm.1, bf16[1,1024,512]{2,1,0:T(8,128)(2,1)} %rows_hbm.1), custom_call_target="tpu_custom_call" | custom-call | flops 262144 | bytes 1024 | tf_op jit(solution)/shard_map/pallas_call | solution.py:416
  2.8 4.0 %collective-permute-start.2 = (bf16[128,512]{1,0:T(8,128)(2,1)}, bf16[128,512]{1,0:T(8,128)(2,1)S(1)}, u32[]{:S(2)}, u32[]{:S(2)}) collective-permute-start(bf16[128,512]{1,0:T(8,128)(2,1)} %shard_map.122.refs_0_), channel_id=1, source_target_pairs={{0,24},{8,16},{16,8},{24,0},{1,25},{9,17},{17,9},{25,1},{2,26},{10... | collective-permute-start | bytes 393224 | tf_op jit(solution)/shard_map/ppermute | solution.py:76
  7.4 1.0 %copy-done.2 = bf16[1,128,2048]{2,1,0:T(8,128)(2,1)S(1)} copy-done((bf16[1,128,2048]{2,1,0:T(8,128)(2,1)S(1)}, bf16[1,128,2048]{2,1,0:T(8,128)(2,1)}, u32[]{:S(2)}) %copy-start.2) | copy-done | bytes 524312
  8.4 1.0 %copy-done.3 = bf16[1,128,2048]{2,1,0:T(8,128)(2,1)S(1)} copy-done((bf16[1,128,2048]{2,1,0:T(8,128)(2,1)S(1)}, bf16[1,128,2048]{2,1,0:T(8,128)(2,1)}, u32[]{:S(2)}) %copy-start.3) | copy-done | bytes 524312
  11.7 1.9 %shard_map.123 = (f32[8,128]{1,0:T(8,128)S(1)}, f32[2048,128]{1,0:T(8,128)S(1)}, f32[2048,128]{1,0:T(8,128)S(1)}, f32[2048,128]{1,0:T(8,128)S(1)}, f32[2048,128]...) custom-call(s32[1,2]{1,0:T(1,128)S(1)} %copy-done.8, bf16[1,32,2048]{2,1,0:T(8,128)(2,1)S(1)} %copy-done.5, ...), custom_call_target="tpu_custom_call" | custom-call | flops 262144 | bytes 1024 | tf_op jit(solution)/shard_map/pallas_call | solution.py:429
  14.5 2.9 %collective-permute-start.5 = (f32[8,128]{1,0:T(8,128)S(1)}, f32[8,128]{1,0:T(8,128)S(1)}, u32[]{:S(2)}, u32[]{:S(2)}) collective-permute-start(f32[8,128]{1,0:T(8,128)S(1)} %get-tuple-element.54.after_ref.refs_0_), channel_id=1, source_target_pairs={{0,24},{8,16},{16,8},{24,0},{1,25},{9,17},{17,9},{25,1},{2,26},{10... | collective-permute-start | bytes 12296 | tf_op jit(solution)/shard_map/ppermute | solution.py:76
  18.1 3.5 %shard_map.125.refs_9_.refs_0_ = bf16[2048,2048]{1,0:T(8,128)(2,1)S(1)} custom-call(bf16[8192,2048]{1,0:T(8,128)(2,1)} %refs_0_.3, f32[8,128]{1,0:T(8,128)S(1)} %get-tuple-element.54.after_ref.refs_0_), custom_call_target="tpu_custom_call" | custom-call | flops 262144 | bytes 1024 | tf_op jit(solution)/shard_map/pallas_call | solution.py:462
  22.0 1.9 %collective-permute-done.6.refs_2_.refs_1_ = bf16[2064,128]{1,0:T(8,128)(2,1)S(1)} collective-permute-done((bf16[2064,128]{1,0:T(8,128)(2,1)S(1)}, bf16[2064,128]{1,0:T(8,128)(2,1)S(1)}, u32[]{:S(2)}, u32[]{:S(2)}) %collective-permute-start.6) | collective-permute-done | bytes 528416 | tf_op jit(solution)/shard_map/ppermute | solution.py:76
  23.9 2.4 %shard_map.127 = (bf16[512,256]{1,0:T(8,128)(2,1)S(1)}, bf16[512,256]{1,0:T(8,128)(2,1)S(1)}, bf16[512,256]{1,0:T(8,128)(2,1)S(1)}, bf16[512,256]{1,0:T(8,128)(2,1)S(1)}, f32[8,128]{1,0:T(8,128)S(1)}) custom-call(bf16[2048,2048]{1,0:T(8,128)(2,1)S(1)} %shard_map.125.refs_9_.refs_0_, bf16[2064,128]{1,0:T(8,128)(2,1)S(1)} %get-tuple-element.58.refs_1_.refs_0_, ...), custom_call_target="tpu_custom_call" | custom-call | flops 2147483648 | bytes 8388608 | tf_op jit(solution)/shard_map/pallas_call | solution.py:64
  26.2 2.9 %collective-permute-start.10 = (bf16[512,256]{1,0:T(8,128)(2,1)S(1)}, bf16[512,256]{1,0:T(8,128)(2,1)S(1)}, u32[]{:S(2)}, u32[]{:S(2)}) collective-permute-start(bf16[512,256]{1,0:T(8,128)(2,1)S(1)} %get-tuple-element.66), channel_id=1, source_target_pairs={{0,24},{8,16},{16,8},{24,0},{1,25},{9,17},{17,9},{25,1},{2,26},{10... | collective-permute-start | bytes 786440 | tf_op jit(solution)/shard_map/ppermute | solution.py:76
  29.8 6.9 %shard_map.128 = (bf16[512,256]{1,0:T(8,128)(2,1)S(1)}, bf16[512,256]{1,0:T(8,128)(2,1)S(1)}, bf16[512,256]{1,0:T(8,128)(2,1)S(1)}, bf16[512,256]{1,0:T(8,128)(2,1)S(1)}, f32[8,128]{1,0:T(8,128)S(1)}) custom-call(bf16[8192,2048]{1,0:T(8,128)(2,1)} %refs_0_.3, bf16[2064,128]{1,0:T(8,128)(2,1)S(1)} %get-tuple-element.58.refs_1_.refs_0_, ...), custom_call_target="tpu_custom_call" | custom-call | flops 2147483648 | bytes 8388608 | tf_op jit(solution)/shard_map/pallas_call | solution.py:64
  36.8 2.0 %collective-permute-start.9 = (bf16[512,256]{1,0:T(8,128)(2,1)S(1)}, bf16[512,256]{1,0:T(8,128)(2,1)S(1)}, u32[]{:S(2)}, u32[]{:S(2)}) collective-permute-start(bf16[512,256]{1,0:T(8,128)(2,1)S(1)} %get-tuple-element.64), channel_id=1, source_target_pairs={{0,8},{8,0},{16,24},{24,16},{1,9},{9,1},{17,25},{25,17},{2,10},{10... | collective-permute-start | bytes 786440 | tf_op jit(solution)/shard_map/ppermute | solution.py:76
  38.7 1.5 %collective-permute-start.7 = (bf16[512,256]{1,0:T(8,128)(2,1)S(1)}, bf16[512,256]{1,0:T(8,128)(2,1)S(1)}, u32[]{:S(2)}, u32[]{:S(2)}) collective-permute-start(bf16[512,256]{1,0:T(8,128)(2,1)S(1)} %get-tuple-element.62), channel_id=1, source_target_pairs={{0,24},{8,16},{16,8},{24,0},{1,25},{9,17},{17,9},{25,1},{2,26},{10... | collective-permute-start | bytes 786440 | tf_op jit(solution)/shard_map/ppermute | solution.py:76
  41.4 1.1 %collective-permute-done.12.refs_5_ = bf16[512,256]{1,0:T(8,128)(2,1)S(1)} collective-permute-done((bf16[512,256]{1,0:T(8,128)(2,1)S(1)}, bf16[512,256]{1,0:T(8,128)(2,1)S(1)}, u32[]{:S(2)}, u32[]{:S(2)}) %collective-permute-start.12) | collective-permute-done | bytes 262176 | tf_op jit(solution)/shard_map/ppermute | solution.py:76
  42.5 5.6 %collective-permute-done.9.refs_6_.refs_5_ = bf16[512,256]{1,0:T(8,128)(2,1)S(1)} collective-permute-done((bf16[512,256]{1,0:T(8,128)(2,1)S(1)}, bf16[512,256]{1,0:T(8,128)(2,1)S(1)}, u32[]{:S(2)}, u32[]{:S(2)}) %collective-permute-start.9) | collective-permute-done | bytes 262176 | tf_op jit(solution)/shard_map/ppermute | solution.py:76
  48.5 3.7 %collective-permute-start.13 = (bf16[128,512]{1,0:T(8,128)(2,1)S(1)}, bf16[128,512]{1,0:T(8,128)(2,1)S(1)}, u32[]{:S(2)}, u32[]{:S(2)}) collective-permute-start(bf16[128,512]{1,0:T(8,128)(2,1)S(1)} %get-tuple-element.72), channel_id=1, source_target_pairs={{0,6},{1,7},{2,4},{3,5},{4,2},{5,3},{6,0},{7,1},{8,14},{9,15},{10,... | collective-permute-start | bytes 393224 | tf_op jit(solution)/shard_map/ppermute | solution.py:76
  53.0 1.5 %shard_map.131 = (bf16[1,32,2048]{2,1,0:T(8,128)(2,1)}, f32[8,128]{1,0:T(8,128)S(1)}) custom-call(s32[1,2]{1,0:T(1,128)S(1)} %copy-done.9, f32[8,128]{1,0:T(8,128)S(1)} %get-tuple-element.75.refs_1_, bf16[1,128,2048]{2,1,0:T(8,128)(2,1)S(1)} %copy-done.4, f32[8,128]{1,0:T(8,128)S(1)} %get-tuple-element.76.refs_3_), custom_call_target="tpu_custom_call" | custom-call | flops 102400000000 | bytes 400000000 | tf_op jit(solution)/shard_map/pallas_call | solution.py:64
  54.5 2.0 %collective-permute-done.13.refs_1_ = bf16[128,512]{1,0:T(8,128)(2,1)S(1)} collective-permute-done((bf16[128,512]{1,0:T(8,128)(2,1)S(1)}, bf16[128,512]{1,0:T(8,128)(2,1)S(1)}, u32[]{:S(2)}, u32[]{:S(2)}) %collective-permute-start.13) | collective-permute-done | bytes 131104 | tf_op jit(solution)/shard_map/ppermute | solution.py:76
  56.5 5.4 %collective-permute-done.14.refs_2_ = bf16[128,512]{1,0:T(8,128)(2,1)S(1)} collective-permute-done((bf16[128,512]{1,0:T(8,128)(2,1)S(1)}, bf16[128,512]{1,0:T(8,128)(2,1)S(1)}, u32[]{:S(2)}, u32[]{:S(2)}) %collective-permute-start.14) | collective-permute-done | bytes 131104 | tf_op jit(solution)/shard_map/ppermute | solution.py:76
  62.5 2.5 %collective-permute-start.16 = (bf16[128,512]{1,0:T(8,128)(2,1)S(1)}, bf16[128,512]{1,0:T(8,128)(2,1)S(1)}, u32[]{:S(2)}, u32[]{:S(2)}) collective-permute-start(bf16[128,512]{1,0:T(8,128)(2,1)S(1)} %get-tuple-element.80), channel_id=1, source_target_pairs={{0,6},{1,7},{2,4},{3,5},{4,2},{5,3},{6,0},{7,1},{8,14},{9,15},{10,... | collective-permute-start | bytes 393224 | tf_op jit(solution)/shard_map/ppermute | solution.py:76
  65.0 1.9 %collective-permute-start.18 = (bf16[128,512]{1,0:T(8,128)(2,1)S(1)}, bf16[128,512]{1,0:T(8,128)(2,1)S(1)}, u32[]{:S(2)}, u32[]{:S(2)}) collective-permute-start(bf16[128,512]{1,0:T(8,128)(2,1)S(1)} %get-tuple-element.82), channel_id=1, source_target_pairs={{0,2},{1,3},{2,0},{3,1},{4,6},{5,7},{6,4},{7,5},{8,10},{9,11},{10,... | collective-permute-start | bytes 393224 | tf_op jit(solution)/shard_map/ppermute | solution.py:76
  69.0 1.9 %collective-permute-done.16.refs_1_ = bf16[128,512]{1,0:T(8,128)(2,1)S(1)} collective-permute-done((bf16[128,512]{1,0:T(8,128)(2,1)S(1)}, bf16[128,512]{1,0:T(8,128)(2,1)S(1)}, u32[]{:S(2)}, u32[]{:S(2)}) %collective-permute-start.16) | collective-permute-done | bytes 131104 | tf_op jit(solution)/shard_map/ppermute | solution.py:76
  70.8 5.3 %collective-permute-done.17.refs_2_ = bf16[128,512]{1,0:T(8,128)(2,1)S(1)} collective-permute-done((bf16[128,512]{1,0:T(8,128)(2,1)S(1)}, bf16[128,512]{1,0:T(8,128)(2,1)S(1)}, u32[]{:S(2)}, u32[]{:S(2)}) %collective-permute-start.17) | collective-permute-done | bytes 131104 | tf_op jit(solution)/shard_map/ppermute | solution.py:76
  77.8 1.6 %shard_map.138 = (bf16[1,2048,256]{2,1,0:T(8,128)(2,1)}, f32[8,128]{1,0:T(8,128)}) custom-call(bf16[256,512]{1,0:T(8,128)(2,1)S(1)} %collective-permute-done.20.refs_0_, f32[2048,256]{1,0:T(8,128)S(1)} %get-tuple-element.84.refs_1_, bf16[1,2048,256]{2,1,0:T(8,128)(2,1)} %get-tuple-element.94.refs_2_, ...), custom_call_target="tpu_custom_call", output_to_operand_aliasing={{0}: (2, {})} | custom-call | flops 262144 | bytes 1024 | tf_op jit(solution)/shard_map/pallas_call | solution.py:64
  (55 shorter events, 12.0 us)
Async XLA Ops:
  2.8 10.9 %copy-start.1 = (bf16[128,512]{1,0:T(8,128)(2,1)S(1)}, bf16[128,512]{1,0:T(8,128)(2,1)}, u32[]{:S(2)}) copy-start(bf16[128,512]{1,0:T(8,128)(2,1)} %shard_map.122.refs_0_) | copy-start | bytes 393220
  2.8 10.8 %collective-permute-start.2 = (bf16[128,512]{1,0:T(8,128)(2,1)}, bf16[128,512]{1,0:T(8,128)(2,1)S(1)}, u32[]{:S(2)}, u32[]{:S(2)}) collective-permute-start(bf16[128,512]{1,0:T(8,128)(2,1)} %shard_map.122.refs_0_), channel_id=1, source_target_pairs={{0,24},{8,16},{16,8},{24,0},{1,25},{9,17},{17,9},{25,1},{2,26},{10... | collective-permute-start | bytes 393224 | tf_op jit(solution)/shard_map/ppermute | solution.py:76
  6.8 6.9 %collective-permute-start.1 = (bf16[128,512]{1,0:T(8,128)(2,1)}, bf16[128,512]{1,0:T(8,128)(2,1)S(1)}, u32[]{:S(2)}, u32[]{:S(2)}) collective-permute-start(bf16[128,512]{1,0:T(8,128)(2,1)} %shard_map.122.refs_0_), channel_id=1, source_target_pairs={{0,16},{8,24},{16,0},{24,8},{1,17},{9,25},{17,1},{25,9},{2,18},{10... | collective-permute-start | bytes 393224 | tf_op jit(solution)/shard_map/ppermute | solution.py:76
  7.3 6.4 %collective-permute-start = (bf16[128,512]{1,0:T(8,128)(2,1)}, bf16[128,512]{1,0:T(8,128)(2,1)S(1)}, u32[]{:S(2)}, u32[]{:S(2)}) collective-permute-start(bf16[128,512]{1,0:T(8,128)(2,1)} %shard_map.122.refs_0_), channel_id=1, source_target_pairs={{0,8},{8,0},{16,24},{24,16},{1,9},{9,1},{17,25},{25,17},{2,10},{10... | collective-permute-start | bytes 393224 | tf_op jit(solution)/shard_map/ppermute | solution.py:76
  14.5 7.0 %collective-permute-start.5 = (f32[8,128]{1,0:T(8,128)S(1)}, f32[8,128]{1,0:T(8,128)S(1)}, u32[]{:S(2)}, u32[]{:S(2)}) collective-permute-start(f32[8,128]{1,0:T(8,128)S(1)} %get-tuple-element.54.after_ref.refs_0_), channel_id=1, source_target_pairs={{0,24},{8,16},{16,8},{24,0},{1,25},{9,17},{17,9},{25,1},{2,26},{10... | collective-permute-start | bytes 12296 | tf_op jit(solution)/shard_map/ppermute | solution.py:76
  17.4 4.1 %collective-permute-start.4 = (f32[8,128]{1,0:T(8,128)S(1)}, f32[8,128]{1,0:T(8,128)S(1)}, u32[]{:S(2)}, u32[]{:S(2)}) collective-permute-start(f32[8,128]{1,0:T(8,128)S(1)} %get-tuple-element.54.after_ref.refs_0_), channel_id=1, source_target_pairs={{0,16},{8,24},{16,0},{24,8},{1,17},{9,25},{17,1},{25,9},{2,18},{10... | collective-permute-start | bytes 12296 | tf_op jit(solution)/shard_map/ppermute | solution.py:76
  17.9 3.6 %collective-permute-start.3 = (f32[8,128]{1,0:T(8,128)S(1)}, f32[8,128]{1,0:T(8,128)S(1)}, u32[]{:S(2)}, u32[]{:S(2)}) collective-permute-start(f32[8,128]{1,0:T(8,128)S(1)} %get-tuple-element.54.after_ref.refs_0_), channel_id=1, source_target_pairs={{0,8},{8,0},{16,24},{24,16},{1,9},{9,1},{17,25},{25,17},{2,10},{10... | collective-permute-start | bytes 12296 | tf_op jit(solution)/shard_map/ppermute | solution.py:76
  21.9 2.0 %collective-permute-start.6 = (bf16[2064,128]{1,0:T(8,128)(2,1)S(1)}, bf16[2064,128]{1,0:T(8,128)(2,1)S(1)}, u32[]{:S(2)}, u32[]{:S(2)}) collective-permute-start(bf16[2064,128]{1,0:T(8,128)(2,1)S(1)} %get-tuple-element.58.refs_1_.refs_0_), channel_id=1, source_target_pairs={{0,1},{1,0},{2,3},{3,2},{4,5},{5,4},{6,7},{7,6},{8,9},{9,8},{10,11... | collective-permute-start | bytes 1585160 | tf_op jit(solution)/shard_map/ppermute | solution.py:76
  26.2 14.9 %collective-permute-start.10 = (bf16[512,256]{1,0:T(8,128)(2,1)S(1)}, bf16[512,256]{1,0:T(8,128)(2,1)S(1)}, u32[]{:S(2)}, u32[]{:S(2)}) collective-permute-start(bf16[512,256]{1,0:T(8,128)(2,1)S(1)} %get-tuple-element.66), channel_id=1, source_target_pairs={{0,24},{8,16},{16,8},{24,0},{1,25},{9,17},{17,9},{25,1},{2,26},{10... | collective-permute-start | bytes 786440 | tf_op jit(solution)/shard_map/ppermute | solution.py:76
  29.1 12.2 %collective-permute-start.11 = (bf16[512,256]{1,0:T(8,128)(2,1)S(1)}, bf16[512,256]{1,0:T(8,128)(2,1)S(1)}, u32[]{:S(2)}, u32[]{:S(2)}) collective-permute-start(bf16[512,256]{1,0:T(8,128)(2,1)S(1)} %get-tuple-element.67), channel_id=1, source_target_pairs={{0,16},{8,24},{16,0},{24,8},{1,17},{9,25},{17,1},{25,9},{2,18},{10... | collective-permute-start | bytes 786440 | tf_op jit(solution)/shard_map/ppermute | solution.py:76
  29.7 12.8 %collective-permute-start.12 = (bf16[512,256]{1,0:T(8,128)(2,1)S(1)}, bf16[512,256]{1,0:T(8,128)(2,1)S(1)}, u32[]{:S(2)}, u32[]{:S(2)}) collective-permute-start(bf16[512,256]{1,0:T(8,128)(2,1)S(1)} %get-tuple-element.68), channel_id=1, source_target_pairs={{0,8},{8,0},{16,24},{24,16},{1,9},{9,1},{17,25},{25,17},{2,10},{10... | collective-permute-start | bytes 786440 | tf_op jit(solution)/shard_map/ppermute | solution.py:76
  36.7 16.3 %copy-start.4 = (bf16[1,128,2048]{2,1,0:T(8,128)(2,1)S(1)}, bf16[1,128,2048]{2,1,0:T(8,128)(2,1)}, u32[]{:S(2)}) copy-start(bf16[1,128,2048]{2,1,0:T(8,128)(2,1)} %refs_2_.1) | copy-start | bytes 1572868
  36.7 16.3 %copy-start.9 = (s32[1,2]{1,0:T(1,128)S(1)}, s32[1,2]{1,0:T(1,128)}, u32[]{:S(2)}) copy-start(s32[1,2]{1,0:T(1,128)} %refs_0_.5) | copy-start | bytes 28
  36.8 11.3 %collective-permute-start.9 = (bf16[512,256]{1,0:T(8,128)(2,1)S(1)}, bf16[512,256]{1,0:T(8,128)(2,1)S(1)}, u32[]{:S(2)}, u32[]{:S(2)}) collective-permute-start(bf16[512,256]{1,0:T(8,128)(2,1)S(1)} %get-tuple-element.64), channel_id=1, source_target_pairs={{0,8},{8,0},{16,24},{24,16},{1,9},{9,1},{17,25},{25,17},{2,10},{10... | collective-permute-start | bytes 786440 | tf_op jit(solution)/shard_map/ppermute | solution.py:76
  38.7 23.4 %collective-permute-start.7 = (bf16[512,256]{1,0:T(8,128)(2,1)S(1)}, bf16[512,256]{1,0:T(8,128)(2,1)S(1)}, u32[]{:S(2)}, u32[]{:S(2)}) collective-permute-start(bf16[512,256]{1,0:T(8,128)(2,1)S(1)} %get-tuple-element.62), channel_id=1, source_target_pairs={{0,24},{8,16},{16,8},{24,0},{1,25},{9,17},{17,9},{25,1},{2,26},{10... | collective-permute-start | bytes 786440 | tf_op jit(solution)/shard_map/ppermute | solution.py:76
  41.2 20.9 %collective-permute-start.8 = (bf16[512,256]{1,0:T(8,128)(2,1)S(1)}, bf16[512,256]{1,0:T(8,128)(2,1)S(1)}, u32[]{:S(2)}, u32[]{:S(2)}) collective-permute-start(bf16[512,256]{1,0:T(8,128)(2,1)S(1)} %get-tuple-element.63), channel_id=1, source_target_pairs={{0,16},{8,24},{16,0},{24,8},{1,17},{9,25},{17,1},{25,9},{2,18},{10... | collective-permute-start | bytes 786440 | tf_op jit(solution)/shard_map/ppermute | solution.py:76
  48.5 8.0 %collective-permute-start.13 = (bf16[128,512]{1,0:T(8,128)(2,1)S(1)}, bf16[128,512]{1,0:T(8,128)(2,1)S(1)}, u32[]{:S(2)}, u32[]{:S(2)}) collective-permute-start(bf16[128,512]{1,0:T(8,128)(2,1)S(1)} %get-tuple-element.72), channel_id=1, source_target_pairs={{0,6},{1,7},{2,4},{3,5},{4,2},{5,3},{6,0},{7,1},{8,14},{9,15},{10,... | collective-permute-start | bytes 393224 | tf_op jit(solution)/shard_map/ppermute | solution.py:76
  52.2 9.7 %collective-permute-start.14 = (bf16[128,512]{1,0:T(8,128)(2,1)S(1)}, bf16[128,512]{1,0:T(8,128)(2,1)S(1)}, u32[]{:S(2)}, u32[]{:S(2)}) collective-permute-start(bf16[128,512]{1,0:T(8,128)(2,1)S(1)} %get-tuple-element.73), channel_id=1, source_target_pairs={{0,4},{1,5},{2,6},{3,7},{4,0},{5,1},{6,2},{7,3},{8,12},{9,13},{10,... | collective-permute-start | bytes 393224 | tf_op jit(solution)/shard_map/ppermute | solution.py:76
  52.2 9.7 %collective-permute-start.15 = (bf16[128,512]{1,0:T(8,128)(2,1)S(1)}, bf16[128,512]{1,0:T(8,128)(2,1)S(1)}, u32[]{:S(2)}, u32[]{:S(2)}) collective-permute-start(bf16[128,512]{1,0:T(8,128)(2,1)S(1)} %get-tuple-element.74), channel_id=1, source_target_pairs={{0,2},{1,3},{2,0},{3,1},{4,6},{5,7},{6,4},{7,5},{8,10},{9,11},{10,... | collective-permute-start | bytes 393224 | tf_op jit(solution)/shard_map/ppermute | solution.py:76
  62.0 6.0 %collective-permute-start.19 = (bf16[256,512]{1,0:T(8,128)(2,1)S(1)}, bf16[256,512]{1,0:T(8,128)(2,1)S(1)}, u32[]{:S(2)}, u32[]{:S(2)}) collective-permute-start(bf16[256,512]{1,0:T(8,128)(2,1)S(1)} %get-tuple-element.83), channel_id=1, source_target_pairs={{0,1},{1,0},{2,3},{3,2},{4,5},{5,4},{6,7},{7,6},{8,9},{9,8},{10,11... | collective-permute-start | bytes 786440 | tf_op jit(solution)/shard_map/ppermute | solution.py:76
  62.5 8.3 %collective-permute-start.16 = (bf16[128,512]{1,0:T(8,128)(2,1)S(1)}, bf16[128,512]{1,0:T(8,128)(2,1)S(1)}, u32[]{:S(2)}, u32[]{:S(2)}) collective-permute-start(bf16[128,512]{1,0:T(8,128)(2,1)S(1)} %get-tuple-element.80), channel_id=1, source_target_pairs={{0,6},{1,7},{2,4},{3,5},{4,2},{5,3},{6,0},{7,1},{8,14},{9,15},{10,... | collective-permute-start | bytes 393224 | tf_op jit(solution)/shard_map/ppermute | solution.py:76
  65.0 11.1 %collective-permute-start.17 = (bf16[128,512]{1,0:T(8,128)(2,1)S(1)}, bf16[128,512]{1,0:T(8,128)(2,1)S(1)}, u32[]{:S(2)}, u32[]{:S(2)}) collective-permute-start(bf16[128,512]{1,0:T(8,128)(2,1)S(1)} %get-tuple-element.81), channel_id=1, source_target_pairs={{0,4},{1,5},{2,6},{3,7},{4,0},{5,1},{6,2},{7,3},{8,12},{9,13},{10,... | collective-permute-start | bytes 393224 | tf_op jit(solution)/shard_map/ppermute | solution.py:76
  65.0 11.1 %collective-permute-start.18 = (bf16[128,512]{1,0:T(8,128)(2,1)S(1)}, bf16[128,512]{1,0:T(8,128)(2,1)S(1)}, u32[]{:S(2)}, u32[]{:S(2)}) collective-permute-start(bf16[128,512]{1,0:T(8,128)(2,1)S(1)} %get-tuple-element.82), channel_id=1, source_target_pairs={{0,2},{1,3},{2,0},{3,1},{4,6},{5,7},{6,4},{7,5},{8,10},{9,11},{10,... | collective-permute-start | bytes 393224 | tf_op jit(solution)/shard_map/ppermute | solution.py:76
  76.2 1.6 %collective-permute-start.20 = (bf16[256,512]{1,0:T(8,128)(2,1)S(1)}, bf16[256,512]{1,0:T(8,128)(2,1)S(1)}, u32[]{:S(2)}, u32[]{:S(2)}) collective-permute-start(bf16[256,512]{1,0:T(8,128)(2,1)S(1)} %get-tuple-element.90), channel_id=1, source_target_pairs={{0,1},{1,0},{2,3},{3,2},{4,5},{5,4},{6,7},{7,6},{8,9},{9,8},{10,11... | collective-permute-start | bytes 786440 | tf_op jit(solution)/shard_map/ppermute | solution.py:76
  (7 other events, 21.8 us)

commit v2 on v1

--- a/solution.py
+++ b/solution.py
@@ -12,7 +12,7 @@
 F32 = jnp.float32
 BF16 = jnp.bfloat16
 LANES = 128
-AHEAD = 3
+AHEAD = 6
 MIB = 1024 * 1024
 GRANT, LOAD_GRANT, PICK_GRANT = 40, 46, 54
 HBM = pl.BlockSpec(memory_space=pltpu.HBM)
@@ -193,12 +193,12 @@
     sums_ref[3:4, :] = jnp.sum(total, axis=0, keepdims=True)
 
 
-def weight_copies(weight_hbm, weights, sems, peers, share, base, rows):
+def weight_copies(weight_hbm, weights, sems, steps, peers, share, base, rows):
     quarter = weight_hbm.shape[0] // peers
     block = min(rows, 256)
     part = lax.rem(lax.axis_index("frame"), share) * (quarter // share)
     copies = []
-    for peer, step in enumerate(far_first(peers)):
+    for peer, step in enumerate(steps):
         first = (lax.axis_index("seq") ^ step) * quarter + part + base
         for at in range(0, rows, block):
             index = len(copies)
@@ -212,9 +212,9 @@
     return copies
 
 
-def preload_kernel(peers, share, rows, weight_hbm, after_ref, weights_ref, sems):
+def preload_kernel(steps, peers, share, rows, weight_hbm, after_ref, weights_ref, sems):
     del after_ref
-    copies = weight_copies(weight_hbm, weights_ref, sems, peers, share, 0, rows)
+    copies = weight_copies(weight_hbm, weights_ref, sems, steps, peers, share, 0, rows)
     for copy in copies:
         copy.start()
     for copy in copies:
@@ -248,17 +248,19 @@
 
 
 def down_kernel(peers, share, base, rows, held, *refs):
-    weight_ref = refs[0]
-    gradt_refs = refs[1 : 1 + share]
-    out_refs = refs[1 + share : 1 + share + peers]
-    scratch = list(refs[1 + share + peers :])
+    weight_refs = refs[: max(held, 1)]
+    gradt_refs = refs[len(weight_refs) : len(weight_refs) + share]
+    scratch = list(refs[len(weight_refs) + share :])
+    out_refs = [scratch.pop(0) for _ in range(peers)]
     joined = scratch.pop(0)
     copies = []
     if held:
-        weights = weight_ref
+        weights = weight_refs
     else:
-        weights, sems = scratch
-        copies = weight_copies(weight_ref, weights, sems, peers, share, base, rows)
+        weights, sems = scratch[:1], scratch[1]
+        copies = weight_copies(
+            weight_refs[0], weights[0], sems, far_first(peers), peers, share, base, rows
+        )
     for copy in copies[:AHEAD]:
         copy.start()
     width, tokens = joined.shape[0], gradt_refs[0].shape[1]
@@ -266,14 +268,16 @@
         joined[:, index * tokens : (index + 1) * tokens] = ref[:width, :]
     block = min(rows, 256)
     inner = rows // block
+    each = peers * inner // len(weights)
     for index in range(peers * inner):
         peer, part = index // inner, index % inner
         if copies:
             copies[index].wait()
         if index + AHEAD < len(copies):
             copies[index + AHEAD].start()
+        place = index % each
         value = jnp.dot(
-            weights[index * block : (index + 1) * block, :],
+            weights[index // each][place * block : (place + 1) * block, :],
             joined[...],
             preferred_element_type=F32,
         )
@@ -456,42 +460,49 @@
     bases = [sum(chunks[:i]) for i in range(len(chunks))]
     chain = Chain()
 
-    def sems(rows):
-        return dma((peers * (rows // min(rows, 256)),))
-
-    preloaded = call(
-        functools.partial(preload_kernel, peers, share, chunks[0]),
-        shape((peers * chunks[0], width), BF16),
-        [HBM, VMEM],
-        [sems(chunks[0])],
-    )(w_down, sums)
-
+    def sems(rows, count=peers):
+        return dma((count * (rows // min(rows, 256)),))
+
+    def preload(caller, steps, after):
+        (weights,) = caller(
+            functools.partial(preload_kernel, steps, peers, share, chunks[0]),
+            [shape((len(steps) * chunks[0], width), BF16)],
+            [HBM, VMEM],
+            [sems(chunks[0], len(steps))],
+        )(w_down, after)
+        return weights
+
+    steps = far_first(peers)
+    preloaded = [preload(call, steps[: peers // 2], sums)]
     gradt, logit = chain.call(
         functools.partial(gate_kernel, features, peers),
         [shape((width + 16, tokens), BF16), row],
         [VMEM] * (peers + 5) + [ANY],
-    )(*sums_all, projt, residt, scaledt, meant, owner, preloaded)
+    )(*sums_all, projt, residt, scaledt, meant, owner, preloaded[0])
+    preloaded.append(preload(chain.call, steps[peers // 2 :], logit))
     gradts = [gradt] + [swap(gradt, "frame", owners_count, k) for k in range(1, share)]
 
     def down(index):
         rows = chunks[index]
         weights = [pltpu.VMEM((peers * rows, width), BF16), sems(rows)]
         partial = chain.call(
-            functools.partial(down_kernel, peers, share, bases[index], rows, index == 0),
+            functools.partial(
+                down_kernel, peers, share, bases[index], rows, 0 if index else len(preloaded)
+            ),
             [shape((rows, share * tokens), BF16)] * peers,
-            [VMEM if index == 0 else HBM] + [VMEM] * share,
+            ([HBM] if index else [VMEM] * len(preloaded)) + [VMEM] * share,
             [pltpu.VMEM((width, share * tokens), BF16)] + (weights if index else []),
             cost=2 * peers * rows * width,
-        )(w_down if index else preloaded, *gradts)
+        )(*([w_down] if index else preloaded), *gradts)
         return swaps(partial, "seq", peers)
 
-    def place(parts, after=()):
+    def place(parts):
         rows = parts[0].shape[0]
         placed = chain.call(
             functools.partial(place_kernel, capacity, share, pieces, len(parts)),
             [shape((slots * share // pieces, rows), BF16)] * pieces,
-            [VMEM] * (share + len(parts)) + [ANY] * len(after),
-        )(*gradts, *parts, *after)
+            [VMEM] * (share + len(parts)),
+        )(*gradts, *parts)
         if paired:
             return swaps(placed, "frame", owners_count, 2)
         order = jnp.arange(owners_count) ^ lax.axis_index("frame")
@@ -509,18 +520,16 @@
         )(*parts)
         return [keep, swap(send, "frame", owners_count, 1)]
 
-    def finish(parts, index, held):
+    def finish(parts, index, turn, held):
         rows = chunks[index]
-        for turn, part in enumerate(parts):
-            held = chain.call(
-                functools.partial(final_kernel, capacity, share, turn, bases[index]),
-                [shape(pre_owned.shape, BF16)],
-                [VMEM, VMEM] + [HBM] * len(held),
-                [pltpu.VMEM((rows, slots), BF16), dma((1,))],
-                {2: 0} if held else None,
-                [HBM],
-            )(part, slopes, *held)
-        return held
+        return chain.call(
+            functools.partial(final_kernel, capacity, share, turn, bases[index]),
+            [shape(pre_owned.shape, BF16)],
+            [VMEM, VMEM] + [HBM] * len(held),
+            [pltpu.VMEM((rows, slots), BF16), dma((1,))],
+            {2: 0} if held else None,
+            [HBM],
+        )(parts[turn], slopes, *held)
 
     waiting = [down(0), down(1)]
     (slopes,) = chain.call(
@@ -529,7 +538,6 @@
         [HBM],
         [pltpu.VMEM(pre_owned.shape[1:], BF16), dma((4,))],
     )(pre_owned)
-    placed = place(waiting[0], waiting[1][-1:])
     (ques_grad,) = chain.call(
         ques_kernel,
         [shape(ques_hidden.shape, BF16)],
@@ -537,14 +545,14 @@
         [pltpu.SMEM((1, 2), jnp.int32), pltpu.VMEM((tokens, width), BF16), dma((2,))],
         cost=400000000,
     )(ques_span, logit, vis_proj)
-    held = []
-    for index in range(len(chunks)):
-        parts = group(placed)
-        if index + 1 < len(chunks):
-            placed = place(waiting[index + 1])
-            if index + 2 < len(chunks):
-                waiting.append(down(index + 2))
-        held = finish(parts, index, held)
+    placed = [place(parts) for parts in waiting]
+    first = group(placed[0])
+    held = finish(first, 0, 0, [])
+    second = group(placed[1])
+    for turn in range(1, share):
+        held = finish(first, 0, turn, held)
+    for turn in range(share):
+        held = finish(second, 1, turn, held)
     return (held[0], ques_grad)
 
 

time: 79.7 us -> 73.7 us (0.925)
  waiting for transfers between devices: 23.9 us -> 15.2 us
  Pallas kernels: 25.8 us -> 26.8 us
  local copies, waits for them, and re-layouts: 4.37 us -> 5.25 us
  starting transfers between devices: 24.4 us -> 25.2 us
    ppermute x21, waiting for transfers between devices: 23.9 us -> 15.2 us  [swap(): return lax.ppermute(value, axis, [(i, i ^ step) for i in range(count)])]
    pallas_call x13 -> x14, Pallas kernels: 17.4 us -> 19.7 us  [apply(): *results, token = run_call(*args, *self.last)]
    pallas_call x1, Pallas kernels: 3.47 us -> 2.2 us  [preload(): caller(functools.partial(preload_kernel, steps, peers, share, chunks[0]),...]
    unnamed x20 -> x18, local copies, waits for them, and re-layouts: 4.37 us -> 5.25 us
  transfers between devices with their start and end apart: 21 -> 21, of which waited for: 8 -> 7; matrix products, arithmetic and copies ran while one was open for 0% -> 0% of each run, Pallas kernels for 23% -> 27%
where the time goes in v2:
time: 73.7 us; the launch traced here: 73.3 us
  Pallas kernels  26.8 us (36%)
  starting transfers between devices  25.2 us (34%)
  waiting for transfers between devices  15.2 us (21%)
  local copies, waits for them, and re-layouts  5.25 us (7%)
  between operations  0.89 us (1%)
    ppermute x21, starting transfers between devices, swap(): return lax.ppermute(value, axis, [(i, i ^ step) for i in range(count)])  25.2 us
    pallas_call x14, Pallas kernels, apply(): *results, token = run_call(*args, *self.last)  19.7 us
    ppermute x21, waiting for transfers between devices, swap(): return lax.ppermute(value, axis, [(i, i ^ step) for i in range(count)])  15.2 us
    unnamed x18, local copies, waits for them, and re-layouts  5.25 us
    pallas_call x1, Pallas kernels, preload(): caller(functools.partial(preload_kernel, steps, peers, share, chunks[0]),...  2.2 us
    pallas_call x1, Pallas kernels, body(): call(functools.partial(pick_kernel, pieces), shape((tokens, key_width), B...  2.15 us
    pallas_call x1, Pallas kernels, body(): call(load_kernel, [row, tall, tall, tall, tall, shape(w_value.shape, BF16...  1.86 us
  transfers between devices with their start and end apart: 21, of which 7 were waited for; matrix products, arithmetic and copies ran while one was open for 0% of the time, Pallas kernels for 27%

profile of v2, /device:TPU:0, one launch (start us, length us, event | category | flops | bytes accessed | tf_op | source)
XLA Modules:
  0.0 73.3 jit_solution(16653734318840513207)
XLA Ops:
  0.6 2.1 %shard_map.122.refs_0_ = bf16[128,512]{1,0:T(8,128)(2,1)} custom-call(s32[1,128]{1,0:T(1,128)} %pos_hbm.1, bf16[1,1024,512]{2,1,0:T(8,128)(2,1)} %rows_hbm.1), custom_call_target="tpu_custom_call" | custom-call | flops 262144 | bytes 1024 | tf_op jit(solution)/shard_map/pallas_call | solution.py:420
  2.8 4.0 %collective-permute-start.2 = (bf16[128,512]{1,0:T(8,128)(2,1)}, bf16[128,512]{1,0:T(8,128)(2,1)S(1)}, u32[]{:S(2)}, u32[]{:S(2)}) collective-permute-start(bf16[128,512]{1,0:T(8,128)(2,1)} %shard_map.122.refs_0_), channel_id=1, source_target_pairs={{0,24},{8,16},{16,8},{24,0},{1,25},{9,17},{17,9},{25,1},{2,26},{10... | collective-permute-start | bytes 393224 | tf_op jit(solution)/shard_map/ppermute | solution.py:76
  7.4 1.0 %copy-done.2 = bf16[1,128,2048]{2,1,0:T(8,128)(2,1)S(1)} copy-done((bf16[1,128,2048]{2,1,0:T(8,128)(2,1)S(1)}, bf16[1,128,2048]{2,1,0:T(8,128)(2,1)}, u32[]{:S(2)}) %copy-start.2) | copy-done | bytes 524312
  8.4 1.0 %copy-done.3 = bf16[1,128,2048]{2,1,0:T(8,128)(2,1)S(1)} copy-done((bf16[1,128,2048]{2,1,0:T(8,128)(2,1)S(1)}, bf16[1,128,2048]{2,1,0:T(8,128)(2,1)}, u32[]{:S(2)}) %copy-start.3) | copy-done | bytes 524312
  11.7 1.9 %shard_map.123 = (f32[8,128]{1,0:T(8,128)S(1)}, f32[2048,128]{1,0:T(8,128)S(1)}, f32[2048,128]{1,0:T(8,128)S(1)}, f32[2048,128]{1,0:T(8,128)S(1)}, f32[2048,128]...) custom-call(s32[1,2]{1,0:T(1,128)S(1)} %copy-done.8, bf16[1,32,2048]{2,1,0:T(8,128)(2,1)S(1)} %copy-done.5, ...), custom_call_target="tpu_custom_call" | custom-call | flops 262144 | bytes 1024 | tf_op jit(solution)/shard_map/pallas_call | solution.py:433
  15.4 2.9 %collective-permute-start.5 = (f32[8,128]{1,0:T(8,128)S(1)}, f32[8,128]{1,0:T(8,128)S(1)}, u32[]{:S(2)}, u32[]{:S(2)}) collective-permute-start(f32[8,128]{1,0:T(8,128)S(1)} %get-tuple-element.56.after_ref.refs_0_), channel_id=1, source_target_pairs={{0,24},{8,16},{16,8},{24,0},{1,25},{9,17},{17,9},{25,1},{2,26},{10... | collective-permute-start | bytes 12296 | tf_op jit(solution)/shard_map/ppermute | solution.py:76
  18.9 2.2 %shard_map.125.refs_9_.refs_0_ = bf16[1024,2048]{1,0:T(8,128)(2,1)S(1)} custom-call(bf16[8192,2048]{1,0:T(8,128)(2,1)} %refs_0_.5, f32[8,128]{1,0:T(8,128)S(1)} %get-tuple-element.56.after_ref.refs_0_), custom_call_target="tpu_custom_call" | custom-call | flops 262144 | bytes 1024 | tf_op jit(solution)/shard_map/pallas_call | solution.py:467
  22.8 2.2 %shard_map.127 = (bf16[1024,2048]{1,0:T(8,128)(2,1)S(1)}, f32[8,128]{1,0:T(8,128)S(1)}) custom-call(bf16[8192,2048]{1,0:T(8,128)(2,1)} %refs_0_.5, f32[8,128]{1,0:T(8,128)S(1)} %get-tuple-element.61.refs_1_, f32[8,128]{1,0:T(8,128)S(1)} %get-tuple-element.62.refs_2_), custom_call_target="tpu_custom_call" | custom-call | flops 262144 | bytes 1024 | tf_op jit(solution)/shard_map/pallas_call | solution.py:64
  25.0 2.4 %shard_map.128 = (bf16[512,256]{1,0:T(8,128)(2,1)S(1)}, bf16[512,256]{1,0:T(8,128)(2,1)S(1)}, bf16[512,256]{1,0:T(8,128)(2,1)S(1)}, bf16[512,256]{1,0:T(8,128)(2,1)S(1)}, f32[8,128]{1,0:T(8,128)S(1)}) custom-call(bf16[1024,2048]{1,0:T(8,128)(2,1)S(1)} %shard_map.125.refs_9_.refs_0_, bf16[1024,2048]{1,0:T(8,128)(2,1)S(1)} %get-tuple-element.63.refs_1_, ...), custom_call_target="tpu_custom_call" | custom-call | flops 2147483648 | bytes 8388608 | tf_op jit(solution)/shard_map/pallas_call | solution.py:64
  27.4 1.7 %collective-permute-start.10 = (bf16[512,256]{1,0:T(8,128)(2,1)S(1)}, bf16[512,256]{1,0:T(8,128)(2,1)S(1)}, u32[]{:S(2)}, u32[]{:S(2)}) collective-permute-start(bf16[512,256]{1,0:T(8,128)(2,1)S(1)} %get-tuple-element.71), channel_id=1, source_target_pairs={{0,24},{8,16},{16,8},{24,0},{1,25},{9,17},{17,9},{25,1},{2,26},{10... | collective-permute-start | bytes 786440 | tf_op jit(solution)/shard_map/ppermute | solution.py:76
  29.6 1.4 %collective-permute-start.12 = (bf16[512,256]{1,0:T(8,128)(2,1)S(1)}, bf16[512,256]{1,0:T(8,128)(2,1)S(1)}, u32[]{:S(2)}, u32[]{:S(2)}) collective-permute-start(bf16[512,256]{1,0:T(8,128)(2,1)S(1)} %get-tuple-element.73), channel_id=1, source_target_pairs={{0,8},{8,0},{16,24},{24,16},{1,9},{9,1},{17,25},{25,17},{2,10},{10... | collective-permute-start | bytes 786440 | tf_op jit(solution)/shard_map/ppermute | solution.py:76
  31.0 7.0 %shard_map.129 = (bf16[512,256]{1,0:T(8,128)(2,1)S(1)}, bf16[512,256]{1,0:T(8,128)(2,1)S(1)}, bf16[512,256]{1,0:T(8,128)(2,1)S(1)}, bf16[512,256]{1,0:T(8,128)(2,1)S(1)}, f32[8,128]{1,0:T(8,128)S(1)}) custom-call(bf16[8192,2048]{1,0:T(8,128)(2,1)} %refs_0_.5, bf16[2064,128]{1,0:T(8,128)(2,1)S(1)} %get-tuple-element.60.refs_2_.refs_1_.refs_0_, ...), custom_call_target="tpu_custom_call" | custom-call | flops 2147483648 | bytes 8388608 | tf_op jit(solution)/shard_map/pallas_call | solution.py:64
  37.9 1.7 %collective-permute-start.7 = (bf16[512,256]{1,0:T(8,128)(2,1)S(1)}, bf16[512,256]{1,0:T(8,128)(2,1)S(1)}, u32[]{:S(2)}, u32[]{:S(2)}) collective-permute-start(bf16[512,256]{1,0:T(8,128)(2,1)S(1)} %get-tuple-element.67), channel_id=1, source_target_pairs={{0,24},{8,16},{16,8},{24,0},{1,25},{9,17},{17,9},{25,1},{2,26},{10... | collective-permute-start | bytes 786440 | tf_op jit(solution)/shard_map/ppermute | solution.py:76
  41.1 1.4 %collective-permute-start.9 = (bf16[512,256]{1,0:T(8,128)(2,1)S(1)}, bf16[512,256]{1,0:T(8,128)(2,1)S(1)}, u32[]{:S(2)}, u32[]{:S(2)}) collective-permute-start(bf16[512,256]{1,0:T(8,128)(2,1)S(1)} %get-tuple-element.69), channel_id=1, source_target_pairs={{0,8},{8,0},{16,24},{24,16},{1,9},{9,1},{17,25},{25,17},{2,10},{10... | collective-permute-start | bytes 786440 | tf_op jit(solution)/shard_map/ppermute | solution.py:76
  42.5 1.5 %shard_map.131 = (bf16[1,32,2048]{2,1,0:T(8,128)(2,1)}, f32[8,128]{1,0:T(8,128)S(1)}) custom-call(s32[1,2]{1,0:T(1,128)S(1)} %copy-done.8, f32[8,128]{1,0:T(8,128)S(1)} %get-tuple-element.61.refs_1_, bf16[1,128,2048]{2,1,0:T(8,128)(2,1)S(1)} %copy-done.4, f32[8,128]{1,0:T(8,128)S(1)} %get-tuple-element.75.refs_3_), custom_call_target="tpu_custom_call" | custom-call | flops 102400000000 | bytes 400000000 | tf_op jit(solution)/shard_map/pallas_call | solution.py:64
  44.5 3.7 %collective-permute-start.16 = (bf16[128,512]{1,0:T(8,128)(2,1)S(1)}, bf16[128,512]{1,0:T(8,128)(2,1)S(1)}, u32[]{:S(2)}, u32[]{:S(2)}) collective-permute-start(bf16[128,512]{1,0:T(8,128)(2,1)S(1)} %get-tuple-element.83), channel_id=1, source_target_pairs={{0,6},{1,7},{2,4},{3,5},{4,2},{5,3},{6,0},{7,1},{8,14},{9,15},{10,... | collective-permute-start | bytes 393224 | tf_op jit(solution)/shard_map/ppermute | solution.py:76
  48.8 1.6 %collective-permute-start.18 = (bf16[128,512]{1,0:T(8,128)(2,1)S(1)}, bf16[128,512]{1,0:T(8,128)(2,1)S(1)}, u32[]{:S(2)}, u32[]{:S(2)}) collective-permute-start(bf16[128,512]{1,0:T(8,128)(2,1)S(1)} %get-tuple-element.85), channel_id=1, source_target_pairs={{0,2},{1,3},{2,0},{3,1},{4,6},{5,7},{6,4},{7,5},{8,10},{9,11},{10,... | collective-permute-start | bytes 393224 | tf_op jit(solution)/shard_map/ppermute | solution.py:76
  50.4 3.5 %collective-permute-done.8.refs_4_ = bf16[512,256]{1,0:T(8,128)(2,1)S(1)} collective-permute-done((bf16[512,256]{1,0:T(8,128)(2,1)S(1)}, bf16[512,256]{1,0:T(8,128)(2,1)S(1)}, u32[]{:S(2)}, u32[]{:S(2)}) %collective-permute-start.8) | collective-permute-done | bytes 262176 | tf_op jit(solution)/shard_map/ppermute | solution.py:76
  54.5 3.7 %collective-permute-start.13 = (bf16[128,512]{1,0:T(8,128)(2,1)S(1)}, bf16[128,512]{1,0:T(8,128)(2,1)S(1)}, u32[]{:S(2)}, u32[]{:S(2)}) collective-permute-start(bf16[128,512]{1,0:T(8,128)(2,1)S(1)} %get-tuple-element.79), channel_id=1, source_target_pairs={{0,6},{1,7},{2,4},{3,5},{4,2},{5,3},{6,0},{7,1},{8,14},{9,15},{10,... | collective-permute-start | bytes 393224 | tf_op jit(solution)/shard_map/ppermute | solution.py:76
  60.1 2.7 %collective-permute-done.13.refs_1_ = bf16[128,512]{1,0:T(8,128)(2,1)S(1)} collective-permute-done((bf16[128,512]{1,0:T(8,128)(2,1)S(1)}, bf16[128,512]{1,0:T(8,128)(2,1)S(1)}, u32[]{:S(2)}, u32[]{:S(2)}) %collective-permute-start.13) | collective-permute-done | bytes 131104 | tf_op jit(solution)/shard_map/ppermute | solution.py:76
  62.8 6.8 %collective-permute-done.14.refs_2_ = bf16[128,512]{1,0:T(8,128)(2,1)S(1)} collective-permute-done((bf16[128,512]{1,0:T(8,128)(2,1)S(1)}, bf16[128,512]{1,0:T(8,128)(2,1)S(1)}, u32[]{:S(2)}, u32[]{:S(2)}) %collective-permute-start.14) | collective-permute-done | bytes 131104 | tf_op jit(solution)/shard_map/ppermute | solution.py:76
  69.8 1.0 %shard_map.137 = (bf16[1,2048,256]{2,1,0:T(8,128)(2,1)}, f32[8,128]{1,0:T(8,128)S(1)}) custom-call(bf16[256,512]{1,0:T(8,128)(2,1)S(1)} %collective-permute-done.20.refs_0_, f32[2048,256]{1,0:T(8,128)S(1)} %get-tuple-element.88.refs_1_, bf16[1,2048,256]{2,1,0:T(8,128)(2,1)} %get-tuple-element.94.refs_2_, ...), custom_call_target="tpu_custom_call", output_to_operand_aliasing={{0}: (2, {})} | custom-call | flops 262144 | bytes 1024 | tf_op jit(solution)/shard_map/pallas_call | solution.py:64
  70.7 1.0 %shard_map.138 = (bf16[1,2048,256]{2,1,0:T(8,128)(2,1)}, f32[8,128]{1,0:T(8,128)S(1)}) custom-call(bf16[256,512]{1,0:T(8,128)(2,1)S(1)} %get-tuple-element.92.refs_0_, f32[2048,256]{1,0:T(8,128)S(1)} %get-tuple-element.88.refs_1_, bf16[1,2048,256]{2,1,0:T(8,128)(2,1)} %get-tuple-element.96.refs_2_, ...), custom_call_target="tpu_custom_call", output_to_operand_aliasing={{0}: (2, {})} | custom-call | flops 262144 | bytes 1024 | tf_op jit(solution)/shard_map/pallas_call | solution.py:64
  71.8 1.6 %shard_map.139 = (bf16[1,2048,256]{2,1,0:T(8,128)(2,1)}, f32[8,128]{1,0:T(8,128)}) custom-call(bf16[256,512]{1,0:T(8,128)(2,1)S(1)} %collective-permute-done.19.refs_0_, f32[2048,256]{1,0:T(8,128)S(1)} %get-tuple-element.88.refs_1_, bf16[1,2048,256]{2,1,0:T(8,128)(2,1)} %get-tuple-element.98.refs_2_, ...), custom_call_target="tpu_custom_call", output_to_operand_aliasing={{0}: (2, {})} | custom-call | flops 262144 | bytes 1024 | tf_op jit(solution)/shard_map/pallas_call | solution.py:64
  (54 shorter events, 12.6 us)
Async XLA Ops:
  2.8 10.8 %collective-permute-start.2 = (bf16[128,512]{1,0:T(8,128)(2,1)}, bf16[128,512]{1,0:T(8,128)(2,1)S(1)}, u32[]{:S(2)}, u32[]{:S(2)}) collective-permute-start(bf16[128,512]{1,0:T(8,128)(2,1)} %shard_map.122.refs_0_), channel_id=1, source_target_pairs={{0,24},{8,16},{16,8},{24,0},{1,25},{9,17},{17,9},{25,1},{2,26},{10... | collective-permute-start | bytes 393224 | tf_op jit(solution)/shard_map/ppermute | solution.py:76
  6.7 6.9 %collective-permute-start.1 = (bf16[128,512]{1,0:T(8,128)(2,1)}, bf16[128,512]{1,0:T(8,128)(2,1)S(1)}, u32[]{:S(2)}, u32[]{:S(2)}) collective-permute-start(bf16[128,512]{1,0:T(8,128)(2,1)} %shard_map.122.refs_0_), channel_id=1, source_target_pairs={{0,16},{8,24},{16,0},{24,8},{1,17},{9,25},{17,1},{25,9},{2,18},{10... | collective-permute-start | bytes 393224 | tf_op jit(solution)/shard_map/ppermute | solution.py:76
  7.2 6.4 %collective-permute-start = (bf16[128,512]{1,0:T(8,128)(2,1)}, bf16[128,512]{1,0:T(8,128)(2,1)S(1)}, u32[]{:S(2)}, u32[]{:S(2)}) collective-permute-start(bf16[128,512]{1,0:T(8,128)(2,1)} %shard_map.122.refs_0_), channel_id=1, source_target_pairs={{0,8},{8,0},{16,24},{24,16},{1,9},{9,1},{17,25},{25,17},{2,10},{10... | collective-permute-start | bytes 393224 | tf_op jit(solution)/shard_map/ppermute | solution.py:76
  15.4 7.0 %copy-start.7 = (s32[1,128,1]{1,2,0:T(1,128)S(1)}, s32[1,128,1]{1,2,0:T(1,128)}, u32[]{:S(2)}) copy-start(s32[1,128,1]{1,2,0:T(1,128)} %param.15) | copy-start | bytes 1540
  15.4 5.8 %collective-permute-start.5 = (f32[8,128]{1,0:T(8,128)S(1)}, f32[8,128]{1,0:T(8,128)S(1)}, u32[]{:S(2)}, u32[]{:S(2)}) collective-permute-start(f32[8,128]{1,0:T(8,128)S(1)} %get-tuple-element.56.after_ref.refs_0_), channel_id=1, source_target_pairs={{0,24},{8,16},{16,8},{24,0},{1,25},{9,17},{17,9},{25,1},{2,26},{10... | collective-permute-start | bytes 12296 | tf_op jit(solution)/shard_map/ppermute | solution.py:76
  18.3 3.6 %collective-permute-start.4 = (f32[8,128]{1,0:T(8,128)S(1)}, f32[8,128]{1,0:T(8,128)S(1)}, u32[]{:S(2)}, u32[]{:S(2)}) collective-permute-start(f32[8,128]{1,0:T(8,128)S(1)} %get-tuple-element.56.after_ref.refs_0_), channel_id=1, source_target_pairs={{0,16},{8,24},{16,0},{24,8},{1,17},{9,25},{17,1},{25,9},{2,18},{10... | collective-permute-start | bytes 12296 | tf_op jit(solution)/shard_map/ppermute | solution.py:76
  18.8 3.6 %collective-permute-start.3 = (f32[8,128]{1,0:T(8,128)S(1)}, f32[8,128]{1,0:T(8,128)S(1)}, u32[]{:S(2)}, u32[]{:S(2)}) collective-permute-start(f32[8,128]{1,0:T(8,128)S(1)} %get-tuple-element.56.after_ref.refs_0_), channel_id=1, source_target_pairs={{0,8},{8,0},{16,24},{24,16},{1,9},{9,1},{17,25},{25,17},{2,10},{10... | collective-permute-start | bytes 12296 | tf_op jit(solution)/shard_map/ppermute | solution.py:76
  22.7 2.3 %collective-permute-start.6 = (bf16[2064,128]{1,0:T(8,128)(2,1)S(1)}, bf16[2064,128]{1,0:T(8,128)(2,1)S(1)}, u32[]{:S(2)}, u32[]{:S(2)}) collective-permute-start(bf16[2064,128]{1,0:T(8,128)(2,1)S(1)} %get-tuple-element.60.refs_2_.refs_1_.refs_0_), channel_id=1, source_target_pairs={{0,1},{1,0},{2,3},{3,2},{4,5},{5,4},{6,7},{7,6},{8,9},{9,8},{10,11... | collective-permute-start | bytes 1585160 | tf_op jit(solution)/shard_map/ppermute | solution.py:76
  27.4 13.7 %collective-permute-start.10 = (bf16[512,256]{1,0:T(8,128)(2,1)S(1)}, bf16[512,256]{1,0:T(8,128)(2,1)S(1)}, u32[]{:S(2)}, u32[]{:S(2)}) collective-permute-start(bf16[512,256]{1,0:T(8,128)(2,1)S(1)} %get-tuple-element.71), channel_id=1, source_target_pairs={{0,24},{8,16},{16,8},{24,0},{1,25},{9,17},{17,9},{25,1},{2,26},{10... | collective-permute-start | bytes 786440 | tf_op jit(solution)/shard_map/ppermute | solution.py:76
  29.1 14.9 %collective-permute-start.11 = (bf16[512,256]{1,0:T(8,128)(2,1)S(1)}, bf16[512,256]{1,0:T(8,128)(2,1)S(1)}, u32[]{:S(2)}, u32[]{:S(2)}) collective-permute-start(bf16[512,256]{1,0:T(8,128)(2,1)S(1)} %get-tuple-element.72), channel_id=1, source_target_pairs={{0,16},{8,24},{16,0},{24,8},{1,17},{9,25},{17,1},{25,9},{2,18},{10... | collective-permute-start | bytes 786440 | tf_op jit(solution)/shard_map/ppermute | solution.py:76
  29.6 14.4 %collective-permute-start.12 = (bf16[512,256]{1,0:T(8,128)(2,1)S(1)}, bf16[512,256]{1,0:T(8,128)(2,1)S(1)}, u32[]{:S(2)}, u32[]{:S(2)}) collective-permute-start(bf16[512,256]{1,0:T(8,128)(2,1)S(1)} %get-tuple-element.73), channel_id=1, source_target_pairs={{0,8},{8,0},{16,24},{24,16},{1,9},{9,1},{17,25},{25,17},{2,10},{10... | collective-permute-start | bytes 786440 | tf_op jit(solution)/shard_map/ppermute | solution.py:76
  31.0 9.2 %copy-start = (bf16[1,2048,256]{2,1,0:T(8,128)(2,1)S(1)}, bf16[1,2048,256]{2,1,0:T(8,128)(2,1)}, u32[]{:S(2)}) copy-start(bf16[1,2048,256]{2,1,0:T(8,128)(2,1)} %refs_0_.6) | copy-start | bytes 3145732
  31.0 11.6 %copy-start.4 = (bf16[1,128,2048]{2,1,0:T(8,128)(2,1)S(1)}, bf16[1,128,2048]{2,1,0:T(8,128)(2,1)}, u32[]{:S(2)}) copy-start(bf16[1,128,2048]{2,1,0:T(8,128)(2,1)} %refs_2_.1) | copy-start | bytes 1572868
  37.9 10.9 %collective-permute-start.7 = (bf16[512,256]{1,0:T(8,128)(2,1)S(1)}, bf16[512,256]{1,0:T(8,128)(2,1)S(1)}, u32[]{:S(2)}, u32[]{:S(2)}) collective-permute-start(bf16[512,256]{1,0:T(8,128)(2,1)S(1)} %get-tuple-element.67), channel_id=1, source_target_pairs={{0,24},{8,16},{16,8},{24,0},{1,25},{9,17},{17,9},{25,1},{2,26},{10... | collective-permute-start | bytes 786440 | tf_op jit(solution)/shard_map/ppermute | solution.py:76
  39.6 14.3 %collective-permute-start.8 = (bf16[512,256]{1,0:T(8,128)(2,1)S(1)}, bf16[512,256]{1,0:T(8,128)(2,1)S(1)}, u32[]{:S(2)}, u32[]{:S(2)}) collective-permute-start(bf16[512,256]{1,0:T(8,128)(2,1)S(1)} %get-tuple-element.68), channel_id=1, source_target_pairs={{0,16},{8,24},{16,0},{24,8},{1,17},{9,25},{17,1},{25,9},{2,18},{10... | collective-permute-start | bytes 786440 | tf_op jit(solution)/shard_map/ppermute | solution.py:76
  41.1 13.0 %collective-permute-start.9 = (bf16[512,256]{1,0:T(8,128)(2,1)S(1)}, bf16[512,256]{1,0:T(8,128)(2,1)S(1)}, u32[]{:S(2)}, u32[]{:S(2)}) collective-permute-start(bf16[512,256]{1,0:T(8,128)(2,1)S(1)} %get-tuple-element.69), channel_id=1, source_target_pairs={{0,8},{8,0},{16,24},{24,16},{1,9},{9,1},{17,25},{25,17},{2,10},{10... | collective-permute-start | bytes 786440 | tf_op jit(solution)/shard_map/ppermute | solution.py:76
  44.5 13.7 %collective-permute-start.16 = (bf16[128,512]{1,0:T(8,128)(2,1)S(1)}, bf16[128,512]{1,0:T(8,128)(2,1)S(1)}, u32[]{:S(2)}, u32[]{:S(2)}) collective-permute-start(bf16[128,512]{1,0:T(8,128)(2,1)S(1)} %get-tuple-element.83), channel_id=1, source_target_pairs={{0,6},{1,7},{2,4},{3,5},{4,2},{5,3},{6,0},{7,1},{8,14},{9,15},{10,... | collective-permute-start | bytes 393224 | tf_op jit(solution)/shard_map/ppermute | solution.py:76
  48.1 10.8 %collective-permute-start.17 = (bf16[128,512]{1,0:T(8,128)(2,1)S(1)}, bf16[128,512]{1,0:T(8,128)(2,1)S(1)}, u32[]{:S(2)}, u32[]{:S(2)}) collective-permute-start(bf16[128,512]{1,0:T(8,128)(2,1)S(1)} %get-tuple-element.84), channel_id=1, source_target_pairs={{0,4},{1,5},{2,6},{3,7},{4,0},{5,1},{6,2},{7,3},{8,12},{9,13},{10,... | collective-permute-start | bytes 393224 | tf_op jit(solution)/shard_map/ppermute | solution.py:76
  48.8 10.2 %collective-permute-start.18 = (bf16[128,512]{1,0:T(8,128)(2,1)S(1)}, bf16[128,512]{1,0:T(8,128)(2,1)S(1)}, u32[]{:S(2)}, u32[]{:S(2)}) collective-permute-start(bf16[128,512]{1,0:T(8,128)(2,1)S(1)} %get-tuple-element.85), channel_id=1, source_target_pairs={{0,2},{1,3},{2,0},{3,1},{4,6},{5,7},{6,4},{7,5},{8,10},{9,11},{10,... | collective-permute-start | bytes 393224 | tf_op jit(solution)/shard_map/ppermute | solution.py:76
  54.5 8.3 %collective-permute-start.13 = (bf16[128,512]{1,0:T(8,128)(2,1)S(1)}, bf16[128,512]{1,0:T(8,128)(2,1)S(1)}, u32[]{:S(2)}, u32[]{:S(2)}) collective-permute-start(bf16[128,512]{1,0:T(8,128)(2,1)S(1)} %get-tuple-element.79), channel_id=1, source_target_pairs={{0,6},{1,7},{2,4},{3,5},{4,2},{5,3},{6,0},{7,1},{8,14},{9,15},{10,... | collective-permute-start | bytes 393224 | tf_op jit(solution)/shard_map/ppermute | solution.py:76
  58.2 11.4 %collective-permute-start.14 = (bf16[128,512]{1,0:T(8,128)(2,1)S(1)}, bf16[128,512]{1,0:T(8,128)(2,1)S(1)}, u32[]{:S(2)}, u32[]{:S(2)}) collective-permute-start(bf16[128,512]{1,0:T(8,128)(2,1)S(1)} %get-tuple-element.80), channel_id=1, source_target_pairs={{0,4},{1,5},{2,6},{3,7},{4,0},{5,1},{6,2},{7,3},{8,12},{9,13},{10,... | collective-permute-start | bytes 393224 | tf_op jit(solution)/shard_map/ppermute | solution.py:76
  58.2 11.4 %collective-permute-start.15 = (bf16[128,512]{1,0:T(8,128)(2,1)S(1)}, bf16[128,512]{1,0:T(8,128)(2,1)S(1)}, u32[]{:S(2)}, u32[]{:S(2)}) collective-permute-start(bf16[128,512]{1,0:T(8,128)(2,1)S(1)} %get-tuple-element.81), channel_id=1, source_target_pairs={{0,2},{1,3},{2,0},{3,1},{4,6},{5,7},{6,4},{7,5},{8,10},{9,11},{10,... | collective-permute-start | bytes 393224 | tf_op jit(solution)/shard_map/ppermute | solution.py:76
  59.0 10.7 %collective-permute-start.20 = (bf16[256,512]{1,0:T(8,128)(2,1)S(1)}, bf16[256,512]{1,0:T(8,128)(2,1)S(1)}, u32[]{:S(2)}, u32[]{:S(2)}) collective-permute-start(bf16[256,512]{1,0:T(8,128)(2,1)S(1)} %get-tuple-element.93), channel_id=1, source_target_pairs={{0,1},{1,0},{2,3},{3,2},{4,5},{5,4},{6,7},{7,6},{8,9},{9,8},{10,11... | collective-permute-start | bytes 786440 | tf_op jit(solution)/shard_map/ppermute | solution.py:76
  69.7 2.1 %collective-permute-start.19 = (bf16[256,512]{1,0:T(8,128)(2,1)S(1)}, bf16[256,512]{1,0:T(8,128)(2,1)S(1)}, u32[]{:S(2)}, u32[]{:S(2)}) collective-permute-start(bf16[256,512]{1,0:T(8,128)(2,1)S(1)} %get-tuple-element.91), channel_id=1, source_target_pairs={{0,1},{1,0},{2,3},{3,2},{4,5},{5,4},{6,7},{7,6},{8,9},{9,8},{10,11... | collective-permute-start | bytes 786440 | tf_op jit(solution)/shard_map/ppermute | solution.py:76
  (6 other events, 5.2 us)

commit v3 on v2

--- a/solution.py
+++ b/solution.py
@@ -12,7 +12,7 @@
 F32 = jnp.float32
 BF16 = jnp.bfloat16
 LANES = 128
-AHEAD = 6
+AHEAD = 4
 MIB = 1024 * 1024
 GRANT, LOAD_GRANT, PICK_GRANT = 40, 46, 54
 HBM = pl.BlockSpec(memory_space=pltpu.HBM)
@@ -193,28 +193,27 @@
     sums_ref[3:4, :] = jnp.sum(total, axis=0, keepdims=True)
 
 
-def weight_copies(weight_hbm, weights, sems, steps, peers, share, base, rows):
+def weight_copy(weight_hbm, weights, sems, peers, share, base, rows, index, skipped=0):
     quarter = weight_hbm.shape[0] // peers
     block = min(rows, 256)
-    part = lax.rem(lax.axis_index("frame"), share) * (quarter // share)
-    copies = []
-    for peer, step in enumerate(steps):
-        first = (lax.axis_index("seq") ^ step) * quarter + part + base
-        for at in range(0, rows, block):
-            index = len(copies)
-            copies.append(
-                pltpu.make_async_copy(
-                    weight_hbm.at[pl.ds(pl.multiple_of(first + at, block), block)],
-                    weights.at[pl.ds(peer * rows + at, block)],
-                    sems.at[index],
-                )
-            )
-    return copies
-
-
-def preload_kernel(steps, peers, share, rows, weight_hbm, after_ref, weights_ref, sems):
+    inner = rows // block
+    step = lax.rem(peers - index // inner, peers)
+    first = (lax.axis_index("seq") ^ step) * quarter + base + lax.rem(index, inner) * block
+    first += lax.rem(lax.axis_index("frame"), share) * (quarter // share)
+    place = index - skipped
+    return pltpu.make_async_copy(
+        weight_hbm.at[pl.ds(pl.multiple_of(first, block), block)],
+        weights.at[pl.ds(pl.multiple_of(place * block, block), block)],
+        sems.at[place],
+    )
+
+
+def preload_kernel(skipped, count, peers, share, rows, weight_hbm, after_ref, weights_ref, sems):
     del after_ref
-    copies = weight_copies(weight_hbm, weights_ref, sems, steps, peers, share, 0, rows)
+    copies = [
+        weight_copy(weight_hbm, weights_ref, sems, peers, share, 0, rows, index, skipped)
+        for index in range(skipped, skipped + count)
+    ]
     for copy in copies:
         copy.start()
     for copy in copies:
@@ -253,35 +252,47 @@
     scratch = list(refs[len(weight_refs) + share :])
     out_refs = [scratch.pop(0) for _ in range(peers)]
     joined = scratch.pop(0)
-    copies = []
-    if held:
-        weights = weight_refs
-    else:
-        weights, sems = scratch[:1], scratch[1]
-        copies = weight_copies(
-            weight_refs[0], weights[0], sems, far_first(peers), peers, share, base, rows
-        )
-    for copy in copies[:AHEAD]:
-        copy.start()
+    block = min(rows, 256)
+    inner = rows // block
+    total = peers * inner
+
+    def copy(index):
+        return weight_copy(weight_refs[0], *scratch, peers, share, base, rows, index)
+
+    if not held:
+        for index in range(min(AHEAD, total)):
+            copy(index).start()
     width, tokens = joined.shape[0], gradt_refs[0].shape[1]
     for index, ref in enumerate(gradt_refs):
         joined[:, index * tokens : (index + 1) * tokens] = ref[:width, :]
-    block = min(rows, 256)
-    inner = rows // block
-    each = peers * inner // len(weights)
-    for index in range(peers * inner):
-        peer, part = index // inner, index % inner
-        if copies:
-            copies[index].wait()
-        if index + AHEAD < len(copies):
-            copies[index + AHEAD].start()
-        place = index % each
-        value = jnp.dot(
-            weights[index // each][place * block : (place + 1) * block, :],
-            joined[...],
-            preferred_element_type=F32,
-        )
-        out_refs[peer][part * block : (part + 1) * block, :] = value.astype(BF16)
+    each = total // len(weight_refs)
+    for peer, ref in enumerate(out_refs):
+        if held:
+            weights = weight_refs[peer * inner // each]
+            for part in range(inner):
+                at = (peer * inner + part) % each * block
+                value = jnp.dot(
+                    weights[at : at + block, :], joined[...], preferred_element_type=F32
+                )
+                ref[part * block : (part + 1) * block, :] = value.astype(BF16)
+            continue
+
+        def step(part, carry, peer=peer, ref=ref):
+            index = peer * inner + part
+            copy(index).wait()
+
+            @pl.when(index + AHEAD < total)
+            def _():
+                copy(index + AHEAD).start()
+
+            at = pl.multiple_of(index * block, block)
+            value = jnp.dot(
+                scratch[0][pl.ds(at, block), :], joined[...], preferred_element_type=F32
+            )
+            ref[pl.ds(pl.multiple_of(part * block, block), block), :] = value.astype(BF16)
+            return carry
+
+        lax.fori_loop(0, inner, step, 0)
 
 
 def ques_kernel(span_hbm, logit_ref, proj_hbm, out_ref, span, proj, sems):
@@ -463,23 +474,23 @@
     def sems(rows, count=peers):
         return dma((count * (rows // min(rows, 256)),))
 
-    def preload(caller, steps, after):
+    def preload(caller, half, after):
+        count = peers // 2 * (chunks[0] // min(chunks[0], 256))
         (weights,) = caller(
-            functools.partial(preload_kernel, steps, peers, share, chunks[0]),
-            [shape((len(steps) * chunks[0], width), BF16)],
+            functools.partial(preload_kernel, half * count, count, peers, share, chunks[0]),
+            [shape((peers // 2 * chunks[0], width), BF16)],
             [HBM, VMEM],
-            [sems(chunks[0], len(steps))],
+            [sems(chunks[0], peers // 2)],
         )(w_down, after)
         return weights
 
-    steps = far_first(peers)
-    preloaded = [preload(call, steps[: peers // 2], sums)]
+    preloaded = [preload(call, 0, sums)]
     gradt, logit = chain.call(
         functools.partial(gate_kernel, features, peers),
         [shape((width + 16, tokens), BF16), row],
         [VMEM] * (peers + 5) + [ANY],
     )(*sums_all, projt, residt, scaledt, meant, owner, preloaded[0])
-    preloaded.append(preload(chain.call, steps[peers // 2 :], logit))
+    preloaded.append(preload(chain.call, 1, logit))
     gradts = [gradt] + [swap(gradt, "frame", owners_count, k) for k in range(1, share)]
 
     def down(index):

time: 73.7 us -> 73.7 us (level)
  Pallas kernels: 26.8 us -> 24.8 us
  waiting for transfers between devices: 15.2 us -> 17.1 us
    pallas_call x14, Pallas kernels: 19.7 us -> 17.8 us  [apply(): *results, token = run_call(*args, *self.last)]
    ppermute x21, waiting for transfers between devices: 15.2 us -> 17.1 us  [swap(): return lax.ppermute(value, axis, [(i, i ^ step) for i in range(count)])]
  transfers between devices with their start and end apart: 21 -> 21, of which waited for: 7 -> 8; matrix products, arithmetic and copies ran while one was open for 0% -> 0% of each run, Pallas kernels for 27% -> 24%
where the time goes in v3:
time: 73.7 us; the launch traced here: 73.3 us
  starting transfers between devices  25.2 us (34%)
  Pallas kernels  24.8 us (34%)
  waiting for transfers between devices  17.1 us (23%)
  local copies, waits for them, and re-layouts  5.25 us (7%)
  between operations  0.88 us (1%)
    ppermute x21, starting transfers between devices, swap(): return lax.ppermute(value, axis, [(i, i ^ step) for i in range(count)])  25.2 us
    pallas_call x14, Pallas kernels, apply(): *results, token = run_call(*args, *self.last)  17.8 us
    ppermute x21, waiting for transfers between devices, swap(): return lax.ppermute(value, axis, [(i, i ^ step) for i in range(count)])  17.1 us
    unnamed x18, local copies, waits for them, and re-layouts  5.25 us
    pallas_call x1, Pallas kernels, preload(): caller(functools.partial(preload_kernel, half * count, count, peers, shar...  2.2 us
    pallas_call x1, Pallas kernels, body(): call(functools.partial(pick_kernel, pieces), shape((tokens, key_width), B...  2.15 us
    pallas_call x1, Pallas kernels, body(): call(load_kernel, [row, tall, tall, tall, tall, shape(w_value.shape, BF16...  1.86 us
  transfers between devices with their start and end apart: 21, of which 8 were waited for; matrix products, arithmetic and copies ran while one was open for 0% of the time, Pallas kernels for 24%

profile of v3, /device:TPU:0, one launch (start us, length us, event | category | flops | bytes accessed | tf_op | source)
XLA Modules:
  0.0 73.3 jit_solution(13338078811591416138)
XLA Ops:
  0.6 2.1 %shard_map.122.refs_0_ = bf16[128,512]{1,0:T(8,128)(2,1)} custom-call(s32[1,128]{1,0:T(1,128)} %pos_hbm.1, bf16[1,1024,512]{2,1,0:T(8,128)(2,1)} %rows_hbm.1), custom_call_target="tpu_custom_call" | custom-call | flops 262144 | bytes 1024 | tf_op jit(solution)/shard_map/pallas_call | solution.py:431
  2.8 4.0 %collective-permute-start.2 = (bf16[128,512]{1,0:T(8,128)(2,1)}, bf16[128,512]{1,0:T(8,128)(2,1)S(1)}, u32[]{:S(2)}, u32[]{:S(2)}) collective-permute-start(bf16[128,512]{1,0:T(8,128)(2,1)} %shard_map.122.refs_0_), channel_id=1, source_target_pairs={{0,24},{8,16},{16,8},{24,0},{1,25},{9,17},{17,9},{25,1},{2,26},{10... | collective-permute-start | bytes 393224 | tf_op jit(solution)/shard_map/ppermute | solution.py:76
  7.4 1.0 %copy-done.2 = bf16[1,128,2048]{2,1,0:T(8,128)(2,1)S(1)} copy-done((bf16[1,128,2048]{2,1,0:T(8,128)(2,1)S(1)}, bf16[1,128,2048]{2,1,0:T(8,128)(2,1)}, u32[]{:S(2)}) %copy-start.2) | copy-done | bytes 524312
  8.4 1.0 %copy-done.3 = bf16[1,128,2048]{2,1,0:T(8,128)(2,1)S(1)} copy-done((bf16[1,128,2048]{2,1,0:T(8,128)(2,1)S(1)}, bf16[1,128,2048]{2,1,0:T(8,128)(2,1)}, u32[]{:S(2)}) %copy-start.3) | copy-done | bytes 524312
  11.7 1.9 %shard_map.123 = (f32[8,128]{1,0:T(8,128)S(1)}, f32[2048,128]{1,0:T(8,128)S(1)}, f32[2048,128]{1,0:T(8,128)S(1)}, f32[2048,128]{1,0:T(8,128)S(1)}, f32[2048,128]...) custom-call(s32[1,2]{1,0:T(1,128)S(1)} %copy-done.8, bf16[1,32,2048]{2,1,0:T(8,128)(2,1)S(1)} %copy-done.5, ...), custom_call_target="tpu_custom_call" | custom-call | flops 262144 | bytes 1024 | tf_op jit(solution)/shard_map/pallas_call | solution.py:444
  15.4 2.9 %collective-permute-start.5 = (f32[8,128]{1,0:T(8,128)S(1)}, f32[8,128]{1,0:T(8,128)S(1)}, u32[]{:S(2)}, u32[]{:S(2)}) collective-permute-start(f32[8,128]{1,0:T(8,128)S(1)} %get-tuple-element.56.after_ref.refs_0_), channel_id=1, source_target_pairs={{0,24},{8,16},{16,8},{24,0},{1,25},{9,17},{17,9},{25,1},{2,26},{10... | collective-permute-start | bytes 12296 | tf_op jit(solution)/shard_map/ppermute | solution.py:76
  18.9 2.2 %shard_map.125.refs_9_.refs_0_ = bf16[1024,2048]{1,0:T(8,128)(2,1)S(1)} custom-call(bf16[8192,2048]{1,0:T(8,128)(2,1)} %refs_0_.5, f32[8,128]{1,0:T(8,128)S(1)} %get-tuple-element.56.after_ref.refs_0_), custom_call_target="tpu_custom_call" | custom-call | flops 262144 | bytes 1024 | tf_op jit(solution)/shard_map/pallas_call | solution.py:479
  22.8 2.2 %shard_map.127 = (bf16[1024,2048]{1,0:T(8,128)(2,1)S(1)}, f32[8,128]{1,0:T(8,128)S(1)}) custom-call(bf16[8192,2048]{1,0:T(8,128)(2,1)} %refs_0_.5, f32[8,128]{1,0:T(8,128)S(1)} %get-tuple-element.61.refs_1_, f32[8,128]{1,0:T(8,128)S(1)} %get-tuple-element.62.refs_2_), custom_call_target="tpu_custom_call" | custom-call | flops 262144 | bytes 1024 | tf_op jit(solution)/shard_map/pallas_call | solution.py:64
  25.0 2.4 %shard_map.128 = (bf16[512,256]{1,0:T(8,128)(2,1)S(1)}, bf16[512,256]{1,0:T(8,128)(2,1)S(1)}, bf16[512,256]{1,0:T(8,128)(2,1)S(1)}, bf16[512,256]{1,0:T(8,128)(2,1)S(1)}, f32[8,128]{1,0:T(8,128)S(1)}) custom-call(bf16[1024,2048]{1,0:T(8,128)(2,1)S(1)} %shard_map.125.refs_9_.refs_0_, bf16[1024,2048]{1,0:T(8,128)(2,1)S(1)} %get-tuple-element.63.refs_1_, ...), custom_call_target="tpu_custom_call" | custom-call | flops 2147483648 | bytes 8388608 | tf_op jit(solution)/shard_map/pallas_call | solution.py:64
  27.4 1.7 %collective-permute-start.10 = (bf16[512,256]{1,0:T(8,128)(2,1)S(1)}, bf16[512,256]{1,0:T(8,128)(2,1)S(1)}, u32[]{:S(2)}, u32[]{:S(2)}) collective-permute-start(bf16[512,256]{1,0:T(8,128)(2,1)S(1)} %get-tuple-element.71), channel_id=1, source_target_pairs={{0,24},{8,16},{16,8},{24,0},{1,25},{9,17},{17,9},{25,1},{2,26},{10... | collective-permute-start | bytes 786440 | tf_op jit(solution)/shard_map/ppermute | solution.py:76
  29.6 1.4 %collective-permute-start.12 = (bf16[512,256]{1,0:T(8,128)(2,1)S(1)}, bf16[512,256]{1,0:T(8,128)(2,1)S(1)}, u32[]{:S(2)}, u32[]{:S(2)}) collective-permute-start(bf16[512,256]{1,0:T(8,128)(2,1)S(1)} %get-tuple-element.73), channel_id=1, source_target_pairs={{0,8},{8,0},{16,24},{24,16},{1,9},{9,1},{17,25},{25,17},{2,10},{10... | collective-permute-start | bytes 786440 | tf_op jit(solution)/shard_map/ppermute | solution.py:76
  31.0 5.0 %shard_map.129 = (bf16[512,256]{1,0:T(8,128)(2,1)S(1)}, bf16[512,256]{1,0:T(8,128)(2,1)S(1)}, bf16[512,256]{1,0:T(8,128)(2,1)S(1)}, bf16[512,256]{1,0:T(8,128)(2,1)S(1)}, f32[8,128]{1,0:T(8,128)S(1)}) custom-call(bf16[8192,2048]{1,0:T(8,128)(2,1)} %refs_0_.5, bf16[2064,128]{1,0:T(8,128)(2,1)S(1)} %get-tuple-element.60.refs_2_.refs_1_.refs_0_, ...), custom_call_target="tpu_custom_call" | custom-call | flops 2147483648 | bytes 8388608 | tf_op jit(solution)/shard_map/pallas_call | solution.py:64
  36.0 1.7 %collective-permute-start.7 = (bf16[512,256]{1,0:T(8,128)(2,1)S(1)}, bf16[512,256]{1,0:T(8,128)(2,1)S(1)}, u32[]{:S(2)}, u32[]{:S(2)}) collective-permute-start(bf16[512,256]{1,0:T(8,128)(2,1)S(1)} %get-tuple-element.67), channel_id=1, source_target_pairs={{0,24},{8,16},{16,8},{24,0},{1,25},{9,17},{17,9},{25,1},{2,26},{10... | collective-permute-start | bytes 786440 | tf_op jit(solution)/shard_map/ppermute | solution.py:76
  39.2 1.4 %collective-permute-start.9 = (bf16[512,256]{1,0:T(8,128)(2,1)S(1)}, bf16[512,256]{1,0:T(8,128)(2,1)S(1)}, u32[]{:S(2)}, u32[]{:S(2)}) collective-permute-start(bf16[512,256]{1,0:T(8,128)(2,1)S(1)} %get-tuple-element.69), channel_id=1, source_target_pairs={{0,8},{8,0},{16,24},{24,16},{1,9},{9,1},{17,25},{25,17},{2,10},{10... | collective-permute-start | bytes 786440 | tf_op jit(solution)/shard_map/ppermute | solution.py:76
  40.6 1.5 %shard_map.131 = (bf16[1,32,2048]{2,1,0:T(8,128)(2,1)}, f32[8,128]{1,0:T(8,128)S(1)}) custom-call(s32[1,2]{1,0:T(1,128)S(1)} %copy-done.8, f32[8,128]{1,0:T(8,128)S(1)} %get-tuple-element.61.refs_1_, bf16[1,128,2048]{2,1,0:T(8,128)(2,1)S(1)} %copy-done.4, f32[8,128]{1,0:T(8,128)S(1)} %get-tuple-element.75.refs_3_), custom_call_target="tpu_custom_call" | custom-call | flops 102400000000 | bytes 400000000 | tf_op jit(solution)/shard_map/pallas_call | solution.py:64
  42.1 1.1 %collective-permute-done.11.refs_4_ = bf16[512,256]{1,0:T(8,128)(2,1)S(1)} collective-permute-done((bf16[512,256]{1,0:T(8,128)(2,1)S(1)}, bf16[512,256]{1,0:T(8,128)(2,1)S(1)}, u32[]{:S(2)}, u32[]{:S(2)}) %collective-permute-start.11) | collective-permute-done | bytes 262176 | tf_op jit(solution)/shard_map/ppermute | solution.py:76
  43.6 3.7 %collective-permute-start.16 = (bf16[128,512]{1,0:T(8,128)(2,1)S(1)}, bf16[128,512]{1,0:T(8,128)(2,1)S(1)}, u32[]{:S(2)}, u32[]{:S(2)}) collective-permute-start(bf16[128,512]{1,0:T(8,128)(2,1)S(1)} %get-tuple-element.83), channel_id=1, source_target_pairs={{0,6},{1,7},{2,4},{3,5},{4,2},{5,3},{6,0},{7,1},{8,14},{9,15},{10,... | collective-permute-start | bytes 393224 | tf_op jit(solution)/shard_map/ppermute | solution.py:76
  47.3 1.5 %collective-permute-done.7.refs_3_ = bf16[512,256]{1,0:T(8,128)(2,1)S(1)} collective-permute-done((bf16[512,256]{1,0:T(8,128)(2,1)S(1)}, bf16[512,256]{1,0:T(8,128)(2,1)S(1)}, u32[]{:S(2)}, u32[]{:S(2)}) %collective-permute-start.7) | collective-permute-done | bytes 262176 | tf_op jit(solution)/shard_map/ppermute | solution.py:76
  48.8 1.6 %collective-permute-start.18 = (bf16[128,512]{1,0:T(8,128)(2,1)S(1)}, bf16[128,512]{1,0:T(8,128)(2,1)S(1)}, u32[]{:S(2)}, u32[]{:S(2)}) collective-permute-start(bf16[128,512]{1,0:T(8,128)(2,1)S(1)} %get-tuple-element.85), channel_id=1, source_target_pairs={{0,2},{1,3},{2,0},{3,1},{4,6},{5,7},{6,4},{7,5},{8,10},{9,11},{10,... | collective-permute-start | bytes 393224 | tf_op jit(solution)/shard_map/ppermute | solution.py:76
  50.4 3.5 %collective-permute-done.8.refs_4_ = bf16[512,256]{1,0:T(8,128)(2,1)S(1)} collective-permute-done((bf16[512,256]{1,0:T(8,128)(2,1)S(1)}, bf16[512,256]{1,0:T(8,128)(2,1)S(1)}, u32[]{:S(2)}, u32[]{:S(2)}) %collective-permute-start.8) | collective-permute-done | bytes 262176 | tf_op jit(solution)/shard_map/ppermute | solution.py:76
  54.5 3.7 %collective-permute-start.13 = (bf16[128,512]{1,0:T(8,128)(2,1)S(1)}, bf16[128,512]{1,0:T(8,128)(2,1)S(1)}, u32[]{:S(2)}, u32[]{:S(2)}) collective-permute-start(bf16[128,512]{1,0:T(8,128)(2,1)S(1)} %get-tuple-element.79), channel_id=1, source_target_pairs={{0,6},{1,7},{2,4},{3,5},{4,2},{5,3},{6,0},{7,1},{8,14},{9,15},{10,... | collective-permute-start | bytes 393224 | tf_op jit(solution)/shard_map/ppermute | solution.py:76
  60.1 2.7 %collective-permute-done.13.refs_1_ = bf16[128,512]{1,0:T(8,128)(2,1)S(1)} collective-permute-done((bf16[128,512]{1,0:T(8,128)(2,1)S(1)}, bf16[128,512]{1,0:T(8,128)(2,1)S(1)}, u32[]{:S(2)}, u32[]{:S(2)}) %collective-permute-start.13) | collective-permute-done | bytes 131104 | tf_op jit(solution)/shard_map/ppermute | solution.py:76
  62.8 6.8 %collective-permute-done.14.refs_2_ = bf16[128,512]{1,0:T(8,128)(2,1)S(1)} collective-permute-done((bf16[128,512]{1,0:T(8,128)(2,1)S(1)}, bf16[128,512]{1,0:T(8,128)(2,1)S(1)}, u32[]{:S(2)}, u32[]{:S(2)}) %collective-permute-start.14) | collective-permute-done | bytes 131104 | tf_op jit(solution)/shard_map/ppermute | solution.py:76
  71.8 1.6 %shard_map.139 = (bf16[1,2048,256]{2,1,0:T(8,128)(2,1)}, f32[8,128]{1,0:T(8,128)}) custom-call(bf16[256,512]{1,0:T(8,128)(2,1)S(1)} %collective-permute-done.19.refs_0_, f32[2048,256]{1,0:T(8,128)S(1)} %get-tuple-element.88.refs_1_, bf16[1,2048,256]{2,1,0:T(8,128)(2,1)} %get-tuple-element.98.refs_2_, ...), custom_call_target="tpu_custom_call", output_to_operand_aliasing={{0}: (2, {})} | custom-call | flops 262144 | bytes 1024 | tf_op jit(solution)/shard_map/pallas_call | solution.py:64
  (54 shorter events, 13.9 us)
Async XLA Ops:
  2.8 10.8 %collective-permute-start.2 = (bf16[128,512]{1,0:T(8,128)(2,1)}, bf16[128,512]{1,0:T(8,128)(2,1)S(1)}, u32[]{:S(2)}, u32[]{:S(2)}) collective-permute-start(bf16[128,512]{1,0:T(8,128)(2,1)} %shard_map.122.refs_0_), channel_id=1, source_target_pairs={{0,24},{8,16},{16,8},{24,0},{1,25},{9,17},{17,9},{25,1},{2,26},{10... | collective-permute-start | bytes 393224 | tf_op jit(solution)/shard_map/ppermute | solution.py:76
  6.7 6.9 %collective-permute-start.1 = (bf16[128,512]{1,0:T(8,128)(2,1)}, bf16[128,512]{1,0:T(8,128)(2,1)S(1)}, u32[]{:S(2)}, u32[]{:S(2)}) collective-permute-start(bf16[128,512]{1,0:T(8,128)(2,1)} %shard_map.122.refs_0_), channel_id=1, source_target_pairs={{0,16},{8,24},{16,0},{24,8},{1,17},{9,25},{17,1},{25,9},{2,18},{10... | collective-permute-start | bytes 393224 | tf_op jit(solution)/shard_map/ppermute | solution.py:76
  7.2 6.4 %collective-permute-start = (bf16[128,512]{1,0:T(8,128)(2,1)}, bf16[128,512]{1,0:T(8,128)(2,1)S(1)}, u32[]{:S(2)}, u32[]{:S(2)}) collective-permute-start(bf16[128,512]{1,0:T(8,128)(2,1)} %shard_map.122.refs_0_), channel_id=1, source_target_pairs={{0,8},{8,0},{16,24},{24,16},{1,9},{9,1},{17,25},{25,17},{2,10},{10... | collective-permute-start | bytes 393224 | tf_op jit(solution)/shard_map/ppermute | solution.py:76
  15.4 7.0 %copy-start.7 = (s32[1,128,1]{1,2,0:T(1,128)S(1)}, s32[1,128,1]{1,2,0:T(1,128)}, u32[]{:S(2)}) copy-start(s32[1,128,1]{1,2,0:T(1,128)} %param.15) | copy-start | bytes 1540
  15.4 5.8 %collective-permute-start.5 = (f32[8,128]{1,0:T(8,128)S(1)}, f32[8,128]{1,0:T(8,128)S(1)}, u32[]{:S(2)}, u32[]{:S(2)}) collective-permute-start(f32[8,128]{1,0:T(8,128)S(1)} %get-tuple-element.56.after_ref.refs_0_), channel_id=1, source_target_pairs={{0,24},{8,16},{16,8},{24,0},{1,25},{9,17},{17,9},{25,1},{2,26},{10... | collective-permute-start | bytes 12296 | tf_op jit(solution)/shard_map/ppermute | solution.py:76
  18.3 3.6 %collective-permute-start.4 = (f32[8,128]{1,0:T(8,128)S(1)}, f32[8,128]{1,0:T(8,128)S(1)}, u32[]{:S(2)}, u32[]{:S(2)}) collective-permute-start(f32[8,128]{1,0:T(8,128)S(1)} %get-tuple-element.56.after_ref.refs_0_), channel_id=1, source_target_pairs={{0,16},{8,24},{16,0},{24,8},{1,17},{9,25},{17,1},{25,9},{2,18},{10... | collective-permute-start | bytes 12296 | tf_op jit(solution)/shard_map/ppermute | solution.py:76
  18.8 3.6 %collective-permute-start.3 = (f32[8,128]{1,0:T(8,128)S(1)}, f32[8,128]{1,0:T(8,128)S(1)}, u32[]{:S(2)}, u32[]{:S(2)}) collective-permute-start(f32[8,128]{1,0:T(8,128)S(1)} %get-tuple-element.56.after_ref.refs_0_), channel_id=1, source_target_pairs={{0,8},{8,0},{16,24},{24,16},{1,9},{9,1},{17,25},{25,17},{2,10},{10... | collective-permute-start | bytes 12296 | tf_op jit(solution)/shard_map/ppermute | solution.py:76
  22.7 2.3 %collective-permute-start.6 = (bf16[2064,128]{1,0:T(8,128)(2,1)S(1)}, bf16[2064,128]{1,0:T(8,128)(2,1)S(1)}, u32[]{:S(2)}, u32[]{:S(2)}) collective-permute-start(bf16[2064,128]{1,0:T(8,128)(2,1)S(1)} %get-tuple-element.60.refs_2_.refs_1_.refs_0_), channel_id=1, source_target_pairs={{0,1},{1,0},{2,3},{3,2},{4,5},{5,4},{6,7},{7,6},{8,9},{9,8},{10,11... | collective-permute-start | bytes 1585160 | tf_op jit(solution)/shard_map/ppermute | solution.py:76
  27.4 11.8 %collective-permute-start.10 = (bf16[512,256]{1,0:T(8,128)(2,1)S(1)}, bf16[512,256]{1,0:T(8,128)(2,1)S(1)}, u32[]{:S(2)}, u32[]{:S(2)}) collective-permute-start(bf16[512,256]{1,0:T(8,128)(2,1)S(1)} %get-tuple-element.71), channel_id=1, source_target_pairs={{0,24},{8,16},{16,8},{24,0},{1,25},{9,17},{17,9},{25,1},{2,26},{10... | collective-permute-start | bytes 786440 | tf_op jit(solution)/shard_map/ppermute | solution.py:76
  29.1 14.1 %collective-permute-start.11 = (bf16[512,256]{1,0:T(8,128)(2,1)S(1)}, bf16[512,256]{1,0:T(8,128)(2,1)S(1)}, u32[]{:S(2)}, u32[]{:S(2)}) collective-permute-start(bf16[512,256]{1,0:T(8,128)(2,1)S(1)} %get-tuple-element.72), channel_id=1, source_target_pairs={{0,16},{8,24},{16,0},{24,8},{1,17},{9,25},{17,1},{25,9},{2,18},{10... | collective-permute-start | bytes 786440 | tf_op jit(solution)/shard_map/ppermute | solution.py:76
  29.6 13.6 %collective-permute-start.12 = (bf16[512,256]{1,0:T(8,128)(2,1)S(1)}, bf16[512,256]{1,0:T(8,128)(2,1)S(1)}, u32[]{:S(2)}, u32[]{:S(2)}) collective-permute-start(bf16[512,256]{1,0:T(8,128)(2,1)S(1)} %get-tuple-element.73), channel_id=1, source_target_pairs={{0,8},{8,0},{16,24},{24,16},{1,9},{9,1},{17,25},{25,17},{2,10},{10... | collective-permute-start | bytes 786440 | tf_op jit(solution)/shard_map/ppermute | solution.py:76
  31.0 7.2 %copy-start = (bf16[1,2048,256]{2,1,0:T(8,128)(2,1)S(1)}, bf16[1,2048,256]{2,1,0:T(8,128)(2,1)}, u32[]{:S(2)}) copy-start(bf16[1,2048,256]{2,1,0:T(8,128)(2,1)} %refs_0_.6) | copy-start | bytes 3145732
  31.0 9.6 %copy-start.4 = (bf16[1,128,2048]{2,1,0:T(8,128)(2,1)S(1)}, bf16[1,128,2048]{2,1,0:T(8,128)(2,1)}, u32[]{:S(2)}) copy-start(bf16[1,128,2048]{2,1,0:T(8,128)(2,1)} %refs_2_.1) | copy-start | bytes 1572868
  36.0 12.8 %collective-permute-start.7 = (bf16[512,256]{1,0:T(8,128)(2,1)S(1)}, bf16[512,256]{1,0:T(8,128)(2,1)S(1)}, u32[]{:S(2)}, u32[]{:S(2)}) collective-permute-start(bf16[512,256]{1,0:T(8,128)(2,1)S(1)} %get-tuple-element.67), channel_id=1, source_target_pairs={{0,24},{8,16},{16,8},{24,0},{1,25},{9,17},{17,9},{25,1},{2,26},{10... | collective-permute-start | bytes 786440 | tf_op jit(solution)/shard_map/ppermute | solution.py:76
  37.7 16.2 %collective-permute-start.8 = (bf16[512,256]{1,0:T(8,128)(2,1)S(1)}, bf16[512,256]{1,0:T(8,128)(2,1)S(1)}, u32[]{:S(2)}, u32[]{:S(2)}) collective-permute-start(bf16[512,256]{1,0:T(8,128)(2,1)S(1)} %get-tuple-element.68), channel_id=1, source_target_pairs={{0,16},{8,24},{16,0},{24,8},{1,17},{9,25},{17,1},{25,9},{2,18},{10... | collective-permute-start | bytes 786440 | tf_op jit(solution)/shard_map/ppermute | solution.py:76
  39.2 14.9 %collective-permute-start.9 = (bf16[512,256]{1,0:T(8,128)(2,1)S(1)}, bf16[512,256]{1,0:T(8,128)(2,1)S(1)}, u32[]{:S(2)}, u32[]{:S(2)}) collective-permute-start(bf16[512,256]{1,0:T(8,128)(2,1)S(1)} %get-tuple-element.69), channel_id=1, source_target_pairs={{0,8},{8,0},{16,24},{24,16},{1,9},{9,1},{17,25},{25,17},{2,10},{10... | collective-permute-start | bytes 786440 | tf_op jit(solution)/shard_map/ppermute | solution.py:76
  43.6 14.5 %collective-permute-start.16 = (bf16[128,512]{1,0:T(8,128)(2,1)S(1)}, bf16[128,512]{1,0:T(8,128)(2,1)S(1)}, u32[]{:S(2)}, u32[]{:S(2)}) collective-permute-start(bf16[128,512]{1,0:T(8,128)(2,1)S(1)} %get-tuple-element.83), channel_id=1, source_target_pairs={{0,6},{1,7},{2,4},{3,5},{4,2},{5,3},{6,0},{7,1},{8,14},{9,15},{10,... | collective-permute-start | bytes 393224 | tf_op jit(solution)/shard_map/ppermute | solution.py:76
  47.3 11.7 %collective-permute-start.17 = (bf16[128,512]{1,0:T(8,128)(2,1)S(1)}, bf16[128,512]{1,0:T(8,128)(2,1)S(1)}, u32[]{:S(2)}, u32[]{:S(2)}) collective-permute-start(bf16[128,512]{1,0:T(8,128)(2,1)S(1)} %get-tuple-element.84), channel_id=1, source_target_pairs={{0,4},{1,5},{2,6},{3,7},{4,0},{5,1},{6,2},{7,3},{8,12},{9,13},{10,... | collective-permute-start | bytes 393224 | tf_op jit(solution)/shard_map/ppermute | solution.py:76
  48.8 10.2 %collective-permute-start.18 = (bf16[128,512]{1,0:T(8,128)(2,1)S(1)}, bf16[128,512]{1,0:T(8,128)(2,1)S(1)}, u32[]{:S(2)}, u32[]{:S(2)}) collective-permute-start(bf16[128,512]{1,0:T(8,128)(2,1)S(1)} %get-tuple-element.85), channel_id=1, source_target_pairs={{0,2},{1,3},{2,0},{3,1},{4,6},{5,7},{6,4},{7,5},{8,10},{9,11},{10,... | collective-permute-start | bytes 393224 | tf_op jit(solution)/shard_map/ppermute | solution.py:76
  54.5 8.3 %collective-permute-start.13 = (bf16[128,512]{1,0:T(8,128)(2,1)S(1)}, bf16[128,512]{1,0:T(8,128)(2,1)S(1)}, u32[]{:S(2)}, u32[]{:S(2)}) collective-permute-start(bf16[128,512]{1,0:T(8,128)(2,1)S(1)} %get-tuple-element.79), channel_id=1, source_target_pairs={{0,6},{1,7},{2,4},{3,5},{4,2},{5,3},{6,0},{7,1},{8,14},{9,15},{10,... | collective-permute-start | bytes 393224 | tf_op jit(solution)/shard_map/ppermute | solution.py:76
  58.2 11.4 %collective-permute-start.14 = (bf16[128,512]{1,0:T(8,128)(2,1)S(1)}, bf16[128,512]{1,0:T(8,128)(2,1)S(1)}, u32[]{:S(2)}, u32[]{:S(2)}) collective-permute-start(bf16[128,512]{1,0:T(8,128)(2,1)S(1)} %get-tuple-element.80), channel_id=1, source_target_pairs={{0,4},{1,5},{2,6},{3,7},{4,0},{5,1},{6,2},{7,3},{8,12},{9,13},{10,... | collective-permute-start | bytes 393224 | tf_op jit(solution)/shard_map/ppermute | solution.py:76
  58.2 11.4 %collective-permute-start.15 = (bf16[128,512]{1,0:T(8,128)(2,1)S(1)}, bf16[128,512]{1,0:T(8,128)(2,1)S(1)}, u32[]{:S(2)}, u32[]{:S(2)}) collective-permute-start(bf16[128,512]{1,0:T(8,128)(2,1)S(1)} %get-tuple-element.81), channel_id=1, source_target_pairs={{0,2},{1,3},{2,0},{3,1},{4,6},{5,7},{6,4},{7,5},{8,10},{9,11},{10,... | collective-permute-start | bytes 393224 | tf_op jit(solution)/shard_map/ppermute | solution.py:76
  59.0 10.7 %collective-permute-start.20 = (bf16[256,512]{1,0:T(8,128)(2,1)S(1)}, bf16[256,512]{1,0:T(8,128)(2,1)S(1)}, u32[]{:S(2)}, u32[]{:S(2)}) collective-permute-start(bf16[256,512]{1,0:T(8,128)(2,1)S(1)} %get-tuple-element.93), channel_id=1, source_target_pairs={{0,1},{1,0},{2,3},{3,2},{4,5},{5,4},{6,7},{7,6},{8,9},{9,8},{10,11... | collective-permute-start | bytes 786440 | tf_op jit(solution)/shard_map/ppermute | solution.py:76
  69.7 2.1 %collective-permute-start.19 = (bf16[256,512]{1,0:T(8,128)(2,1)S(1)}, bf16[256,512]{1,0:T(8,128)(2,1)S(1)}, u32[]{:S(2)}, u32[]{:S(2)}) collective-permute-start(bf16[256,512]{1,0:T(8,128)(2,1)S(1)} %get-tuple-element.91), channel_id=1, source_target_pairs={{0,1},{1,0},{2,3},{3,2},{4,5},{5,4},{6,7},{7,6},{8,9},{9,8},{10,11... | collective-permute-start | bytes 786440 | tf_op jit(solution)/shard_map/ppermute | solution.py:76
  (6 other events, 5.2 us)

commit v4 on v3

--- a/solution.py
+++ b/solution.py
@@ -14,7 +14,7 @@
 LANES = 128
 AHEAD = 4
 MIB = 1024 * 1024
-GRANT, LOAD_GRANT, PICK_GRANT = 40, 46, 54
+GRANT, LOAD_GRANT, PICK_GRANT = 40, 46, 53
 HBM = pl.BlockSpec(memory_space=pltpu.HBM)
 VMEM = pl.BlockSpec(memory_space=pltpu.VMEM)
 ANY = pl.BlockSpec(memory_space=pl.ANY)
@@ -125,49 +125,39 @@
 
 
 def load_kernel(
-    span_hbm, hidden_hbm, gain_hbm, proj_hbm, resid_hbm, weight_hbm,
+    span_hbm, hidden_ref, gain_ref, proj_ref, resid_ref, weight_hbm,
     stats_ref, projt_ref, residt_ref, gaint_ref, meant_ref, weight_ref,
-    span, hidden, gain, proj, resid, sems,
+    span, sems,
 ):
-    copies = [
-        pltpu.make_async_copy(source, target, sems.at[index])
-        for index, (source, target) in enumerate(
-            [
-                (span_hbm, span),
-                (hidden_hbm.at[0], hidden),
-                (gain_hbm, gain),
-                (proj_hbm.at[0], proj),
-                (resid_hbm.at[0], resid),
-                (weight_hbm, weight_ref),
-            ]
-        )
-    ]
-    for copy in copies:
-        copy.start()
-    for copy in copies[:5]:
-        copy.wait()
+    load = pltpu.make_async_copy(weight_hbm, weight_ref, sems.at[0])
+    head = pltpu.make_async_copy(span_hbm, span, sems.at[1])
+    head.start()
+    load.start()
+    tokens, width = proj_ref.shape[1:]
+    for at in range(0, width, LANES):
+        cut = slice(at, at + LANES)
+        gaint_ref[cut, :] = to_column(gain_ref[:, cut])
+        projt_ref[cut, :] = jnp.transpose(proj_ref[0, :, cut].astype(F32), (1, 0))
+        residt_ref[cut, :] = jnp.transpose(resid_ref[0, :, cut].astype(F32), (1, 0))
+    head.wait()
     start, count = span[0, 0], span[0, 1]
-    tokens, width = proj.shape
-    places = lax.broadcasted_iota(jnp.int32, (hidden.shape[0], 1), 0)
+    places = lax.broadcasted_iota(jnp.int32, (hidden_ref.shape[1], 1), 0)
     mask = ((places >= start) & (places < start + count)).astype(F32)
     query = square = cross = jnp.zeros((LANES, tokens), F32)
     for at in range(0, width, LANES):
         cut = slice(at, at + LANES)
-        mean = jnp.sum(hidden[:, cut].astype(F32) * mask, axis=0, keepdims=True)
+        mean = jnp.sum(hidden_ref[0, :, cut].astype(F32) * mask, axis=0, keepdims=True)
         meant = to_column(mean / count.astype(F32))
-        projt = jnp.transpose(proj[:, cut].astype(F32), (1, 0))
-        residt = jnp.transpose(resid[:, cut].astype(F32), (1, 0))
         meant_ref[cut, :] = meant
-        projt_ref[cut, :] = projt
-        residt_ref[cut, :] = residt
-        gaint_ref[cut, :] = to_column(gain[:, cut])
+        projt = projt_ref[cut, :]
+        residt = residt_ref[cut, :]
         query = query + projt * meant
         square = square + projt * projt
         cross = cross + projt * residt
     stats_ref[...] = jnp.zeros(stats_ref.shape, F32)
     for row, value in enumerate((query, square, cross)):
         stats_ref[row : row + 1, :] = jnp.sum(value, axis=0, keepdims=True)
-    copies[5].wait()
+    load.wait()
 
 
 def norm_kernel(peers, *refs):
@@ -444,15 +434,8 @@
     stats, projt, residt, gaint, meant, weight = call(
         load_kernel,
         [row, tall, tall, tall, tall, shape(w_value.shape, BF16)],
-        [HBM] * 6,
-        [
-            pltpu.SMEM((1, 2), jnp.int32),
-            pltpu.VMEM((length, width), BF16),
-            pltpu.VMEM((1, width), F32),
-            pltpu.VMEM((tokens, width), BF16),
-            pltpu.VMEM((tokens, width), BF16),
-            dma((6,)),
-        ],
+        [HBM, VMEM, VMEM, VMEM, VMEM, HBM],
+        [pltpu.SMEM((1, 2), jnp.int32), dma((2,))],
         grant=LOAD_GRANT,
     )(ques_span, ques_hidden, gain, vis_proj, vis_resid, w_value)
 

time: 73.7 us -> 73.1 us (level)
  no operation moved by 1% of the time
where the time goes in v4:
time: 73.1 us; the launch traced here: 72.7 us
  starting transfers between devices  25.2 us (34%)
  Pallas kernels  24.4 us (33%)
  waiting for transfers between devices  17.2 us (24%)
  local copies, waits for them, and re-layouts  5 us (7%)
  between operations  0.88 us (1%)
    ppermute x21, starting transfers between devices, swap(): return lax.ppermute(value, axis, [(i, i ^ step) for i in range(count)])  25.2 us
    pallas_call x14, Pallas kernels, apply(): *results, token = run_call(*args, *self.last)  17.7 us
    ppermute x21, waiting for transfers between devices, swap(): return lax.ppermute(value, axis, [(i, i ^ step) for i in range(count)])  17.2 us
    unnamed x18, local copies, waits for them, and re-layouts  5 us
    pallas_call x1, Pallas kernels, preload(): caller(functools.partial(preload_kernel, half * count, count, peers, shar...  2.2 us
    pallas_call x1, Pallas kernels, body(): call(load_kernel, [row, tall, tall, tall, tall, shape(w_value.shape, BF16...  2.12 us
    pallas_call x1, Pallas kernels, body(): call(functools.partial(pick_kernel, pieces), shape((tokens, key_width), B...  1.48 us
  transfers between devices with their start and end apart: 21, of which 8 were waited for; matrix products, arithmetic and copies ran while one was open for 0% of the time, Pallas kernels for 24%

profile of v4, /device:TPU:0, one launch (start us, length us, event | category | flops | bytes accessed | tf_op | source)
XLA Modules:
  0.0 72.7 jit_solution(15125340891697676228)
XLA Ops:
  1.3 1.5 %shard_map.122.refs_0_ = bf16[128,512]{1,0:T(8,128)(2,1)S(1)} custom-call(s32[1,128]{1,0:T(1,128)S(1)} %copy-done.5, bf16[1,1024,512]{2,1,0:T(8,128)(2,1)} %rows_hbm.1), custom_call_target="tpu_custom_call" | custom-call | flops 262144 | bytes 1024 | tf_op jit(solution)/shard_map/pallas_call | solution.py:421
  2.8 4.0 %collective-permute-start.2 = (bf16[128,512]{1,0:T(8,128)(2,1)S(1)}, bf16[128,512]{1,0:T(8,128)(2,1)S(1)}, u32[]{:S(2)}, u32[]{:S(2)}) collective-permute-start(bf16[128,512]{1,0:T(8,128)(2,1)S(1)} %shard_map.122.refs_0_), channel_id=1, source_target_pairs={{0,24},{8,16},{16,8},{24,0},{1,25},{9,17},{17,9},{25,1},{2,26},{10... | collective-permute-start | bytes 393224 | tf_op jit(solution)/shard_map/ppermute | solution.py:76
  7.4 1.0 %copy-done.1 = bf16[1,128,2048]{2,1,0:T(8,128)(2,1)S(1)} copy-done((bf16[1,128,2048]{2,1,0:T(8,128)(2,1)S(1)}, bf16[1,128,2048]{2,1,0:T(8,128)(2,1)}, u32[]{:S(2)}) %copy-start.1) | copy-done | bytes 524312
  8.4 1.0 %copy-done.2 = bf16[1,128,2048]{2,1,0:T(8,128)(2,1)S(1)} copy-done((bf16[1,128,2048]{2,1,0:T(8,128)(2,1)S(1)}, bf16[1,128,2048]{2,1,0:T(8,128)(2,1)}, u32[]{:S(2)}) %copy-start.2) | copy-done | bytes 524312
  11.7 2.1 %shard_map.123 = (f32[8,128]{1,0:T(8,128)S(1)}, f32[2048,128]{1,0:T(8,128)S(1)}, f32[2048,128]{1,0:T(8,128)S(1)}, f32[2048,128]{1,0:T(8,128)S(1)}, f32[2048,128]...) custom-call(s32[1,2]{1,0:T(1,128)S(1)} %copy-done.7, bf16[1,32,2048]{2,1,0:T(8,128)(2,1)S(1)} %copy-done.3, ...), custom_call_target="tpu_custom_call" | custom-call | flops 262144 | bytes 1024 | tf_op jit(solution)/shard_map/pallas_call | solution.py:434
  14.7 2.9 %collective-permute-start.5 = (f32[8,128]{1,0:T(8,128)S(1)}, f32[8,128]{1,0:T(8,128)S(1)}, u32[]{:S(2)}, u32[]{:S(2)}) collective-permute-start(f32[8,128]{1,0:T(8,128)S(1)} %get-tuple-element.56.after_ref.refs_0_), channel_id=1, source_target_pairs={{0,24},{8,16},{16,8},{24,0},{1,25},{9,17},{17,9},{25,1},{2,26},{10... | collective-permute-start | bytes 12296 | tf_op jit(solution)/shard_map/ppermute | solution.py:76
  18.3 2.2 %shard_map.125.refs_9_.refs_0_ = bf16[1024,2048]{1,0:T(8,128)(2,1)S(1)} custom-call(bf16[8192,2048]{1,0:T(8,128)(2,1)} %refs_0_.5, f32[8,128]{1,0:T(8,128)S(1)} %get-tuple-element.56.after_ref.refs_0_), custom_call_target="tpu_custom_call" | custom-call | flops 262144 | bytes 1024 | tf_op jit(solution)/shard_map/pallas_call | solution.py:462
  22.1 2.2 %shard_map.127 = (bf16[1024,2048]{1,0:T(8,128)(2,1)S(1)}, f32[8,128]{1,0:T(8,128)S(1)}) custom-call(bf16[8192,2048]{1,0:T(8,128)(2,1)} %refs_0_.5, f32[8,128]{1,0:T(8,128)S(1)} %get-tuple-element.61.refs_1_, f32[8,128]{1,0:T(8,128)S(1)} %get-tuple-element.62.refs_2_), custom_call_target="tpu_custom_call" | custom-call | flops 262144 | bytes 1024 | tf_op jit(solution)/shard_map/pallas_call | solution.py:64
  24.4 2.4 %shard_map.128 = (bf16[512,256]{1,0:T(8,128)(2,1)S(1)}, bf16[512,256]{1,0:T(8,128)(2,1)S(1)}, bf16[512,256]{1,0:T(8,128)(2,1)S(1)}, bf16[512,256]{1,0:T(8,128)(2,1)S(1)}, f32[8,128]{1,0:T(8,128)S(1)}) custom-call(bf16[1024,2048]{1,0:T(8,128)(2,1)S(1)} %shard_map.125.refs_9_.refs_0_, bf16[1024,2048]{1,0:T(8,128)(2,1)S(1)} %get-tuple-element.63.refs_1_, ...), custom_call_target="tpu_custom_call" | custom-call | flops 2147483648 | bytes 8388608 | tf_op jit(solution)/shard_map/pallas_call | solution.py:64
  26.8 1.7 %collective-permute-start.10 = (bf16[512,256]{1,0:T(8,128)(2,1)S(1)}, bf16[512,256]{1,0:T(8,128)(2,1)S(1)}, u32[]{:S(2)}, u32[]{:S(2)}) collective-permute-start(bf16[512,256]{1,0:T(8,128)(2,1)S(1)} %get-tuple-element.71), channel_id=1, source_target_pairs={{0,24},{8,16},{16,8},{24,0},{1,25},{9,17},{17,9},{25,1},{2,26},{10... | collective-permute-start | bytes 786440 | tf_op jit(solution)/shard_map/ppermute | solution.py:76
  29.0 1.4 %collective-permute-start.12 = (bf16[512,256]{1,0:T(8,128)(2,1)S(1)}, bf16[512,256]{1,0:T(8,128)(2,1)S(1)}, u32[]{:S(2)}, u32[]{:S(2)}) collective-permute-start(bf16[512,256]{1,0:T(8,128)(2,1)S(1)} %get-tuple-element.73), channel_id=1, source_target_pairs={{0,8},{8,0},{16,24},{24,16},{1,9},{9,1},{17,25},{25,17},{2,10},{10... | collective-permute-start | bytes 786440 | tf_op jit(solution)/shard_map/ppermute | solution.py:76
  30.3 4.9 %shard_map.129 = (bf16[512,256]{1,0:T(8,128)(2,1)S(1)}, bf16[512,256]{1,0:T(8,128)(2,1)S(1)}, bf16[512,256]{1,0:T(8,128)(2,1)S(1)}, bf16[512,256]{1,0:T(8,128)(2,1)S(1)}, f32[8,128]{1,0:T(8,128)S(1)}) custom-call(bf16[8192,2048]{1,0:T(8,128)(2,1)} %refs_0_.5, bf16[2064,128]{1,0:T(8,128)(2,1)S(1)} %get-tuple-element.60.refs_2_.refs_1_.refs_0_, ...), custom_call_target="tpu_custom_call" | custom-call | flops 2147483648 | bytes 8388608 | tf_op jit(solution)/shard_map/pallas_call | solution.py:64
  35.3 1.7 %collective-permute-start.7 = (bf16[512,256]{1,0:T(8,128)(2,1)S(1)}, bf16[512,256]{1,0:T(8,128)(2,1)S(1)}, u32[]{:S(2)}, u32[]{:S(2)}) collective-permute-start(bf16[512,256]{1,0:T(8,128)(2,1)S(1)} %get-tuple-element.67), channel_id=1, source_target_pairs={{0,24},{8,16},{16,8},{24,0},{1,25},{9,17},{17,9},{25,1},{2,26},{10... | collective-permute-start | bytes 786440 | tf_op jit(solution)/shard_map/ppermute | solution.py:76
  38.5 1.4 %collective-permute-start.9 = (bf16[512,256]{1,0:T(8,128)(2,1)S(1)}, bf16[512,256]{1,0:T(8,128)(2,1)S(1)}, u32[]{:S(2)}, u32[]{:S(2)}) collective-permute-start(bf16[512,256]{1,0:T(8,128)(2,1)S(1)} %get-tuple-element.69), channel_id=1, source_target_pairs={{0,8},{8,0},{16,24},{24,16},{1,9},{9,1},{17,25},{25,17},{2,10},{10... | collective-permute-start | bytes 786440 | tf_op jit(solution)/shard_map/ppermute | solution.py:76
  39.9 1.5 %shard_map.131 = (bf16[1,32,2048]{2,1,0:T(8,128)(2,1)}, f32[8,128]{1,0:T(8,128)S(1)}) custom-call(s32[1,2]{1,0:T(1,128)S(1)} %copy-done.8, f32[8,128]{1,0:T(8,128)S(1)} %get-tuple-element.61.refs_1_, bf16[1,128,2048]{2,1,0:T(8,128)(2,1)S(1)} %copy-done.2, f32[8,128]{1,0:T(8,128)S(1)} %get-tuple-element.75.refs_3_), custom_call_target="tpu_custom_call" | custom-call | flops 102400000000 | bytes 400000000 | tf_op jit(solution)/shard_map/pallas_call | solution.py:64
  41.4 1.2 %collective-permute-done.11.refs_4_ = bf16[512,256]{1,0:T(8,128)(2,1)S(1)} collective-permute-done((bf16[512,256]{1,0:T(8,128)(2,1)S(1)}, bf16[512,256]{1,0:T(8,128)(2,1)S(1)}, u32[]{:S(2)}, u32[]{:S(2)}) %collective-permute-start.11) | collective-permute-done | bytes 262176 | tf_op jit(solution)/shard_map/ppermute | solution.py:76
  43.0 3.7 %collective-permute-start.16 = (bf16[128,512]{1,0:T(8,128)(2,1)S(1)}, bf16[128,512]{1,0:T(8,128)(2,1)S(1)}, u32[]{:S(2)}, u32[]{:S(2)}) collective-permute-start(bf16[128,512]{1,0:T(8,128)(2,1)S(1)} %get-tuple-element.83), channel_id=1, source_target_pairs={{0,6},{1,7},{2,4},{3,5},{4,2},{5,3},{6,0},{7,1},{8,14},{9,15},{10,... | collective-permute-start | bytes 393224 | tf_op jit(solution)/shard_map/ppermute | solution.py:76
  46.7 1.5 %collective-permute-done.7.refs_3_ = bf16[512,256]{1,0:T(8,128)(2,1)S(1)} collective-permute-done((bf16[512,256]{1,0:T(8,128)(2,1)S(1)}, bf16[512,256]{1,0:T(8,128)(2,1)S(1)}, u32[]{:S(2)}, u32[]{:S(2)}) %collective-permute-start.7) | collective-permute-done | bytes 262176 | tf_op jit(solution)/shard_map/ppermute | solution.py:76
  48.2 1.6 %collective-permute-start.18 = (bf16[128,512]{1,0:T(8,128)(2,1)S(1)}, bf16[128,512]{1,0:T(8,128)(2,1)S(1)}, u32[]{:S(2)}, u32[]{:S(2)}) collective-permute-start(bf16[128,512]{1,0:T(8,128)(2,1)S(1)} %get-tuple-element.85), channel_id=1, source_target_pairs={{0,2},{1,3},{2,0},{3,1},{4,6},{5,7},{6,4},{7,5},{8,10},{9,11},{10,... | collective-permute-start | bytes 393224 | tf_op jit(solution)/shard_map/ppermute | solution.py:76
  49.8 3.5 %collective-permute-done.8.refs_4_ = bf16[512,256]{1,0:T(8,128)(2,1)S(1)} collective-permute-done((bf16[512,256]{1,0:T(8,128)(2,1)S(1)}, bf16[512,256]{1,0:T(8,128)(2,1)S(1)}, u32[]{:S(2)}, u32[]{:S(2)}) %collective-permute-start.8) | collective-permute-done | bytes 262176 | tf_op jit(solution)/shard_map/ppermute | solution.py:76
  53.9 3.7 %collective-permute-start.13 = (bf16[128,512]{1,0:T(8,128)(2,1)S(1)}, bf16[128,512]{1,0:T(8,128)(2,1)S(1)}, u32[]{:S(2)}, u32[]{:S(2)}) collective-permute-start(bf16[128,512]{1,0:T(8,128)(2,1)S(1)} %get-tuple-element.79), channel_id=1, source_target_pairs={{0,6},{1,7},{2,4},{3,5},{4,2},{5,3},{6,0},{7,1},{8,14},{9,15},{10,... | collective-permute-start | bytes 393224 | tf_op jit(solution)/shard_map/ppermute | solution.py:76
  59.5 2.7 %collective-permute-done.13.refs_1_ = bf16[128,512]{1,0:T(8,128)(2,1)S(1)} collective-permute-done((bf16[128,512]{1,0:T(8,128)(2,1)S(1)}, bf16[128,512]{1,0:T(8,128)(2,1)S(1)}, u32[]{:S(2)}, u32[]{:S(2)}) %collective-permute-start.13) | collective-permute-done | bytes 131104 | tf_op jit(solution)/shard_map/ppermute | solution.py:76
  62.2 6.8 %collective-permute-done.14.refs_2_ = bf16[128,512]{1,0:T(8,128)(2,1)S(1)} collective-permute-done((bf16[128,512]{1,0:T(8,128)(2,1)S(1)}, bf16[128,512]{1,0:T(8,128)(2,1)S(1)}, u32[]{:S(2)}, u32[]{:S(2)}) %collective-permute-start.14) | collective-permute-done | bytes 131104 | tf_op jit(solution)/shard_map/ppermute | solution.py:76
  71.1 1.6 %shard_map.139 = (bf16[1,2048,256]{2,1,0:T(8,128)(2,1)}, f32[8,128]{1,0:T(8,128)}) custom-call(bf16[256,512]{1,0:T(8,128)(2,1)S(1)} %collective-permute-done.19.refs_0_, f32[2048,256]{1,0:T(8,128)S(1)} %get-tuple-element.88.refs_1_, bf16[1,2048,256]{2,1,0:T(8,128)(2,1)} %get-tuple-element.98.refs_2_, ...), custom_call_target="tpu_custom_call", output_to_operand_aliasing={{0}: (2, {})} | custom-call | flops 262144 | bytes 1024 | tf_op jit(solution)/shard_map/pallas_call | solution.py:64
  (54 shorter events, 13.6 us)
Async XLA Ops:
  2.8 11.1 %collective-permute-start.2 = (bf16[128,512]{1,0:T(8,128)(2,1)S(1)}, bf16[128,512]{1,0:T(8,128)(2,1)S(1)}, u32[]{:S(2)}, u32[]{:S(2)}) collective-permute-start(bf16[128,512]{1,0:T(8,128)(2,1)S(1)} %shard_map.122.refs_0_), channel_id=1, source_target_pairs={{0,24},{8,16},{16,8},{24,0},{1,25},{9,17},{17,9},{25,1},{2,26},{10... | collective-permute-start | bytes 393224 | tf_op jit(solution)/shard_map/ppermute | solution.py:76
  6.7 7.1 %collective-permute-start.1 = (bf16[128,512]{1,0:T(8,128)(2,1)S(1)}, bf16[128,512]{1,0:T(8,128)(2,1)S(1)}, u32[]{:S(2)}, u32[]{:S(2)}) collective-permute-start(bf16[128,512]{1,0:T(8,128)(2,1)S(1)} %shard_map.122.refs_0_), channel_id=1, source_target_pairs={{0,16},{8,24},{16,0},{24,8},{1,17},{9,25},{17,1},{25,9},{2,18},{10... | collective-permute-start | bytes 393224 | tf_op jit(solution)/shard_map/ppermute | solution.py:76
  7.2 6.6 %collective-permute-start = (bf16[128,512]{1,0:T(8,128)(2,1)S(1)}, bf16[128,512]{1,0:T(8,128)(2,1)S(1)}, u32[]{:S(2)}, u32[]{:S(2)}) collective-permute-start(bf16[128,512]{1,0:T(8,128)(2,1)S(1)} %shard_map.122.refs_0_), channel_id=1, source_target_pairs={{0,8},{8,0},{16,24},{24,16},{1,9},{9,1},{17,25},{25,17},{2,10},{10... | collective-permute-start | bytes 393224 | tf_op jit(solution)/shard_map/ppermute | solution.py:76
  14.7 7.0 %copy-start.6 = (s32[1,128,1]{1,2,0:T(1,128)S(1)}, s32[1,128,1]{1,2,0:T(1,128)}, u32[]{:S(2)}) copy-start(s32[1,128,1]{1,2,0:T(1,128)} %param.15) | copy-start | bytes 1540
  14.7 5.8 %collective-permute-start.5 = (f32[8,128]{1,0:T(8,128)S(1)}, f32[8,128]{1,0:T(8,128)S(1)}, u32[]{:S(2)}, u32[]{:S(2)}) collective-permute-start(f32[8,128]{1,0:T(8,128)S(1)} %get-tuple-element.56.after_ref.refs_0_), channel_id=1, source_target_pairs={{0,24},{8,16},{16,8},{24,0},{1,25},{9,17},{17,9},{25,1},{2,26},{10... | collective-permute-start | bytes 12296 | tf_op jit(solution)/shard_map/ppermute | solution.py:76
  17.7 3.6 %collective-permute-start.4 = (f32[8,128]{1,0:T(8,128)S(1)}, f32[8,128]{1,0:T(8,128)S(1)}, u32[]{:S(2)}, u32[]{:S(2)}) collective-permute-start(f32[8,128]{1,0:T(8,128)S(1)} %get-tuple-element.56.after_ref.refs_0_), channel_id=1, source_target_pairs={{0,16},{8,24},{16,0},{24,8},{1,17},{9,25},{17,1},{25,9},{2,18},{10... | collective-permute-start | bytes 12296 | tf_op jit(solution)/shard_map/ppermute | solution.py:76
  18.2 3.6 %collective-permute-start.3 = (f32[8,128]{1,0:T(8,128)S(1)}, f32[8,128]{1,0:T(8,128)S(1)}, u32[]{:S(2)}, u32[]{:S(2)}) collective-permute-start(f32[8,128]{1,0:T(8,128)S(1)} %get-tuple-element.56.after_ref.refs_0_), channel_id=1, source_target_pairs={{0,8},{8,0},{16,24},{24,16},{1,9},{9,1},{17,25},{25,17},{2,10},{10... | collective-permute-start | bytes 12296 | tf_op jit(solution)/shard_map/ppermute | solution.py:76
  22.1 2.3 %collective-permute-start.6 = (bf16[2064,128]{1,0:T(8,128)(2,1)S(1)}, bf16[2064,128]{1,0:T(8,128)(2,1)S(1)}, u32[]{:S(2)}, u32[]{:S(2)}) collective-permute-start(bf16[2064,128]{1,0:T(8,128)(2,1)S(1)} %get-tuple-element.60.refs_2_.refs_1_.refs_0_), channel_id=1, source_target_pairs={{0,1},{1,0},{2,3},{3,2},{4,5},{5,4},{6,7},{7,6},{8,9},{9,8},{10,11... | collective-permute-start | bytes 1585160 | tf_op jit(solution)/shard_map/ppermute | solution.py:76
  26.8 11.7 %collective-permute-start.10 = (bf16[512,256]{1,0:T(8,128)(2,1)S(1)}, bf16[512,256]{1,0:T(8,128)(2,1)S(1)}, u32[]{:S(2)}, u32[]{:S(2)}) collective-permute-start(bf16[512,256]{1,0:T(8,128)(2,1)S(1)} %get-tuple-element.71), channel_id=1, source_target_pairs={{0,24},{8,16},{16,8},{24,0},{1,25},{9,17},{17,9},{25,1},{2,26},{10... | collective-permute-start | bytes 786440 | tf_op jit(solution)/shard_map/ppermute | solution.py:76
  28.5 14.1 %collective-permute-start.11 = (bf16[512,256]{1,0:T(8,128)(2,1)S(1)}, bf16[512,256]{1,0:T(8,128)(2,1)S(1)}, u32[]{:S(2)}, u32[]{:S(2)}) collective-permute-start(bf16[512,256]{1,0:T(8,128)(2,1)S(1)} %get-tuple-element.72), channel_id=1, source_target_pairs={{0,16},{8,24},{16,0},{24,8},{1,17},{9,25},{17,1},{25,9},{2,18},{10... | collective-permute-start | bytes 786440 | tf_op jit(solution)/shard_map/ppermute | solution.py:76
  29.0 13.6 %collective-permute-start.12 = (bf16[512,256]{1,0:T(8,128)(2,1)S(1)}, bf16[512,256]{1,0:T(8,128)(2,1)S(1)}, u32[]{:S(2)}, u32[]{:S(2)}) collective-permute-start(bf16[512,256]{1,0:T(8,128)(2,1)S(1)} %get-tuple-element.73), channel_id=1, source_target_pairs={{0,8},{8,0},{16,24},{24,16},{1,9},{9,1},{17,25},{25,17},{2,10},{10... | collective-permute-start | bytes 786440 | tf_op jit(solution)/shard_map/ppermute | solution.py:76
  30.3 7.2 %copy-start = (bf16[1,2048,256]{2,1,0:T(8,128)(2,1)S(1)}, bf16[1,2048,256]{2,1,0:T(8,128)(2,1)}, u32[]{:S(2)}) copy-start(bf16[1,2048,256]{2,1,0:T(8,128)(2,1)} %refs_0_.6) | copy-start | bytes 3145732
  30.3 9.5 %copy-start.8 = (s32[1,2]{1,0:T(1,128)S(1)}, s32[1,2]{1,0:T(1,128)}, u32[]{:S(2)}) copy-start(s32[1,2]{1,0:T(1,128)} %refs_0_.7) | copy-start | bytes 28
  35.3 12.9 %collective-permute-start.7 = (bf16[512,256]{1,0:T(8,128)(2,1)S(1)}, bf16[512,256]{1,0:T(8,128)(2,1)S(1)}, u32[]{:S(2)}, u32[]{:S(2)}) collective-permute-start(bf16[512,256]{1,0:T(8,128)(2,1)S(1)} %get-tuple-element.67), channel_id=1, source_target_pairs={{0,24},{8,16},{16,8},{24,0},{1,25},{9,17},{17,9},{25,1},{2,26},{10... | collective-permute-start | bytes 786440 | tf_op jit(solution)/shard_map/ppermute | solution.py:76
  37.0 16.3 %collective-permute-start.8 = (bf16[512,256]{1,0:T(8,128)(2,1)S(1)}, bf16[512,256]{1,0:T(8,128)(2,1)S(1)}, u32[]{:S(2)}, u32[]{:S(2)}) collective-permute-start(bf16[512,256]{1,0:T(8,128)(2,1)S(1)} %get-tuple-element.68), channel_id=1, source_target_pairs={{0,16},{8,24},{16,0},{24,8},{1,17},{9,25},{17,1},{25,9},{2,18},{10... | collective-permute-start | bytes 786440 | tf_op jit(solution)/shard_map/ppermute | solution.py:76
  38.5 15.0 %collective-permute-start.9 = (bf16[512,256]{1,0:T(8,128)(2,1)S(1)}, bf16[512,256]{1,0:T(8,128)(2,1)S(1)}, u32[]{:S(2)}, u32[]{:S(2)}) collective-permute-start(bf16[512,256]{1,0:T(8,128)(2,1)S(1)} %get-tuple-element.69), channel_id=1, source_target_pairs={{0,8},{8,0},{16,24},{24,16},{1,9},{9,1},{17,25},{25,17},{2,10},{10... | collective-permute-start | bytes 786440 | tf_op jit(solution)/shard_map/ppermute | solution.py:76
  43.0 14.5 %collective-permute-start.16 = (bf16[128,512]{1,0:T(8,128)(2,1)S(1)}, bf16[128,512]{1,0:T(8,128)(2,1)S(1)}, u32[]{:S(2)}, u32[]{:S(2)}) collective-permute-start(bf16[128,512]{1,0:T(8,128)(2,1)S(1)} %get-tuple-element.83), channel_id=1, source_target_pairs={{0,6},{1,7},{2,4},{3,5},{4,2},{5,3},{6,0},{7,1},{8,14},{9,15},{10,... | collective-permute-start | bytes 393224 | tf_op jit(solution)/shard_map/ppermute | solution.py:76
  46.7 11.6 %collective-permute-start.17 = (bf16[128,512]{1,0:T(8,128)(2,1)S(1)}, bf16[128,512]{1,0:T(8,128)(2,1)S(1)}, u32[]{:S(2)}, u32[]{:S(2)}) collective-permute-start(bf16[128,512]{1,0:T(8,128)(2,1)S(1)} %get-tuple-element.84), channel_id=1, source_target_pairs={{0,4},{1,5},{2,6},{3,7},{4,0},{5,1},{6,2},{7,3},{8,12},{9,13},{10,... | collective-permute-start | bytes 393224 | tf_op jit(solution)/shard_map/ppermute | solution.py:76
  48.2 10.2 %collective-permute-start.18 = (bf16[128,512]{1,0:T(8,128)(2,1)S(1)}, bf16[128,512]{1,0:T(8,128)(2,1)S(1)}, u32[]{:S(2)}, u32[]{:S(2)}) collective-permute-start(bf16[128,512]{1,0:T(8,128)(2,1)S(1)} %get-tuple-element.85), channel_id=1, source_target_pairs={{0,2},{1,3},{2,0},{3,1},{4,6},{5,7},{6,4},{7,5},{8,10},{9,11},{10,... | collective-permute-start | bytes 393224 | tf_op jit(solution)/shard_map/ppermute | solution.py:76
  53.9 8.3 %collective-permute-start.13 = (bf16[128,512]{1,0:T(8,128)(2,1)S(1)}, bf16[128,512]{1,0:T(8,128)(2,1)S(1)}, u32[]{:S(2)}, u32[]{:S(2)}) collective-permute-start(bf16[128,512]{1,0:T(8,128)(2,1)S(1)} %get-tuple-element.79), channel_id=1, source_target_pairs={{0,6},{1,7},{2,4},{3,5},{4,2},{5,3},{6,0},{7,1},{8,14},{9,15},{10,... | collective-permute-start | bytes 393224 | tf_op jit(solution)/shard_map/ppermute | solution.py:76
  57.6 11.4 %collective-permute-start.14 = (bf16[128,512]{1,0:T(8,128)(2,1)S(1)}, bf16[128,512]{1,0:T(8,128)(2,1)S(1)}, u32[]{:S(2)}, u32[]{:S(2)}) collective-permute-start(bf16[128,512]{1,0:T(8,128)(2,1)S(1)} %get-tuple-element.80), channel_id=1, source_target_pairs={{0,4},{1,5},{2,6},{3,7},{4,0},{5,1},{6,2},{7,3},{8,12},{9,13},{10,... | collective-permute-start | bytes 393224 | tf_op jit(solution)/shard_map/ppermute | solution.py:76
  57.6 11.4 %collective-permute-start.15 = (bf16[128,512]{1,0:T(8,128)(2,1)S(1)}, bf16[128,512]{1,0:T(8,128)(2,1)S(1)}, u32[]{:S(2)}, u32[]{:S(2)}) collective-permute-start(bf16[128,512]{1,0:T(8,128)(2,1)S(1)} %get-tuple-element.81), channel_id=1, source_target_pairs={{0,2},{1,3},{2,0},{3,1},{4,6},{5,7},{6,4},{7,5},{8,10},{9,11},{10,... | collective-permute-start | bytes 393224 | tf_op jit(solution)/shard_map/ppermute | solution.py:76
  58.4 10.7 %collective-permute-start.20 = (bf16[256,512]{1,0:T(8,128)(2,1)S(1)}, bf16[256,512]{1,0:T(8,128)(2,1)S(1)}, u32[]{:S(2)}, u32[]{:S(2)}) collective-permute-start(bf16[256,512]{1,0:T(8,128)(2,1)S(1)} %get-tuple-element.93), channel_id=1, source_target_pairs={{0,1},{1,0},{2,3},{3,2},{4,5},{5,4},{6,7},{7,6},{8,9},{9,8},{10,11... | collective-permute-start | bytes 786440 | tf_op jit(solution)/shard_map/ppermute | solution.py:76
  69.0 2.1 %collective-permute-start.19 = (bf16[256,512]{1,0:T(8,128)(2,1)S(1)}, bf16[256,512]{1,0:T(8,128)(2,1)S(1)}, u32[]{:S(2)}, u32[]{:S(2)}) collective-permute-start(bf16[256,512]{1,0:T(8,128)(2,1)S(1)} %get-tuple-element.91), channel_id=1, source_target_pairs={{0,1},{1,0},{2,3},{3,2},{4,5},{5,4},{6,7},{7,6},{8,9},{9,8},{10,11... | collective-permute-start | bytes 786440 | tf_op jit(solution)/shard_map/ppermute | solution.py:76
  (6 other events, 5.0 us)

commit v5 on v4

--- a/solution.py
+++ b/solution.py
@@ -40,30 +40,40 @@
         self.last = []
 
     def call(
-        self, kernel, out_shape, in_specs, scratch=(), aliases=None, out_specs=None, cost=1024
+        self,
+        kernel,
+        out_shape,
+        in_specs,
+        scratch=(),
+        aliases=None,
+        out_specs=None,
+        cost=1024,
+        final=False,
     ):
         given, made, linked = len(in_specs), len(out_shape), len(self.last)
+        marks = [] if final else [shape((8, LANES), F32)]
 
         def run(*refs):
             outs = refs[given + linked :]
-            outs[made][...] = jnp.zeros(outs[made].shape, F32)
-            kernel(*refs[:given], *outs[:made], *outs[made + 1 :])
+            for mark in outs[made : made + len(marks)]:
+                mark[...] = jnp.zeros(mark.shape, F32)
+            kernel(*refs[:given], *outs[:made], *outs[made + len(marks) :])
 
         out_specs = [VMEM] * made if out_specs is None else out_specs
         run_call = call(
             run,
-            [*out_shape, shape((8, LANES), F32)],
+            [*out_shape, *marks],
             [*in_specs, *[VMEM] * linked],
             scratch,
             aliases,
-            [*out_specs, VMEM],
+            [*out_specs, *[VMEM] * len(marks)],
             cost=cost,
         )
 
         def apply(*args):
-            *results, token = run_call(*args, *self.last)
-            self.last = [token]
-            return results
+            results = run_call(*args, *self.last)
+            self.last = list(results[made:])
+            return list(results[:made])
 
         return apply
 
@@ -137,8 +147,8 @@
     for at in range(0, width, LANES):
         cut = slice(at, at + LANES)
         gaint_ref[cut, :] = to_column(gain_ref[:, cut])
-        projt_ref[cut, :] = jnp.transpose(proj_ref[0, :, cut].astype(F32), (1, 0))
-        residt_ref[cut, :] = jnp.transpose(resid_ref[0, :, cut].astype(F32), (1, 0))
+        projt_ref[cut, :] = jnp.transpose(proj_ref[0, :, cut], (1, 0)).astype(F32)
+        residt_ref[cut, :] = jnp.transpose(resid_ref[0, :, cut], (1, 0)).astype(F32)
     head.wait()
     start, count = span[0, 0], span[0, 1]
     places = lax.broadcasted_iota(jnp.int32, (hidden_ref.shape[1], 1), 0)
@@ -523,9 +533,12 @@
             [pltpu.VMEM((rows, slots), BF16), dma((1,))],
             {2: 0} if held else None,
             [HBM],
+            final=index == len(chunks) - 1 and turn == share - 1,
         )(parts[turn], slopes, *held)
 
     waiting = [down(0), down(1)]
+    placed = [place(parts) for parts in waiting]
+    first = group(placed[0])
     (slopes,) = chain.call(
         functools.partial(slope_kernel, 4),
         [shape(pre_owned.shape[1:], F32)],
@@ -537,10 +550,7 @@
         [shape(ques_hidden.shape, BF16)],
         [HBM, VMEM, HBM],
         [pltpu.SMEM((1, 2), jnp.int32), pltpu.VMEM((tokens, width), BF16), dma((2,))],
-        cost=400000000,
     )(ques_span, logit, vis_proj)
-    placed = [place(parts) for parts in waiting]
-    first = group(placed[0])
     held = finish(first, 0, 0, [])
     second = group(placed[1])
     for turn in range(1, share):

time: 73.1 us -> 72 us (0.985)
  Pallas kernels: 24.4 us -> 23.2 us
where the time goes in v5:
time: 72 us; the launch traced here: 71.6 us
  starting transfers between devices  25.2 us (35%)
  Pallas kernels  23.2 us (32%)
  waiting for transfers between devices  17.3 us (24%)
  local copies, waits for them, and re-layouts  5 us (7%)
  between operations  0.9 us (1%)
    ppermute x21, starting transfers between devices, swap(): return lax.ppermute(value, axis, [(i, i ^ step) for i in range(count)])  25.2 us
    ppermute x21, waiting for transfers between devices, swap(): return lax.ppermute(value, axis, [(i, i ^ step) for i in range(count)])  17.3 us
    pallas_call x14, Pallas kernels, apply(): results = run_call(*args, *self.last)  17 us
    unnamed x18, local copies, waits for them, and re-layouts  5 us
    pallas_call x1, Pallas kernels, preload(): caller(functools.partial(preload_kernel, half * count, count, peers, shar...  2.2 us
    pallas_call x1, Pallas kernels, body(): call(load_kernel, [row, tall, tall, tall, tall, shape(w_value.shape, BF16...  1.61 us
    pallas_call x1, Pallas kernels, body(): call(functools.partial(pick_kernel, pieces), shape((tokens, key_width), B...  1.48 us
  transfers between devices with their start and end apart: 21, of which 8 were waited for; matrix products, arithmetic and copies ran while one was open for 0% of the time, Pallas kernels for 24%

profile of v5, /device:TPU:0, one launch (start us, length us, event | category | flops | bytes accessed | tf_op | source)
XLA Modules:
  0.0 71.6 jit_solution(3512495741364828165)
XLA Ops:
  1.3 1.5 %shard_map.122.refs_0_ = bf16[128,512]{1,0:T(8,128)(2,1)S(1)} custom-call(s32[1,128]{1,0:T(1,128)S(1)} %copy-done.7, bf16[1,1024,512]{2,1,0:T(8,128)(2,1)} %rows_hbm.1), custom_call_target="tpu_custom_call" | custom-call | flops 262144 | bytes 1024 | tf_op jit(solution)/shard_map/pallas_call | solution.py:431
  2.8 4.0 %collective-permute-start.2 = (bf16[128,512]{1,0:T(8,128)(2,1)S(1)}, bf16[128,512]{1,0:T(8,128)(2,1)S(1)}, u32[]{:S(2)}, u32[]{:S(2)}) collective-permute-start(bf16[128,512]{1,0:T(8,128)(2,1)S(1)} %shard_map.122.refs_0_), channel_id=1, source_target_pairs={{0,24},{8,16},{16,8},{24,0},{1,25},{9,17},{17,9},{25,1},{2,26},{10... | collective-permute-start | bytes 393224 | tf_op jit(solution)/shard_map/ppermute | solution.py:86
  7.4 1.0 %copy-done = bf16[1,128,2048]{2,1,0:T(8,128)(2,1)S(1)} copy-done((bf16[1,128,2048]{2,1,0:T(8,128)(2,1)S(1)}, bf16[1,128,2048]{2,1,0:T(8,128)(2,1)}, u32[]{:S(2)}) %copy-start) | copy-done | bytes 524312
  8.4 1.0 %copy-done.2 = bf16[1,128,2048]{2,1,0:T(8,128)(2,1)S(1)} copy-done((bf16[1,128,2048]{2,1,0:T(8,128)(2,1)S(1)}, bf16[1,128,2048]{2,1,0:T(8,128)(2,1)}, u32[]{:S(2)}) %copy-start.2) | copy-done | bytes 524312
  11.7 1.6 %shard_map.123 = (f32[8,128]{1,0:T(8,128)S(1)}, f32[2048,128]{1,0:T(8,128)S(1)}, f32[2048,128]{1,0:T(8,128)S(1)}, f32[2048,128]{1,0:T(8,128)S(1)}, f32[2048,128]...) custom-call(s32[1,2]{1,0:T(1,128)S(1)} %copy-done.5, bf16[1,32,2048]{2,1,0:T(8,128)(2,1)S(1)} %copy-done.3, ...), custom_call_target="tpu_custom_call" | custom-call | flops 262144 | bytes 1024 | tf_op jit(solution)/shard_map/pallas_call | solution.py:444
  14.2 2.9 %collective-permute-start.5 = (f32[8,128]{1,0:T(8,128)S(1)}, f32[8,128]{1,0:T(8,128)S(1)}, u32[]{:S(2)}, u32[]{:S(2)}) collective-permute-start(f32[8,128]{1,0:T(8,128)S(1)} %get-tuple-element.55.after_ref.refs_0_), channel_id=1, source_target_pairs={{0,24},{8,16},{16,8},{24,0},{1,25},{9,17},{17,9},{25,1},{2,26},{10... | collective-permute-start | bytes 12296 | tf_op jit(solution)/shard_map/ppermute | solution.py:86
  17.8 2.2 %shard_map.125.refs_9_.refs_0_ = bf16[1024,2048]{1,0:T(8,128)(2,1)S(1)} custom-call(bf16[8192,2048]{1,0:T(8,128)(2,1)} %refs_0_.5, f32[8,128]{1,0:T(8,128)S(1)} %get-tuple-element.55.after_ref.refs_0_), custom_call_target="tpu_custom_call" | custom-call | flops 262144 | bytes 1024 | tf_op jit(solution)/shard_map/pallas_call | solution.py:472
  21.6 2.2 %shard_map.127 = (bf16[1024,2048]{1,0:T(8,128)(2,1)S(1)}, f32[8,128]{1,0:T(8,128)S(1)}) custom-call(bf16[8192,2048]{1,0:T(8,128)(2,1)} %refs_0_.5, f32[8,128]{1,0:T(8,128)S(1)} %get-tuple-element.60.refs_1_, f32[8,128]{1,0:T(8,128)S(1)} %get-tuple-element.61.refs_2_), custom_call_target="tpu_custom_call" | custom-call | flops 262144 | bytes 1024 | tf_op jit(solution)/shard_map/pallas_call | solution.py:74
  23.9 2.4 %shard_map.128 = (bf16[512,256]{1,0:T(8,128)(2,1)S(1)}, bf16[512,256]{1,0:T(8,128)(2,1)S(1)}, bf16[512,256]{1,0:T(8,128)(2,1)S(1)}, bf16[512,256]{1,0:T(8,128)(2,1)S(1)}, f32[8,128]{1,0:T(8,128)S(1)}) custom-call(bf16[1024,2048]{1,0:T(8,128)(2,1)S(1)} %shard_map.125.refs_9_.refs_0_, bf16[1024,2048]{1,0:T(8,128)(2,1)S(1)} %get-tuple-element.62.refs_1_, ...), custom_call_target="tpu_custom_call" | custom-call | flops 2147483648 | bytes 8388608 | tf_op jit(solution)/shard_map/pallas_call | solution.py:74
  26.3 1.7 %collective-permute-start.10 = (bf16[512,256]{1,0:T(8,128)(2,1)S(1)}, bf16[512,256]{1,0:T(8,128)(2,1)S(1)}, u32[]{:S(2)}, u32[]{:S(2)}) collective-permute-start(bf16[512,256]{1,0:T(8,128)(2,1)S(1)} %get-tuple-element.70), channel_id=1, source_target_pairs={{0,24},{8,16},{16,8},{24,0},{1,25},{9,17},{17,9},{25,1},{2,26},{10... | collective-permute-start | bytes 786440 | tf_op jit(solution)/shard_map/ppermute | solution.py:86
  28.5 1.4 %collective-permute-start.12 = (bf16[512,256]{1,0:T(8,128)(2,1)S(1)}, bf16[512,256]{1,0:T(8,128)(2,1)S(1)}, u32[]{:S(2)}, u32[]{:S(2)}) collective-permute-start(bf16[512,256]{1,0:T(8,128)(2,1)S(1)} %get-tuple-element.72), channel_id=1, source_target_pairs={{0,8},{8,0},{16,24},{24,16},{1,9},{9,1},{17,25},{25,17},{2,10},{10... | collective-permute-start | bytes 786440 | tf_op jit(solution)/shard_map/ppermute | solution.py:86
  29.8 4.9 %shard_map.129 = (bf16[512,256]{1,0:T(8,128)(2,1)S(1)}, bf16[512,256]{1,0:T(8,128)(2,1)S(1)}, bf16[512,256]{1,0:T(8,128)(2,1)S(1)}, bf16[512,256]{1,0:T(8,128)(2,1)S(1)}, f32[8,128]{1,0:T(8,128)S(1)}) custom-call(bf16[8192,2048]{1,0:T(8,128)(2,1)} %refs_0_.5, bf16[2064,128]{1,0:T(8,128)(2,1)S(1)} %get-tuple-element.59.refs_2_.refs_1_.refs_0_, ...), custom_call_target="tpu_custom_call" | custom-call | flops 2147483648 | bytes 8388608 | tf_op jit(solution)/shard_map/pallas_call | solution.py:74
  34.7 1.7 %collective-permute-start.7 = (bf16[512,256]{1,0:T(8,128)(2,1)S(1)}, bf16[512,256]{1,0:T(8,128)(2,1)S(1)}, u32[]{:S(2)}, u32[]{:S(2)}) collective-permute-start(bf16[512,256]{1,0:T(8,128)(2,1)S(1)} %get-tuple-element.66), channel_id=1, source_target_pairs={{0,24},{8,16},{16,8},{24,0},{1,25},{9,17},{17,9},{25,1},{2,26},{10... | collective-permute-start | bytes 786440 | tf_op jit(solution)/shard_map/ppermute | solution.py:86
  36.9 1.4 %collective-permute-start.9 = (bf16[512,256]{1,0:T(8,128)(2,1)S(1)}, bf16[512,256]{1,0:T(8,128)(2,1)S(1)}, u32[]{:S(2)}, u32[]{:S(2)}) collective-permute-start(bf16[512,256]{1,0:T(8,128)(2,1)S(1)} %get-tuple-element.68), channel_id=1, source_target_pairs={{0,8},{8,0},{16,24},{24,16},{1,9},{9,1},{17,25},{25,17},{2,10},{10... | collective-permute-start | bytes 786440 | tf_op jit(solution)/shard_map/ppermute | solution.py:86
  38.3 3.8 %collective-permute-done.11.refs_4_ = bf16[512,256]{1,0:T(8,128)(2,1)S(1)} collective-permute-done((bf16[512,256]{1,0:T(8,128)(2,1)S(1)}, bf16[512,256]{1,0:T(8,128)(2,1)S(1)}, u32[]{:S(2)}, u32[]{:S(2)}) %collective-permute-start.11) | collective-permute-done | bytes 262176 | tf_op jit(solution)/shard_map/ppermute | solution.py:86
  42.5 3.7 %collective-permute-start.16 = (bf16[128,512]{1,0:T(8,128)(2,1)S(1)}, bf16[128,512]{1,0:T(8,128)(2,1)S(1)}, u32[]{:S(2)}, u32[]{:S(2)}) collective-permute-start(bf16[128,512]{1,0:T(8,128)(2,1)S(1)} %get-tuple-element.80), channel_id=1, source_target_pairs={{0,6},{1,7},{2,4},{3,5},{4,2},{5,3},{6,0},{7,1},{8,14},{9,15},{10,... | collective-permute-start | bytes 393224 | tf_op jit(solution)/shard_map/ppermute | solution.py:86
  46.2 1.5 %collective-permute-done.7.refs_3_ = bf16[512,256]{1,0:T(8,128)(2,1)S(1)} collective-permute-done((bf16[512,256]{1,0:T(8,128)(2,1)S(1)}, bf16[512,256]{1,0:T(8,128)(2,1)S(1)}, u32[]{:S(2)}, u32[]{:S(2)}) %collective-permute-start.7) | collective-permute-done | bytes 262176 | tf_op jit(solution)/shard_map/ppermute | solution.py:86
  47.7 1.6 %collective-permute-start.18 = (bf16[128,512]{1,0:T(8,128)(2,1)S(1)}, bf16[128,512]{1,0:T(8,128)(2,1)S(1)}, u32[]{:S(2)}, u32[]{:S(2)}) collective-permute-start(bf16[128,512]{1,0:T(8,128)(2,1)S(1)} %get-tuple-element.82), channel_id=1, source_target_pairs={{0,2},{1,3},{2,0},{3,1},{4,6},{5,7},{6,4},{7,5},{8,10},{9,11},{10,... | collective-permute-start | bytes 393224 | tf_op jit(solution)/shard_map/ppermute | solution.py:86
  49.3 3.5 %collective-permute-done.8.refs_4_ = bf16[512,256]{1,0:T(8,128)(2,1)S(1)} collective-permute-done((bf16[512,256]{1,0:T(8,128)(2,1)S(1)}, bf16[512,256]{1,0:T(8,128)(2,1)S(1)}, u32[]{:S(2)}, u32[]{:S(2)}) %collective-permute-start.8) | collective-permute-done | bytes 262176 | tf_op jit(solution)/shard_map/ppermute | solution.py:86
  53.4 3.7 %collective-permute-start.13 = (bf16[128,512]{1,0:T(8,128)(2,1)S(1)}, bf16[128,512]{1,0:T(8,128)(2,1)S(1)}, u32[]{:S(2)}, u32[]{:S(2)}) collective-permute-start(bf16[128,512]{1,0:T(8,128)(2,1)S(1)} %get-tuple-element.76), channel_id=1, source_target_pairs={{0,6},{1,7},{2,4},{3,5},{4,2},{5,3},{6,0},{7,1},{8,14},{9,15},{10,... | collective-permute-start | bytes 393224 | tf_op jit(solution)/shard_map/ppermute | solution.py:86
  58.9 1.5 %shard_map.134 = (bf16[1,32,2048]{2,1,0:T(8,128)(2,1)}, f32[8,128]{1,0:T(8,128)S(1)}) custom-call(s32[1,2]{1,0:T(1,128)S(1)} %copy-done.6, f32[8,128]{1,0:T(8,128)S(1)} %get-tuple-element.60.refs_1_, bf16[1,128,2048]{2,1,0:T(8,128)(2,1)S(1)} %copy-done, f32[8,128]{1,0:T(8,128)S(1)} %get-tuple-element.87.refs_3_), custom_call_target="tpu_custom_call" | custom-call | flops 262144 | bytes 1024 | tf_op jit(solution)/shard_map/pallas_call | solution.py:74
  61.7 6.8 %collective-permute-done.14.refs_2_ = bf16[128,512]{1,0:T(8,128)(2,1)S(1)} collective-permute-done((bf16[128,512]{1,0:T(8,128)(2,1)S(1)}, bf16[128,512]{1,0:T(8,128)(2,1)S(1)}, u32[]{:S(2)}, u32[]{:S(2)}) %collective-permute-start.14) | collective-permute-done | bytes 131104 | tf_op jit(solution)/shard_map/ppermute | solution.py:86
  68.6 1.0 %shard_map.137 = (bf16[1,2048,256]{2,1,0:T(8,128)(2,1)}, f32[8,128]{1,0:T(8,128)S(1)}) custom-call(bf16[256,512]{1,0:T(8,128)(2,1)S(1)} %collective-permute-done.20.refs_0_, f32[2048,256]{1,0:T(8,128)S(1)} %get-tuple-element.86.refs_1_, bf16[1,2048,256]{2,1,0:T(8,128)(2,1)} %get-tuple-element.93.refs_2_, ...), custom_call_target="tpu_custom_call", output_to_operand_aliasing={{0}: (2, {})} | custom-call | flops 262144 | bytes 1024 | tf_op jit(solution)/shard_map/pallas_call | solution.py:74
  69.6 1.0 %shard_map.138 = (bf16[1,2048,256]{2,1,0:T(8,128)(2,1)}, f32[8,128]{1,0:T(8,128)S(1)}) custom-call(bf16[256,512]{1,0:T(8,128)(2,1)S(1)} %get-tuple-element.91.refs_0_, f32[2048,256]{1,0:T(8,128)S(1)} %get-tuple-element.86.refs_1_, bf16[1,2048,256]{2,1,0:T(8,128)(2,1)} %get-tuple-element.95.refs_2_, ...), custom_call_target="tpu_custom_call", output_to_operand_aliasing={{0}: (2, {})} | custom-call | flops 262144 | bytes 1024 | tf_op jit(solution)/shard_map/pallas_call | solution.py:74
  (54 shorter events, 12.9 us)
Async XLA Ops:
  2.8 10.6 %collective-permute-start.2 = (bf16[128,512]{1,0:T(8,128)(2,1)S(1)}, bf16[128,512]{1,0:T(8,128)(2,1)S(1)}, u32[]{:S(2)}, u32[]{:S(2)}) collective-permute-start(bf16[128,512]{1,0:T(8,128)(2,1)S(1)} %shard_map.122.refs_0_), channel_id=1, source_target_pairs={{0,24},{8,16},{16,8},{24,0},{1,25},{9,17},{17,9},{25,1},{2,26},{10... | collective-permute-start | bytes 393224 | tf_op jit(solution)/shard_map/ppermute | solution.py:86
  6.7 6.6 %collective-permute-start.1 = (bf16[128,512]{1,0:T(8,128)(2,1)S(1)}, bf16[128,512]{1,0:T(8,128)(2,1)S(1)}, u32[]{:S(2)}, u32[]{:S(2)}) collective-permute-start(bf16[128,512]{1,0:T(8,128)(2,1)S(1)} %shard_map.122.refs_0_), channel_id=1, source_target_pairs={{0,16},{8,24},{16,0},{24,8},{1,17},{9,25},{17,1},{25,9},{2,18},{10... | collective-permute-start | bytes 393224 | tf_op jit(solution)/shard_map/ppermute | solution.py:86
  7.2 6.1 %collective-permute-start = (bf16[128,512]{1,0:T(8,128)(2,1)S(1)}, bf16[128,512]{1,0:T(8,128)(2,1)S(1)}, u32[]{:S(2)}, u32[]{:S(2)}) collective-permute-start(bf16[128,512]{1,0:T(8,128)(2,1)S(1)} %shard_map.122.refs_0_), channel_id=1, source_target_pairs={{0,8},{8,0},{16,24},{24,16},{1,9},{9,1},{17,25},{25,17},{2,10},{10... | collective-permute-start | bytes 393224 | tf_op jit(solution)/shard_map/ppermute | solution.py:86
  14.2 7.0 %copy-start.8 = (s32[1,128,1]{1,2,0:T(1,128)S(1)}, s32[1,128,1]{1,2,0:T(1,128)}, u32[]{:S(2)}) copy-start(s32[1,128,1]{1,2,0:T(1,128)} %param.15) | copy-start | bytes 1540
  14.2 5.8 %collective-permute-start.5 = (f32[8,128]{1,0:T(8,128)S(1)}, f32[8,128]{1,0:T(8,128)S(1)}, u32[]{:S(2)}, u32[]{:S(2)}) collective-permute-start(f32[8,128]{1,0:T(8,128)S(1)} %get-tuple-element.55.after_ref.refs_0_), channel_id=1, source_target_pairs={{0,24},{8,16},{16,8},{24,0},{1,25},{9,17},{17,9},{25,1},{2,26},{10... | collective-permute-start | bytes 12296 | tf_op jit(solution)/shard_map/ppermute | solution.py:86
  17.2 3.6 %collective-permute-start.4 = (f32[8,128]{1,0:T(8,128)S(1)}, f32[8,128]{1,0:T(8,128)S(1)}, u32[]{:S(2)}, u32[]{:S(2)}) collective-permute-start(f32[8,128]{1,0:T(8,128)S(1)} %get-tuple-element.55.after_ref.refs_0_), channel_id=1, source_target_pairs={{0,16},{8,24},{16,0},{24,8},{1,17},{9,25},{17,1},{25,9},{2,18},{10... | collective-permute-start | bytes 12296 | tf_op jit(solution)/shard_map/ppermute | solution.py:86
  17.7 3.6 %collective-permute-start.3 = (f32[8,128]{1,0:T(8,128)S(1)}, f32[8,128]{1,0:T(8,128)S(1)}, u32[]{:S(2)}, u32[]{:S(2)}) collective-permute-start(f32[8,128]{1,0:T(8,128)S(1)} %get-tuple-element.55.after_ref.refs_0_), channel_id=1, source_target_pairs={{0,8},{8,0},{16,24},{24,16},{1,9},{9,1},{17,25},{25,17},{2,10},{10... | collective-permute-start | bytes 12296 | tf_op jit(solution)/shard_map/ppermute | solution.py:86
  21.6 2.3 %collective-permute-start.6 = (bf16[2064,128]{1,0:T(8,128)(2,1)S(1)}, bf16[2064,128]{1,0:T(8,128)(2,1)S(1)}, u32[]{:S(2)}, u32[]{:S(2)}) collective-permute-start(bf16[2064,128]{1,0:T(8,128)(2,1)S(1)} %get-tuple-element.59.refs_2_.refs_1_.refs_0_), channel_id=1, source_target_pairs={{0,1},{1,0},{2,3},{3,2},{4,5},{5,4},{6,7},{7,6},{8,9},{9,8},{10,11... | collective-permute-start | bytes 1585160 | tf_op jit(solution)/shard_map/ppermute | solution.py:86
  26.3 10.6 %collective-permute-start.10 = (bf16[512,256]{1,0:T(8,128)(2,1)S(1)}, bf16[512,256]{1,0:T(8,128)(2,1)S(1)}, u32[]{:S(2)}, u32[]{:S(2)}) collective-permute-start(bf16[512,256]{1,0:T(8,128)(2,1)S(1)} %get-tuple-element.70), channel_id=1, source_target_pairs={{0,24},{8,16},{16,8},{24,0},{1,25},{9,17},{17,9},{25,1},{2,26},{10... | collective-permute-start | bytes 786440 | tf_op jit(solution)/shard_map/ppermute | solution.py:86
  28.0 14.1 %collective-permute-start.11 = (bf16[512,256]{1,0:T(8,128)(2,1)S(1)}, bf16[512,256]{1,0:T(8,128)(2,1)S(1)}, u32[]{:S(2)}, u32[]{:S(2)}) collective-permute-start(bf16[512,256]{1,0:T(8,128)(2,1)S(1)} %get-tuple-element.71), channel_id=1, source_target_pairs={{0,16},{8,24},{16,0},{24,8},{1,17},{9,25},{17,1},{25,9},{2,18},{10... | collective-permute-start | bytes 786440 | tf_op jit(solution)/shard_map/ppermute | solution.py:86
  28.5 13.6 %collective-permute-start.12 = (bf16[512,256]{1,0:T(8,128)(2,1)S(1)}, bf16[512,256]{1,0:T(8,128)(2,1)S(1)}, u32[]{:S(2)}, u32[]{:S(2)}) collective-permute-start(bf16[512,256]{1,0:T(8,128)(2,1)S(1)} %get-tuple-element.72), channel_id=1, source_target_pairs={{0,8},{8,0},{16,24},{24,16},{1,9},{9,1},{17,25},{25,17},{2,10},{10... | collective-permute-start | bytes 786440 | tf_op jit(solution)/shard_map/ppermute | solution.py:86
  34.7 23.3 %copy-start.1 = (bf16[1,2048,256]{2,1,0:T(8,128)(2,1)S(1)}, bf16[1,2048,256]{2,1,0:T(8,128)(2,1)}, u32[]{:S(2)}) copy-start(bf16[1,2048,256]{2,1,0:T(8,128)(2,1)} %refs_0_.6) | copy-start | bytes 3145732
  34.7 24.2 %copy-start.6 = (s32[1,2]{1,0:T(1,128)S(1)}, s32[1,2]{1,0:T(1,128)}, u32[]{:S(2)}) copy-start(s32[1,2]{1,0:T(1,128)} %refs_0_.7) | copy-start | bytes 28
  34.7 13.0 %collective-permute-start.7 = (bf16[512,256]{1,0:T(8,128)(2,1)S(1)}, bf16[512,256]{1,0:T(8,128)(2,1)S(1)}, u32[]{:S(2)}, u32[]{:S(2)}) collective-permute-start(bf16[512,256]{1,0:T(8,128)(2,1)S(1)} %get-tuple-element.66), channel_id=1, source_target_pairs={{0,24},{8,16},{16,8},{24,0},{1,25},{9,17},{17,9},{25,1},{2,26},{10... | collective-permute-start | bytes 786440 | tf_op jit(solution)/shard_map/ppermute | solution.py:86
  36.4 16.4 %collective-permute-start.8 = (bf16[512,256]{1,0:T(8,128)(2,1)S(1)}, bf16[512,256]{1,0:T(8,128)(2,1)S(1)}, u32[]{:S(2)}, u32[]{:S(2)}) collective-permute-start(bf16[512,256]{1,0:T(8,128)(2,1)S(1)} %get-tuple-element.67), channel_id=1, source_target_pairs={{0,16},{8,24},{16,0},{24,8},{1,17},{9,25},{17,1},{25,9},{2,18},{10... | collective-permute-start | bytes 786440 | tf_op jit(solution)/shard_map/ppermute | solution.py:86
  36.9 16.0 %collective-permute-start.9 = (bf16[512,256]{1,0:T(8,128)(2,1)S(1)}, bf16[512,256]{1,0:T(8,128)(2,1)S(1)}, u32[]{:S(2)}, u32[]{:S(2)}) collective-permute-start(bf16[512,256]{1,0:T(8,128)(2,1)S(1)} %get-tuple-element.68), channel_id=1, source_target_pairs={{0,8},{8,0},{16,24},{24,16},{1,9},{9,1},{17,25},{25,17},{2,10},{10... | collective-permute-start | bytes 786440 | tf_op jit(solution)/shard_map/ppermute | solution.py:86
  42.5 14.5 %collective-permute-start.16 = (bf16[128,512]{1,0:T(8,128)(2,1)S(1)}, bf16[128,512]{1,0:T(8,128)(2,1)S(1)}, u32[]{:S(2)}, u32[]{:S(2)}) collective-permute-start(bf16[128,512]{1,0:T(8,128)(2,1)S(1)} %get-tuple-element.80), channel_id=1, source_target_pairs={{0,6},{1,7},{2,4},{3,5},{4,2},{5,3},{6,0},{7,1},{8,14},{9,15},{10,... | collective-permute-start | bytes 393224 | tf_op jit(solution)/shard_map/ppermute | solution.py:86
  46.2 11.6 %collective-permute-start.17 = (bf16[128,512]{1,0:T(8,128)(2,1)S(1)}, bf16[128,512]{1,0:T(8,128)(2,1)S(1)}, u32[]{:S(2)}, u32[]{:S(2)}) collective-permute-start(bf16[128,512]{1,0:T(8,128)(2,1)S(1)} %get-tuple-element.81), channel_id=1, source_target_pairs={{0,4},{1,5},{2,6},{3,7},{4,0},{5,1},{6,2},{7,3},{8,12},{9,13},{10,... | collective-permute-start | bytes 393224 | tf_op jit(solution)/shard_map/ppermute | solution.py:86
  47.7 10.2 %collective-permute-start.18 = (bf16[128,512]{1,0:T(8,128)(2,1)S(1)}, bf16[128,512]{1,0:T(8,128)(2,1)S(1)}, u32[]{:S(2)}, u32[]{:S(2)}) collective-permute-start(bf16[128,512]{1,0:T(8,128)(2,1)S(1)} %get-tuple-element.82), channel_id=1, source_target_pairs={{0,2},{1,3},{2,0},{3,1},{4,6},{5,7},{6,4},{7,5},{8,10},{9,11},{10,... | collective-permute-start | bytes 393224 | tf_op jit(solution)/shard_map/ppermute | solution.py:86
  53.4 8.3 %collective-permute-start.13 = (bf16[128,512]{1,0:T(8,128)(2,1)S(1)}, bf16[128,512]{1,0:T(8,128)(2,1)S(1)}, u32[]{:S(2)}, u32[]{:S(2)}) collective-permute-start(bf16[128,512]{1,0:T(8,128)(2,1)S(1)} %get-tuple-element.76), channel_id=1, source_target_pairs={{0,6},{1,7},{2,4},{3,5},{4,2},{5,3},{6,0},{7,1},{8,14},{9,15},{10,... | collective-permute-start | bytes 393224 | tf_op jit(solution)/shard_map/ppermute | solution.py:86
  57.0 11.4 %collective-permute-start.14 = (bf16[128,512]{1,0:T(8,128)(2,1)S(1)}, bf16[128,512]{1,0:T(8,128)(2,1)S(1)}, u32[]{:S(2)}, u32[]{:S(2)}) collective-permute-start(bf16[128,512]{1,0:T(8,128)(2,1)S(1)} %get-tuple-element.77), channel_id=1, source_target_pairs={{0,4},{1,5},{2,6},{3,7},{4,0},{5,1},{6,2},{7,3},{8,12},{9,13},{10,... | collective-permute-start | bytes 393224 | tf_op jit(solution)/shard_map/ppermute | solution.py:86
  57.0 11.4 %collective-permute-start.15 = (bf16[128,512]{1,0:T(8,128)(2,1)S(1)}, bf16[128,512]{1,0:T(8,128)(2,1)S(1)}, u32[]{:S(2)}, u32[]{:S(2)}) collective-permute-start(bf16[128,512]{1,0:T(8,128)(2,1)S(1)} %get-tuple-element.78), channel_id=1, source_target_pairs={{0,2},{1,3},{2,0},{3,1},{4,6},{5,7},{6,4},{7,5},{8,10},{9,11},{10,... | collective-permute-start | bytes 393224 | tf_op jit(solution)/shard_map/ppermute | solution.py:86
  57.9 10.7 %collective-permute-start.20 = (bf16[256,512]{1,0:T(8,128)(2,1)S(1)}, bf16[256,512]{1,0:T(8,128)(2,1)S(1)}, u32[]{:S(2)}, u32[]{:S(2)}) collective-permute-start(bf16[256,512]{1,0:T(8,128)(2,1)S(1)} %get-tuple-element.92), channel_id=1, source_target_pairs={{0,1},{1,0},{2,3},{3,2},{4,5},{5,4},{6,7},{7,6},{8,9},{9,8},{10,11... | collective-permute-start | bytes 786440 | tf_op jit(solution)/shard_map/ppermute | solution.py:86
  68.5 2.1 %collective-permute-start.19 = (bf16[256,512]{1,0:T(8,128)(2,1)S(1)}, bf16[256,512]{1,0:T(8,128)(2,1)S(1)}, u32[]{:S(2)}, u32[]{:S(2)}) collective-permute-start(bf16[256,512]{1,0:T(8,128)(2,1)S(1)} %get-tuple-element.90), channel_id=1, source_target_pairs={{0,1},{1,0},{2,3},{3,2},{4,5},{5,4},{6,7},{7,6},{8,9},{9,8},{10,11... | collective-permute-start | bytes 786440 | tf_op jit(solution)/shard_map/ppermute | solution.py:86
  (6 other events, 5.0 us)

commit v6 on v5

--- a/solution.py
+++ b/solution.py
@@ -536,9 +536,7 @@
             final=index == len(chunks) - 1 and turn == share - 1,
         )(parts[turn], slopes, *held)
 
-    waiting = [down(0), down(1)]
-    placed = [place(parts) for parts in waiting]
-    first = group(placed[0])
+    waiting = [down(0)]
     (slopes,) = chain.call(
         functools.partial(slope_kernel, 4),
         [shape(pre_owned.shape[1:], F32)],
@@ -551,6 +549,9 @@
         [HBM, VMEM, HBM],
         [pltpu.SMEM((1, 2), jnp.int32), pltpu.VMEM((tokens, width), BF16), dma((2,))],
     )(ques_span, logit, vis_proj)
+    waiting.append(down(1))
+    placed = [place(parts) for parts in waiting]
+    first = group(placed[0])
     held = finish(first, 0, 0, [])
     second = group(placed[1])
     for turn in range(1, share):

time: 72 us -> 72 us (level)
  no operation moved by 1% of the time
where the time goes in v6:
time: 72 us; the launch traced here: 71.6 us
  starting transfers between devices  25.2 us (35%)
  Pallas kernels  23.2 us (32%)
  waiting for transfers between devices  17.3 us (24%)
  local copies, waits for them, and re-layouts  5 us (7%)
  between operations  0.89 us (1%)
    ppermute x21, starting transfers between devices, swap(): return lax.ppermute(value, axis, [(i, i ^ step) for i in range(count)])  25.2 us
    ppermute x21, waiting for transfers between devices, swap(): return lax.ppermute(value, axis, [(i, i ^ step) for i in range(count)])  17.3 us
    pallas_call x14, Pallas kernels, apply(): results = run_call(*args, *self.last)  17.1 us
    unnamed x18, local copies, waits for them, and re-layouts  5 us
    pallas_call x1, Pallas kernels, preload(): caller(functools.partial(preload_kernel, half * count, count, peers, shar...  2.2 us
    pallas_call x1, Pallas kernels, body(): call(load_kernel, [row, tall, tall, tall, tall, shape(w_value.shape, BF16...  1.61 us
    pallas_call x1, Pallas kernels, body(): call(functools.partial(pick_kernel, pieces), shape((tokens, key_width), B...  1.48 us
  transfers between devices with their start and end apart: 21, of which 8 were waited for; matrix products, arithmetic and copies ran while one was open for 0% of the time, Pallas kernels for 24%

profile of v6, /device:TPU:0, one launch (start us, length us, event | category | flops | bytes accessed | tf_op | source)
XLA Modules:
  0.0 71.6 jit_solution(6136778885922455328)
XLA Ops:
  1.3 1.5 %shard_map.122.refs_0_ = bf16[128,512]{1,0:T(8,128)(2,1)S(1)} custom-call(s32[1,128]{1,0:T(1,128)S(1)} %copy-done.7, bf16[1,1024,512]{2,1,0:T(8,128)(2,1)} %rows_hbm.1), custom_call_target="tpu_custom_call" | custom-call | flops 262144 | bytes 1024 | tf_op jit(solution)/shard_map/pallas_call | solution.py:431
  2.8 4.0 %collective-permute-start.2 = (bf16[128,512]{1,0:T(8,128)(2,1)S(1)}, bf16[128,512]{1,0:T(8,128)(2,1)S(1)}, u32[]{:S(2)}, u32[]{:S(2)}) collective-permute-start(bf16[128,512]{1,0:T(8,128)(2,1)S(1)} %shard_map.122.refs_0_), channel_id=1, source_target_pairs={{0,24},{8,16},{16,8},{24,0},{1,25},{9,17},{17,9},{25,1},{2,26},{10... | collective-permute-start | bytes 393224 | tf_op jit(solution)/shard_map/ppermute | solution.py:86
  7.4 1.0 %copy-done = bf16[1,128,2048]{2,1,0:T(8,128)(2,1)S(1)} copy-done((bf16[1,128,2048]{2,1,0:T(8,128)(2,1)S(1)}, bf16[1,128,2048]{2,1,0:T(8,128)(2,1)}, u32[]{:S(2)}) %copy-start) | copy-done | bytes 524312
  8.4 1.0 %copy-done.2 = bf16[1,128,2048]{2,1,0:T(8,128)(2,1)S(1)} copy-done((bf16[1,128,2048]{2,1,0:T(8,128)(2,1)S(1)}, bf16[1,128,2048]{2,1,0:T(8,128)(2,1)}, u32[]{:S(2)}) %copy-start.2) | copy-done | bytes 524312
  11.7 1.6 %shard_map.123 = (f32[8,128]{1,0:T(8,128)S(1)}, f32[2048,128]{1,0:T(8,128)S(1)}, f32[2048,128]{1,0:T(8,128)S(1)}, f32[2048,128]{1,0:T(8,128)S(1)}, f32[2048,128]...) custom-call(s32[1,2]{1,0:T(1,128)S(1)} %copy-done.5, bf16[1,32,2048]{2,1,0:T(8,128)(2,1)S(1)} %copy-done.3, ...), custom_call_target="tpu_custom_call" | custom-call | flops 262144 | bytes 1024 | tf_op jit(solution)/shard_map/pallas_call | solution.py:444
  14.2 2.9 %collective-permute-start.5 = (f32[8,128]{1,0:T(8,128)S(1)}, f32[8,128]{1,0:T(8,128)S(1)}, u32[]{:S(2)}, u32[]{:S(2)}) collective-permute-start(f32[8,128]{1,0:T(8,128)S(1)} %get-tuple-element.55.after_ref.refs_0_), channel_id=1, source_target_pairs={{0,24},{8,16},{16,8},{24,0},{1,25},{9,17},{17,9},{25,1},{2,26},{10... | collective-permute-start | bytes 12296 | tf_op jit(solution)/shard_map/ppermute | solution.py:86
  17.8 2.2 %shard_map.125.refs_9_.refs_0_ = bf16[1024,2048]{1,0:T(8,128)(2,1)S(1)} custom-call(bf16[8192,2048]{1,0:T(8,128)(2,1)} %refs_0_.7, f32[8,128]{1,0:T(8,128)S(1)} %get-tuple-element.55.after_ref.refs_0_), custom_call_target="tpu_custom_call" | custom-call | flops 262144 | bytes 1024 | tf_op jit(solution)/shard_map/pallas_call | solution.py:472
  21.6 2.2 %shard_map.127 = (bf16[1024,2048]{1,0:T(8,128)(2,1)S(1)}, f32[8,128]{1,0:T(8,128)S(1)}) custom-call(bf16[8192,2048]{1,0:T(8,128)(2,1)} %refs_0_.7, f32[8,128]{1,0:T(8,128)S(1)} %get-tuple-element.60.refs_1_, f32[8,128]{1,0:T(8,128)S(1)} %get-tuple-element.61.refs_2_), custom_call_target="tpu_custom_call" | custom-call | flops 262144 | bytes 1024 | tf_op jit(solution)/shard_map/pallas_call | solution.py:74
  23.9 2.4 %shard_map.128 = (bf16[512,256]{1,0:T(8,128)(2,1)S(1)}, bf16[512,256]{1,0:T(8,128)(2,1)S(1)}, bf16[512,256]{1,0:T(8,128)(2,1)S(1)}, bf16[512,256]{1,0:T(8,128)(2,1)S(1)}, f32[8,128]{1,0:T(8,128)S(1)}) custom-call(bf16[1024,2048]{1,0:T(8,128)(2,1)S(1)} %shard_map.125.refs_9_.refs_0_, bf16[1024,2048]{1,0:T(8,128)(2,1)S(1)} %get-tuple-element.62.refs_1_, ...), custom_call_target="tpu_custom_call" | custom-call | flops 2147483648 | bytes 8388608 | tf_op jit(solution)/shard_map/pallas_call | solution.py:74
  26.3 1.7 %collective-permute-start.10 = (bf16[512,256]{1,0:T(8,128)(2,1)S(1)}, bf16[512,256]{1,0:T(8,128)(2,1)S(1)}, u32[]{:S(2)}, u32[]{:S(2)}) collective-permute-start(bf16[512,256]{1,0:T(8,128)(2,1)S(1)} %get-tuple-element.72), channel_id=1, source_target_pairs={{0,24},{8,16},{16,8},{24,0},{1,25},{9,17},{17,9},{25,1},{2,26},{10... | collective-permute-start | bytes 786440 | tf_op jit(solution)/shard_map/ppermute | solution.py:86
  28.5 1.3 %collective-permute-start.12 = (bf16[512,256]{1,0:T(8,128)(2,1)S(1)}, bf16[512,256]{1,0:T(8,128)(2,1)S(1)}, u32[]{:S(2)}, u32[]{:S(2)}) collective-permute-start(bf16[512,256]{1,0:T(8,128)(2,1)S(1)} %get-tuple-element.74), channel_id=1, source_target_pairs={{0,8},{8,0},{16,24},{24,16},{1,9},{9,1},{17,25},{25,17},{2,10},{10... | collective-permute-start | bytes 786440 | tf_op jit(solution)/shard_map/ppermute | solution.py:86
  30.8 1.5 %shard_map.130 = (bf16[1,32,2048]{2,1,0:T(8,128)(2,1)}, f32[8,128]{1,0:T(8,128)S(1)}) custom-call(s32[1,2]{1,0:T(1,128)S(1)} %copy-done.6, f32[8,128]{1,0:T(8,128)S(1)} %get-tuple-element.60.refs_1_, bf16[1,128,2048]{2,1,0:T(8,128)(2,1)S(1)} %copy-done, f32[8,128]{1,0:T(8,128)S(1)} %get-tuple-element.65.refs_3_), custom_call_target="tpu_custom_call" | custom-call | flops 262144 | bytes 1024 | tf_op jit(solution)/shard_map/pallas_call | solution.py:74
  32.3 4.9 %shard_map.131 = (bf16[512,256]{1,0:T(8,128)(2,1)S(1)}, bf16[512,256]{1,0:T(8,128)(2,1)S(1)}, bf16[512,256]{1,0:T(8,128)(2,1)S(1)}, bf16[512,256]{1,0:T(8,128)(2,1)S(1)}, f32[8,128]{1,0:T(8,128)S(1)}) custom-call(bf16[8192,2048]{1,0:T(8,128)(2,1)} %refs_0_.7, bf16[2064,128]{1,0:T(8,128)(2,1)S(1)} %get-tuple-element.59.refs_2_.refs_1_.refs_0_, ...), custom_call_target="tpu_custom_call" | custom-call | flops 2147483648 | bytes 8388608 | tf_op jit(solution)/shard_map/pallas_call | solution.py:74
  37.2 1.7 %collective-permute-start.7 = (bf16[512,256]{1,0:T(8,128)(2,1)S(1)}, bf16[512,256]{1,0:T(8,128)(2,1)S(1)}, u32[]{:S(2)}, u32[]{:S(2)}) collective-permute-start(bf16[512,256]{1,0:T(8,128)(2,1)S(1)} %get-tuple-element.68), channel_id=1, source_target_pairs={{0,24},{8,16},{16,8},{24,0},{1,25},{9,17},{17,9},{25,1},{2,26},{10... | collective-permute-start | bytes 786440 | tf_op jit(solution)/shard_map/ppermute | solution.py:86
  39.4 1.4 %collective-permute-start.9 = (bf16[512,256]{1,0:T(8,128)(2,1)S(1)}, bf16[512,256]{1,0:T(8,128)(2,1)S(1)}, u32[]{:S(2)}, u32[]{:S(2)}) collective-permute-start(bf16[512,256]{1,0:T(8,128)(2,1)S(1)} %get-tuple-element.70), channel_id=1, source_target_pairs={{0,8},{8,0},{16,24},{24,16},{1,9},{9,1},{17,25},{25,17},{2,10},{10... | collective-permute-start | bytes 786440 | tf_op jit(solution)/shard_map/ppermute | solution.py:86
  40.7 1.3 %collective-permute-done.11.refs_4_ = bf16[512,256]{1,0:T(8,128)(2,1)S(1)} collective-permute-done((bf16[512,256]{1,0:T(8,128)(2,1)S(1)}, bf16[512,256]{1,0:T(8,128)(2,1)S(1)}, u32[]{:S(2)}, u32[]{:S(2)}) %collective-permute-start.11) | collective-permute-done | bytes 262176 | tf_op jit(solution)/shard_map/ppermute | solution.py:86
  42.5 3.7 %collective-permute-start.16 = (bf16[128,512]{1,0:T(8,128)(2,1)S(1)}, bf16[128,512]{1,0:T(8,128)(2,1)S(1)}, u32[]{:S(2)}, u32[]{:S(2)}) collective-permute-start(bf16[128,512]{1,0:T(8,128)(2,1)S(1)} %get-tuple-element.82), channel_id=1, source_target_pairs={{0,6},{1,7},{2,4},{3,5},{4,2},{5,3},{6,0},{7,1},{8,14},{9,15},{10,... | collective-permute-start | bytes 393224 | tf_op jit(solution)/shard_map/ppermute | solution.py:86
  46.2 1.5 %collective-permute-done.7.refs_3_ = bf16[512,256]{1,0:T(8,128)(2,1)S(1)} collective-permute-done((bf16[512,256]{1,0:T(8,128)(2,1)S(1)}, bf16[512,256]{1,0:T(8,128)(2,1)S(1)}, u32[]{:S(2)}, u32[]{:S(2)}) %collective-permute-start.7) | collective-permute-done | bytes 262176 | tf_op jit(solution)/shard_map/ppermute | solution.py:86
  47.7 1.6 %collective-permute-start.18 = (bf16[128,512]{1,0:T(8,128)(2,1)S(1)}, bf16[128,512]{1,0:T(8,128)(2,1)S(1)}, u32[]{:S(2)}, u32[]{:S(2)}) collective-permute-start(bf16[128,512]{1,0:T(8,128)(2,1)S(1)} %get-tuple-element.84), channel_id=1, source_target_pairs={{0,2},{1,3},{2,0},{3,1},{4,6},{5,7},{6,4},{7,5},{8,10},{9,11},{10,... | collective-permute-start | bytes 393224 | tf_op jit(solution)/shard_map/ppermute | solution.py:86
  49.3 3.5 %collective-permute-done.8.refs_4_ = bf16[512,256]{1,0:T(8,128)(2,1)S(1)} collective-permute-done((bf16[512,256]{1,0:T(8,128)(2,1)S(1)}, bf16[512,256]{1,0:T(8,128)(2,1)S(1)}, u32[]{:S(2)}, u32[]{:S(2)}) %collective-permute-start.8) | collective-permute-done | bytes 262176 | tf_op jit(solution)/shard_map/ppermute | solution.py:86
  53.4 3.7 %collective-permute-start.13 = (bf16[128,512]{1,0:T(8,128)(2,1)S(1)}, bf16[128,512]{1,0:T(8,128)(2,1)S(1)}, u32[]{:S(2)}, u32[]{:S(2)}) collective-permute-start(bf16[128,512]{1,0:T(8,128)(2,1)S(1)} %get-tuple-element.78), channel_id=1, source_target_pairs={{0,6},{1,7},{2,4},{3,5},{4,2},{5,3},{6,0},{7,1},{8,14},{9,15},{10,... | collective-permute-start | bytes 393224 | tf_op jit(solution)/shard_map/ppermute | solution.py:86
  59.0 2.7 %collective-permute-done.13.refs_1_ = bf16[128,512]{1,0:T(8,128)(2,1)S(1)} collective-permute-done((bf16[128,512]{1,0:T(8,128)(2,1)S(1)}, bf16[128,512]{1,0:T(8,128)(2,1)S(1)}, u32[]{:S(2)}, u32[]{:S(2)}) %collective-permute-start.13) | collective-permute-done | bytes 131104 | tf_op jit(solution)/shard_map/ppermute | solution.py:86
  61.7 6.8 %collective-permute-done.14.refs_2_ = bf16[128,512]{1,0:T(8,128)(2,1)S(1)} collective-permute-done((bf16[128,512]{1,0:T(8,128)(2,1)S(1)}, bf16[128,512]{1,0:T(8,128)(2,1)S(1)}, u32[]{:S(2)}, u32[]{:S(2)}) %collective-permute-start.14) | collective-permute-done | bytes 131104 | tf_op jit(solution)/shard_map/ppermute | solution.py:86
  68.6 1.0 %shard_map.137 = (bf16[1,2048,256]{2,1,0:T(8,128)(2,1)}, f32[8,128]{1,0:T(8,128)S(1)}) custom-call(bf16[256,512]{1,0:T(8,128)(2,1)S(1)} %collective-permute-done.20.refs_0_, f32[2048,256]{1,0:T(8,128)S(1)} %get-tuple-element.87.refs_1_, bf16[1,2048,256]{2,1,0:T(8,128)(2,1)} %get-tuple-element.93.refs_2_, ...), custom_call_target="tpu_custom_call", output_to_operand_aliasing={{0}: (2, {})} | custom-call | flops 262144 | bytes 1024 | tf_op jit(solution)/shard_map/pallas_call | solution.py:74
  (54 shorter events, 13.7 us)
Async XLA Ops:
  2.8 10.6 %collective-permute-start.2 = (bf16[128,512]{1,0:T(8,128)(2,1)S(1)}, bf16[128,512]{1,0:T(8,128)(2,1)S(1)}, u32[]{:S(2)}, u32[]{:S(2)}) collective-permute-start(bf16[128,512]{1,0:T(8,128)(2,1)S(1)} %shard_map.122.refs_0_), channel_id=1, source_target_pairs={{0,24},{8,16},{16,8},{24,0},{1,25},{9,17},{17,9},{25,1},{2,26},{10... | collective-permute-start | bytes 393224 | tf_op jit(solution)/shard_map/ppermute | solution.py:86
  6.7 6.6 %collective-permute-start.1 = (bf16[128,512]{1,0:T(8,128)(2,1)S(1)}, bf16[128,512]{1,0:T(8,128)(2,1)S(1)}, u32[]{:S(2)}, u32[]{:S(2)}) collective-permute-start(bf16[128,512]{1,0:T(8,128)(2,1)S(1)} %shard_map.122.refs_0_), channel_id=1, source_target_pairs={{0,16},{8,24},{16,0},{24,8},{1,17},{9,25},{17,1},{25,9},{2,18},{10... | collective-permute-start | bytes 393224 | tf_op jit(solution)/shard_map/ppermute | solution.py:86
  7.2 6.1 %collective-permute-start = (bf16[128,512]{1,0:T(8,128)(2,1)S(1)}, bf16[128,512]{1,0:T(8,128)(2,1)S(1)}, u32[]{:S(2)}, u32[]{:S(2)}) collective-permute-start(bf16[128,512]{1,0:T(8,128)(2,1)S(1)} %shard_map.122.refs_0_), channel_id=1, source_target_pairs={{0,8},{8,0},{16,24},{24,16},{1,9},{9,1},{17,25},{25,17},{2,10},{10... | collective-permute-start | bytes 393224 | tf_op jit(solution)/shard_map/ppermute | solution.py:86
  14.2 7.0 %copy-start.8 = (s32[1,128,1]{1,2,0:T(1,128)S(1)}, s32[1,128,1]{1,2,0:T(1,128)}, u32[]{:S(2)}) copy-start(s32[1,128,1]{1,2,0:T(1,128)} %param.15) | copy-start | bytes 1540
  14.2 5.8 %collective-permute-start.5 = (f32[8,128]{1,0:T(8,128)S(1)}, f32[8,128]{1,0:T(8,128)S(1)}, u32[]{:S(2)}, u32[]{:S(2)}) collective-permute-start(f32[8,128]{1,0:T(8,128)S(1)} %get-tuple-element.55.after_ref.refs_0_), channel_id=1, source_target_pairs={{0,24},{8,16},{16,8},{24,0},{1,25},{9,17},{17,9},{25,1},{2,26},{10... | collective-permute-start | bytes 12296 | tf_op jit(solution)/shard_map/ppermute | solution.py:86
  17.2 3.6 %collective-permute-start.4 = (f32[8,128]{1,0:T(8,128)S(1)}, f32[8,128]{1,0:T(8,128)S(1)}, u32[]{:S(2)}, u32[]{:S(2)}) collective-permute-start(f32[8,128]{1,0:T(8,128)S(1)} %get-tuple-element.55.after_ref.refs_0_), channel_id=1, source_target_pairs={{0,16},{8,24},{16,0},{24,8},{1,17},{9,25},{17,1},{25,9},{2,18},{10... | collective-permute-start | bytes 12296 | tf_op jit(solution)/shard_map/ppermute | solution.py:86
  17.7 3.6 %collective-permute-start.3 = (f32[8,128]{1,0:T(8,128)S(1)}, f32[8,128]{1,0:T(8,128)S(1)}, u32[]{:S(2)}, u32[]{:S(2)}) collective-permute-start(f32[8,128]{1,0:T(8,128)S(1)} %get-tuple-element.55.after_ref.refs_0_), channel_id=1, source_target_pairs={{0,8},{8,0},{16,24},{24,16},{1,9},{9,1},{17,25},{25,17},{2,10},{10... | collective-permute-start | bytes 12296 | tf_op jit(solution)/shard_map/ppermute | solution.py:86
  21.6 2.3 %collective-permute-start.6 = (bf16[2064,128]{1,0:T(8,128)(2,1)S(1)}, bf16[2064,128]{1,0:T(8,128)(2,1)S(1)}, u32[]{:S(2)}, u32[]{:S(2)}) collective-permute-start(bf16[2064,128]{1,0:T(8,128)(2,1)S(1)} %get-tuple-element.59.refs_2_.refs_1_.refs_0_), channel_id=1, source_target_pairs={{0,1},{1,0},{2,3},{3,2},{4,5},{5,4},{6,7},{7,6},{8,9},{9,8},{10,11... | collective-permute-start | bytes 1585160 | tf_op jit(solution)/shard_map/ppermute | solution.py:86
  23.9 6.0 %copy-start.1 = (bf16[1,2048,256]{2,1,0:T(8,128)(2,1)S(1)}, bf16[1,2048,256]{2,1,0:T(8,128)(2,1)}, u32[]{:S(2)}) copy-start(bf16[1,2048,256]{2,1,0:T(8,128)(2,1)} %refs_0_.5) | copy-start | bytes 3145732
  23.9 6.9 %copy-start.6 = (s32[1,2]{1,0:T(1,128)S(1)}, s32[1,2]{1,0:T(1,128)}, u32[]{:S(2)}) copy-start(s32[1,2]{1,0:T(1,128)} %refs_0_.6) | copy-start | bytes 28
  26.3 13.1 %collective-permute-start.10 = (bf16[512,256]{1,0:T(8,128)(2,1)S(1)}, bf16[512,256]{1,0:T(8,128)(2,1)S(1)}, u32[]{:S(2)}, u32[]{:S(2)}) collective-permute-start(bf16[512,256]{1,0:T(8,128)(2,1)S(1)} %get-tuple-element.72), channel_id=1, source_target_pairs={{0,24},{8,16},{16,8},{24,0},{1,25},{9,17},{17,9},{25,1},{2,26},{10... | collective-permute-start | bytes 786440 | tf_op jit(solution)/shard_map/ppermute | solution.py:86
  28.0 14.1 %collective-permute-start.11 = (bf16[512,256]{1,0:T(8,128)(2,1)S(1)}, bf16[512,256]{1,0:T(8,128)(2,1)S(1)}, u32[]{:S(2)}, u32[]{:S(2)}) collective-permute-start(bf16[512,256]{1,0:T(8,128)(2,1)S(1)} %get-tuple-element.73), channel_id=1, source_target_pairs={{0,16},{8,24},{16,0},{24,8},{1,17},{9,25},{17,1},{25,9},{2,18},{10... | collective-permute-start | bytes 786440 | tf_op jit(solution)/shard_map/ppermute | solution.py:86
  28.5 13.6 %collective-permute-start.12 = (bf16[512,256]{1,0:T(8,128)(2,1)S(1)}, bf16[512,256]{1,0:T(8,128)(2,1)S(1)}, u32[]{:S(2)}, u32[]{:S(2)}) collective-permute-start(bf16[512,256]{1,0:T(8,128)(2,1)S(1)} %get-tuple-element.74), channel_id=1, source_target_pairs={{0,8},{8,0},{16,24},{24,16},{1,9},{9,1},{17,25},{25,17},{2,10},{10... | collective-permute-start | bytes 786440 | tf_op jit(solution)/shard_map/ppermute | solution.py:86
  37.2 10.5 %collective-permute-start.7 = (bf16[512,256]{1,0:T(8,128)(2,1)S(1)}, bf16[512,256]{1,0:T(8,128)(2,1)S(1)}, u32[]{:S(2)}, u32[]{:S(2)}) collective-permute-start(bf16[512,256]{1,0:T(8,128)(2,1)S(1)} %get-tuple-element.68), channel_id=1, source_target_pairs={{0,24},{8,16},{16,8},{24,0},{1,25},{9,17},{17,9},{25,1},{2,26},{10... | collective-permute-start | bytes 786440 | tf_op jit(solution)/shard_map/ppermute | solution.py:86
  38.9 13.9 %collective-permute-start.8 = (bf16[512,256]{1,0:T(8,128)(2,1)S(1)}, bf16[512,256]{1,0:T(8,128)(2,1)S(1)}, u32[]{:S(2)}, u32[]{:S(2)}) collective-permute-start(bf16[512,256]{1,0:T(8,128)(2,1)S(1)} %get-tuple-element.69), channel_id=1, source_target_pairs={{0,16},{8,24},{16,0},{24,8},{1,17},{9,25},{17,1},{25,9},{2,18},{10... | collective-permute-start | bytes 786440 | tf_op jit(solution)/shard_map/ppermute | solution.py:86
  39.4 13.6 %collective-permute-start.9 = (bf16[512,256]{1,0:T(8,128)(2,1)S(1)}, bf16[512,256]{1,0:T(8,128)(2,1)S(1)}, u32[]{:S(2)}, u32[]{:S(2)}) collective-permute-start(bf16[512,256]{1,0:T(8,128)(2,1)S(1)} %get-tuple-element.70), channel_id=1, source_target_pairs={{0,8},{8,0},{16,24},{24,16},{1,9},{9,1},{17,25},{25,17},{2,10},{10... | collective-permute-start | bytes 786440 | tf_op jit(solution)/shard_map/ppermute | solution.py:86
  42.5 14.5 %collective-permute-start.16 = (bf16[128,512]{1,0:T(8,128)(2,1)S(1)}, bf16[128,512]{1,0:T(8,128)(2,1)S(1)}, u32[]{:S(2)}, u32[]{:S(2)}) collective-permute-start(bf16[128,512]{1,0:T(8,128)(2,1)S(1)} %get-tuple-element.82), channel_id=1, source_target_pairs={{0,6},{1,7},{2,4},{3,5},{4,2},{5,3},{6,0},{7,1},{8,14},{9,15},{10,... | collective-permute-start | bytes 393224 | tf_op jit(solution)/shard_map/ppermute | solution.py:86
  46.2 11.6 %collective-permute-start.17 = (bf16[128,512]{1,0:T(8,128)(2,1)S(1)}, bf16[128,512]{1,0:T(8,128)(2,1)S(1)}, u32[]{:S(2)}, u32[]{:S(2)}) collective-permute-start(bf16[128,512]{1,0:T(8,128)(2,1)S(1)} %get-tuple-element.83), channel_id=1, source_target_pairs={{0,4},{1,5},{2,6},{3,7},{4,0},{5,1},{6,2},{7,3},{8,12},{9,13},{10,... | collective-permute-start | bytes 393224 | tf_op jit(solution)/shard_map/ppermute | solution.py:86
  47.7 10.2 %collective-permute-start.18 = (bf16[128,512]{1,0:T(8,128)(2,1)S(1)}, bf16[128,512]{1,0:T(8,128)(2,1)S(1)}, u32[]{:S(2)}, u32[]{:S(2)}) collective-permute-start(bf16[128,512]{1,0:T(8,128)(2,1)S(1)} %get-tuple-element.84), channel_id=1, source_target_pairs={{0,2},{1,3},{2,0},{3,1},{4,6},{5,7},{6,4},{7,5},{8,10},{9,11},{10,... | collective-permute-start | bytes 393224 | tf_op jit(solution)/shard_map/ppermute | solution.py:86
  53.4 8.3 %collective-permute-start.13 = (bf16[128,512]{1,0:T(8,128)(2,1)S(1)}, bf16[128,512]{1,0:T(8,128)(2,1)S(1)}, u32[]{:S(2)}, u32[]{:S(2)}) collective-permute-start(bf16[128,512]{1,0:T(8,128)(2,1)S(1)} %get-tuple-element.78), channel_id=1, source_target_pairs={{0,6},{1,7},{2,4},{3,5},{4,2},{5,3},{6,0},{7,1},{8,14},{9,15},{10,... | collective-permute-start | bytes 393224 | tf_op jit(solution)/shard_map/ppermute | solution.py:86
  57.1 11.4 %collective-permute-start.14 = (bf16[128,512]{1,0:T(8,128)(2,1)S(1)}, bf16[128,512]{1,0:T(8,128)(2,1)S(1)}, u32[]{:S(2)}, u32[]{:S(2)}) collective-permute-start(bf16[128,512]{1,0:T(8,128)(2,1)S(1)} %get-tuple-element.79), channel_id=1, source_target_pairs={{0,4},{1,5},{2,6},{3,7},{4,0},{5,1},{6,2},{7,3},{8,12},{9,13},{10,... | collective-permute-start | bytes 393224 | tf_op jit(solution)/shard_map/ppermute | solution.py:86
  57.1 11.4 %collective-permute-start.15 = (bf16[128,512]{1,0:T(8,128)(2,1)S(1)}, bf16[128,512]{1,0:T(8,128)(2,1)S(1)}, u32[]{:S(2)}, u32[]{:S(2)}) collective-permute-start(bf16[128,512]{1,0:T(8,128)(2,1)S(1)} %get-tuple-element.80), channel_id=1, source_target_pairs={{0,2},{1,3},{2,0},{3,1},{4,6},{5,7},{6,4},{7,5},{8,10},{9,11},{10,... | collective-permute-start | bytes 393224 | tf_op jit(solution)/shard_map/ppermute | solution.py:86
  57.9 10.7 %collective-permute-start.20 = (bf16[256,512]{1,0:T(8,128)(2,1)S(1)}, bf16[256,512]{1,0:T(8,128)(2,1)S(1)}, u32[]{:S(2)}, u32[]{:S(2)}) collective-permute-start(bf16[256,512]{1,0:T(8,128)(2,1)S(1)} %get-tuple-element.92), channel_id=1, source_target_pairs={{0,1},{1,0},{2,3},{3,2},{4,5},{5,4},{6,7},{7,6},{8,9},{9,8},{10,11... | collective-permute-start | bytes 786440 | tf_op jit(solution)/shard_map/ppermute | solution.py:86
  68.6 2.1 %collective-permute-start.19 = (bf16[256,512]{1,0:T(8,128)(2,1)S(1)}, bf16[256,512]{1,0:T(8,128)(2,1)S(1)}, u32[]{:S(2)}, u32[]{:S(2)}) collective-permute-start(bf16[256,512]{1,0:T(8,128)(2,1)S(1)} %get-tuple-element.90), channel_id=1, source_target_pairs={{0,1},{1,0},{2,3},{3,2},{4,5},{5,4},{6,7},{7,6},{8,9},{9,8},{10,11... | collective-permute-start | bytes 786440 | tf_op jit(solution)/shard_map/ppermute | solution.py:86
  (6 other events, 5.0 us)

commit v7 on v5

--- a/solution.py
+++ b/solution.py
@@ -135,8 +135,8 @@
 
 
 def load_kernel(
-    span_hbm, hidden_ref, gain_ref, proj_ref, resid_ref, weight_hbm,
-    stats_ref, projt_ref, residt_ref, gaint_ref, meant_ref, weight_ref,
+    span_hbm, hidden_ref, proj_ref, resid_ref, weight_hbm,
+    stats_ref, projt_ref, residt_ref, meant_ref, weight_ref,
     span, sems,
 ):
     load = pltpu.make_async_copy(weight_hbm, weight_ref, sems.at[0])
@@ -146,7 +146,6 @@
     tokens, width = proj_ref.shape[1:]
     for at in range(0, width, LANES):
         cut = slice(at, at + LANES)
-        gaint_ref[cut, :] = to_column(gain_ref[:, cut])
         projt_ref[cut, :] = jnp.transpose(proj_ref[0, :, cut], (1, 0)).astype(F32)
         residt_ref[cut, :] = jnp.transpose(resid_ref[0, :, cut], (1, 0)).astype(F32)
     head.wait()
@@ -172,7 +171,7 @@
 
 def norm_kernel(peers, *refs):
     own_refs = refs[:peers]
-    stats_ref, weight_ref, gaint_ref, projt_ref, scaledt_ref, sums_ref, pickedt = refs[peers:]
+    stats_ref, weight_ref, gain_ref, projt_ref, scaledt_ref, sums_ref, pickedt = refs[peers:]
     key_width = own_refs[0].shape[1]
     for at in range(0, key_width, LANES):
         cut = slice(at, at + LANES)
@@ -185,7 +184,8 @@
     for at in range(0, width, 256):
         cut = slice(at, at + 256)
         normed = jnp.dot(weight_ref[cut, :], pickedt[...], preferred_element_type=F32)
-        scaled = normed * gaint_ref[cut, :]
+        gain = [to_column(gain_ref[:, first : first + LANES]) for first in (at, at + LANES)]
+        scaled = normed * jnp.concatenate(gain, axis=0)
         scaledt_ref[cut, :] = scaled
         terms = scaled * projt_ref[cut, :]
         total = total + terms[:LANES] + terms[LANES:]
@@ -441,20 +441,20 @@
     )(vis_pos, value_grad)
     own_all = [own] + [swap(own, "seq", peers, k) for k in range(1, peers)]
 
-    stats, projt, residt, gaint, meant, weight = call(
+    stats, projt, residt, meant, weight = call(
         load_kernel,
-        [row, tall, tall, tall, tall, shape(w_value.shape, BF16)],
-        [HBM, VMEM, VMEM, VMEM, VMEM, HBM],
+        [row, tall, tall, tall, shape(w_value.shape, BF16)],
+        [HBM, VMEM, VMEM, VMEM, HBM],
         [pltpu.SMEM((1, 2), jnp.int32), dma((2,))],
         grant=LOAD_GRANT,
-    )(ques_span, ques_hidden, gain, vis_proj, vis_resid, w_value)
+    )(ques_span, ques_hidden, vis_proj, vis_resid, w_value)
 
     scaledt, sums = call(
         functools.partial(norm_kernel, peers),
         [tall, row],
         [VMEM] * (peers + 4),
         [pltpu.VMEM((key_width, tokens), BF16)],
-    )(*own_all, stats, weight, gaint, projt)
+    )(*own_all, stats, weight, gain, projt)
     sums_all = [sums] + [swap(sums, "seq", peers, k) for k in range(1, peers)]
 
     paired = capacity % 16 == 0 and owners_count % 2 == 0

time: 72 us -> 71.6 us (level)
  transfers between devices with their start and end apart: 21 -> 21, of which waited for: 8 -> 9; matrix products, arithmetic and copies ran while one was open for 0% -> 0% of each run, Pallas kernels for 24% -> 24%
where the time goes in v7:
time: 71.6 us; the launch traced here: 71.2 us
  starting transfers between devices  25.2 us (35%)
  Pallas kernels  23.2 us (32%)
  waiting for transfers between devices  17.6 us (25%)
  local copies, waits for them, and re-layouts  4.32 us (6%)
  between operations  0.89 us (1%)
    ppermute x21, starting transfers between devices, swap(): return lax.ppermute(value, axis, [(i, i ^ step) for i in range(count)])  25.2 us
    ppermute x21, waiting for transfers between devices, swap(): return lax.ppermute(value, axis, [(i, i ^ step) for i in range(count)])  17.6 us
    pallas_call x14, Pallas kernels, apply(): results = run_call(*args, *self.last)  17.1 us
    unnamed x18, local copies, waits for them, and re-layouts  4.32 us
    pallas_call x1, Pallas kernels, preload(): caller(functools.partial(preload_kernel, half * count, count, peers, shar...  2.2 us
    pallas_call x1, Pallas kernels, body(): call(load_kernel, [row, tall, tall, tall, shape(w_value.shape, BF16)], [H...  1.61 us
    pallas_call x1, Pallas kernels, body(): call(functools.partial(pick_kernel, pieces), shape((tokens, key_width), B...  1.48 us
  transfers between devices with their start and end apart: 21, of which 9 were waited for; matrix products, arithmetic and copies ran while one was open for 0% of the time, Pallas kernels for 24%

profile of v7, /device:TPU:0, one launch (start us, length us, event | category | flops | bytes accessed | tf_op | source)
XLA Modules:
  0.0 71.2 jit_solution(1125300648473463426)
XLA Ops:
  1.3 1.5 %shard_map.122.refs_0_ = bf16[128,512]{1,0:T(8,128)(2,1)S(1)} custom-call(s32[1,128]{1,0:T(1,128)S(1)} %copy-done.7, bf16[1,1024,512]{2,1,0:T(8,128)(2,1)} %rows_hbm.1), custom_call_target="tpu_custom_call" | custom-call | flops 262144 | bytes 1024 | tf_op jit(solution)/shard_map/pallas_call | solution.py:431
  2.8 4.0 %collective-permute-start.2 = (bf16[128,512]{1,0:T(8,128)(2,1)S(1)}, bf16[128,512]{1,0:T(8,128)(2,1)S(1)}, u32[]{:S(2)}, u32[]{:S(2)}) collective-permute-start(bf16[128,512]{1,0:T(8,128)(2,1)S(1)} %shard_map.122.refs_0_), channel_id=1, source_target_pairs={{0,24},{8,16},{16,8},{24,0},{1,25},{9,17},{17,9},{25,1},{2,26},{10... | collective-permute-start | bytes 393224 | tf_op jit(solution)/shard_map/ppermute | solution.py:86
  7.4 1.0 %copy-done = bf16[1,128,2048]{2,1,0:T(8,128)(2,1)S(1)} copy-done((bf16[1,128,2048]{2,1,0:T(8,128)(2,1)S(1)}, bf16[1,128,2048]{2,1,0:T(8,128)(2,1)}, u32[]{:S(2)}) %copy-start) | copy-done | bytes 524312
  8.4 1.0 %copy-done.2 = bf16[1,128,2048]{2,1,0:T(8,128)(2,1)S(1)} copy-done((bf16[1,128,2048]{2,1,0:T(8,128)(2,1)S(1)}, bf16[1,128,2048]{2,1,0:T(8,128)(2,1)}, u32[]{:S(2)}) %copy-start.2) | copy-done | bytes 524312
  11.0 1.6 %shard_map.123 = (f32[8,128]{1,0:T(8,128)S(1)}, f32[2048,128]{1,0:T(8,128)S(1)}, f32[2048,128]{1,0:T(8,128)S(1)}, f32[2048,128]{1,0:T(8,128)S(1)}, bf16[2048,512]{1,0:T(8,128)(2,1)S(1)}) custom-call(s32[1,2]{1,0:T(1,128)S(1)} %copy-done.5, bf16[1,32,2048]{2,1,0:T(8,128)(2,1)S(1)} %copy-done.3, bf16[1,128,2048]{2,1,0:T(8,128)(2,1)S(1)} %copy-done, ...), custom_call_target="tpu_custom_call" | custom-call | flops 262144 | bytes 1024 | tf_op jit(solution)/shard_map/pallas_call | solution.py:444
  14.2 2.3 %collective-permute-start.5 = (f32[8,128]{1,0:T(8,128)S(1)}, f32[8,128]{1,0:T(8,128)S(1)}, u32[]{:S(2)}, u32[]{:S(2)}) collective-permute-start(f32[8,128]{1,0:T(8,128)S(1)} %get-tuple-element.53.after_ref.refs_0_), channel_id=1, source_target_pairs={{0,24},{8,16},{16,8},{24,0},{1,25},{9,17},{17,9},{25,1},{2,26},{10... | collective-permute-start | bytes 12296 | tf_op jit(solution)/shard_map/ppermute | solution.py:86
  17.7 2.2 %shard_map.125.refs_9_.refs_0_ = bf16[1024,2048]{1,0:T(8,128)(2,1)S(1)} custom-call(bf16[8192,2048]{1,0:T(8,128)(2,1)} %refs_0_.5, f32[8,128]{1,0:T(8,128)S(1)} %get-tuple-element.53.after_ref.refs_0_), custom_call_target="tpu_custom_call" | custom-call | flops 262144 | bytes 1024 | tf_op jit(solution)/shard_map/pallas_call | solution.py:472
  21.2 2.2 %shard_map.127 = (bf16[1024,2048]{1,0:T(8,128)(2,1)S(1)}, f32[8,128]{1,0:T(8,128)S(1)}) custom-call(bf16[8192,2048]{1,0:T(8,128)(2,1)} %refs_0_.5, f32[8,128]{1,0:T(8,128)S(1)} %get-tuple-element.58.refs_1_, f32[8,128]{1,0:T(8,128)S(1)} %get-tuple-element.59.refs_2_), custom_call_target="tpu_custom_call" | custom-call | flops 262144 | bytes 1024 | tf_op jit(solution)/shard_map/pallas_call | solution.py:74
  23.5 2.4 %shard_map.128 = (bf16[512,256]{1,0:T(8,128)(2,1)S(1)}, bf16[512,256]{1,0:T(8,128)(2,1)S(1)}, bf16[512,256]{1,0:T(8,128)(2,1)S(1)}, bf16[512,256]{1,0:T(8,128)(2,1)S(1)}, f32[8,128]{1,0:T(8,128)S(1)}) custom-call(bf16[1024,2048]{1,0:T(8,128)(2,1)S(1)} %shard_map.125.refs_9_.refs_0_, bf16[1024,2048]{1,0:T(8,128)(2,1)S(1)} %get-tuple-element.60.refs_1_, ...), custom_call_target="tpu_custom_call" | custom-call | flops 2147483648 | bytes 8388608 | tf_op jit(solution)/shard_map/pallas_call | solution.py:74
  25.9 1.5 %collective-permute-start.10 = (bf16[512,256]{1,0:T(8,128)(2,1)S(1)}, bf16[512,256]{1,0:T(8,128)(2,1)S(1)}, u32[]{:S(2)}, u32[]{:S(2)}) collective-permute-start(bf16[512,256]{1,0:T(8,128)(2,1)S(1)} %get-tuple-element.68), channel_id=1, source_target_pairs={{0,24},{8,16},{16,8},{24,0},{1,25},{9,17},{17,9},{25,1},{2,26},{10... | collective-permute-start | bytes 786440 | tf_op jit(solution)/shard_map/ppermute | solution.py:86
  28.1 1.4 %collective-permute-start.12 = (bf16[512,256]{1,0:T(8,128)(2,1)S(1)}, bf16[512,256]{1,0:T(8,128)(2,1)S(1)}, u32[]{:S(2)}, u32[]{:S(2)}) collective-permute-start(bf16[512,256]{1,0:T(8,128)(2,1)S(1)} %get-tuple-element.70), channel_id=1, source_target_pairs={{0,8},{8,0},{16,24},{24,16},{1,9},{9,1},{17,25},{25,17},{2,10},{10... | collective-permute-start | bytes 786440 | tf_op jit(solution)/shard_map/ppermute | solution.py:86
  29.4 4.9 %shard_map.129 = (bf16[512,256]{1,0:T(8,128)(2,1)S(1)}, bf16[512,256]{1,0:T(8,128)(2,1)S(1)}, bf16[512,256]{1,0:T(8,128)(2,1)S(1)}, bf16[512,256]{1,0:T(8,128)(2,1)S(1)}, f32[8,128]{1,0:T(8,128)S(1)}) custom-call(bf16[8192,2048]{1,0:T(8,128)(2,1)} %refs_0_.5, bf16[2064,128]{1,0:T(8,128)(2,1)S(1)} %get-tuple-element.57.refs_2_.refs_1_.refs_0_, ...), custom_call_target="tpu_custom_call" | custom-call | flops 2147483648 | bytes 8388608 | tf_op jit(solution)/shard_map/pallas_call | solution.py:74
  34.3 1.5 %collective-permute-start.7 = (bf16[512,256]{1,0:T(8,128)(2,1)S(1)}, bf16[512,256]{1,0:T(8,128)(2,1)S(1)}, u32[]{:S(2)}, u32[]{:S(2)}) collective-permute-start(bf16[512,256]{1,0:T(8,128)(2,1)S(1)} %get-tuple-element.64), channel_id=1, source_target_pairs={{0,24},{8,16},{16,8},{24,0},{1,25},{9,17},{17,9},{25,1},{2,26},{10... | collective-permute-start | bytes 786440 | tf_op jit(solution)/shard_map/ppermute | solution.py:86
  36.5 1.4 %collective-permute-start.9 = (bf16[512,256]{1,0:T(8,128)(2,1)S(1)}, bf16[512,256]{1,0:T(8,128)(2,1)S(1)}, u32[]{:S(2)}, u32[]{:S(2)}) collective-permute-start(bf16[512,256]{1,0:T(8,128)(2,1)S(1)} %get-tuple-element.66), channel_id=1, source_target_pairs={{0,8},{8,0},{16,24},{24,16},{1,9},{9,1},{17,25},{25,17},{2,10},{10... | collective-permute-start | bytes 786440 | tf_op jit(solution)/shard_map/ppermute | solution.py:86
  37.9 3.8 %collective-permute-done.11.refs_4_ = bf16[512,256]{1,0:T(8,128)(2,1)S(1)} collective-permute-done((bf16[512,256]{1,0:T(8,128)(2,1)S(1)}, bf16[512,256]{1,0:T(8,128)(2,1)S(1)}, u32[]{:S(2)}, u32[]{:S(2)}) %collective-permute-start.11) | collective-permute-done | bytes 262176 | tf_op jit(solution)/shard_map/ppermute | solution.py:86
  42.1 3.7 %collective-permute-start.16 = (bf16[128,512]{1,0:T(8,128)(2,1)S(1)}, bf16[128,512]{1,0:T(8,128)(2,1)S(1)}, u32[]{:S(2)}, u32[]{:S(2)}) collective-permute-start(bf16[128,512]{1,0:T(8,128)(2,1)S(1)} %get-tuple-element.78), channel_id=1, source_target_pairs={{0,6},{1,7},{2,4},{3,5},{4,2},{5,3},{6,0},{7,1},{8,14},{9,15},{10,... | collective-permute-start | bytes 393224 | tf_op jit(solution)/shard_map/ppermute | solution.py:86
  45.8 1.5 %collective-permute-done.7.refs_3_ = bf16[512,256]{1,0:T(8,128)(2,1)S(1)} collective-permute-done((bf16[512,256]{1,0:T(8,128)(2,1)S(1)}, bf16[512,256]{1,0:T(8,128)(2,1)S(1)}, u32[]{:S(2)}, u32[]{:S(2)}) %collective-permute-start.7) | collective-permute-done | bytes 262176 | tf_op jit(solution)/shard_map/ppermute | solution.py:86
  47.3 1.6 %collective-permute-start.18 = (bf16[128,512]{1,0:T(8,128)(2,1)S(1)}, bf16[128,512]{1,0:T(8,128)(2,1)S(1)}, u32[]{:S(2)}, u32[]{:S(2)}) collective-permute-start(bf16[128,512]{1,0:T(8,128)(2,1)S(1)} %get-tuple-element.80), channel_id=1, source_target_pairs={{0,2},{1,3},{2,0},{3,1},{4,6},{5,7},{6,4},{7,5},{8,10},{9,11},{10,... | collective-permute-start | bytes 393224 | tf_op jit(solution)/shard_map/ppermute | solution.py:86
  48.8 3.5 %collective-permute-done.8.refs_4_ = bf16[512,256]{1,0:T(8,128)(2,1)S(1)} collective-permute-done((bf16[512,256]{1,0:T(8,128)(2,1)S(1)}, bf16[512,256]{1,0:T(8,128)(2,1)S(1)}, u32[]{:S(2)}, u32[]{:S(2)}) %collective-permute-start.8) | collective-permute-done | bytes 262176 | tf_op jit(solution)/shard_map/ppermute | solution.py:86
  52.8 3.7 %collective-permute-start.13 = (bf16[128,512]{1,0:T(8,128)(2,1)S(1)}, bf16[128,512]{1,0:T(8,128)(2,1)S(1)}, u32[]{:S(2)}, u32[]{:S(2)}) collective-permute-start(bf16[128,512]{1,0:T(8,128)(2,1)S(1)} %get-tuple-element.74), channel_id=1, source_target_pairs={{0,6},{1,7},{2,4},{3,5},{4,2},{5,3},{6,0},{7,1},{8,14},{9,15},{10,... | collective-permute-start | bytes 393224 | tf_op jit(solution)/shard_map/ppermute | solution.py:86
  58.4 1.5 %shard_map.134 = (bf16[1,32,2048]{2,1,0:T(8,128)(2,1)}, f32[8,128]{1,0:T(8,128)S(1)}) custom-call(s32[1,2]{1,0:T(1,128)S(1)} %copy-done.6, f32[8,128]{1,0:T(8,128)S(1)} %get-tuple-element.58.refs_1_, bf16[1,128,2048]{2,1,0:T(8,128)(2,1)S(1)} %copy-done, f32[8,128]{1,0:T(8,128)S(1)} %get-tuple-element.85.refs_3_), custom_call_target="tpu_custom_call" | custom-call | flops 262144 | bytes 1024 | tf_op jit(solution)/shard_map/pallas_call | solution.py:74
  61.1 6.9 %collective-permute-done.14.refs_2_ = bf16[128,512]{1,0:T(8,128)(2,1)S(1)} collective-permute-done((bf16[128,512]{1,0:T(8,128)(2,1)S(1)}, bf16[128,512]{1,0:T(8,128)(2,1)S(1)}, u32[]{:S(2)}, u32[]{:S(2)}) %collective-permute-start.14) | collective-permute-done | bytes 131104 | tf_op jit(solution)/shard_map/ppermute | solution.py:86
  68.2 1.0 %shard_map.137 = (bf16[1,2048,256]{2,1,0:T(8,128)(2,1)}, f32[8,128]{1,0:T(8,128)S(1)}) custom-call(bf16[256,512]{1,0:T(8,128)(2,1)S(1)} %collective-permute-done.20.refs_0_, f32[2048,256]{1,0:T(8,128)S(1)} %get-tuple-element.84.refs_1_, bf16[1,2048,256]{2,1,0:T(8,128)(2,1)} %get-tuple-element.91.refs_2_, ...), custom_call_target="tpu_custom_call", output_to_operand_aliasing={{0}: (2, {})} | custom-call | flops 262144 | bytes 1024 | tf_op jit(solution)/shard_map/pallas_call | solution.py:74
  69.2 1.0 %shard_map.138 = (bf16[1,2048,256]{2,1,0:T(8,128)(2,1)}, f32[8,128]{1,0:T(8,128)S(1)}) custom-call(bf16[256,512]{1,0:T(8,128)(2,1)S(1)} %get-tuple-element.89.refs_0_, f32[2048,256]{1,0:T(8,128)S(1)} %get-tuple-element.84.refs_1_, bf16[1,2048,256]{2,1,0:T(8,128)(2,1)} %get-tuple-element.93.refs_2_, ...), custom_call_target="tpu_custom_call", output_to_operand_aliasing={{0}: (2, {})} | custom-call | flops 262144 | bytes 1024 | tf_op jit(solution)/shard_map/pallas_call | solution.py:74
  (54 shorter events, 13.5 us)
Async XLA Ops:
  0.6 12.7 %copy-start.4 = (f32[2048]{0:T(1024)S(1)}, f32[2048]{0:T(1024)}, u32[]{:S(2)}) copy-start(f32[2048]{0:T(1024)} %param.13) | copy-start | bytes 24580
  2.8 9.9 %collective-permute-start.2 = (bf16[128,512]{1,0:T(8,128)(2,1)S(1)}, bf16[128,512]{1,0:T(8,128)(2,1)S(1)}, u32[]{:S(2)}, u32[]{:S(2)}) collective-permute-start(bf16[128,512]{1,0:T(8,128)(2,1)S(1)} %shard_map.122.refs_0_), channel_id=1, source_target_pairs={{0,24},{8,16},{16,8},{24,0},{1,25},{9,17},{17,9},{25,1},{2,26},{10... | collective-permute-start | bytes 393224 | tf_op jit(solution)/shard_map/ppermute | solution.py:86
  6.7 6.3 %collective-permute-start.1 = (bf16[128,512]{1,0:T(8,128)(2,1)S(1)}, bf16[128,512]{1,0:T(8,128)(2,1)S(1)}, u32[]{:S(2)}, u32[]{:S(2)}) collective-permute-start(bf16[128,512]{1,0:T(8,128)(2,1)S(1)} %shard_map.122.refs_0_), channel_id=1, source_target_pairs={{0,16},{8,24},{16,0},{24,8},{1,17},{9,25},{17,1},{25,9},{2,18},{10... | collective-permute-start | bytes 393224 | tf_op jit(solution)/shard_map/ppermute | solution.py:86
  7.2 6.1 %collective-permute-start = (bf16[128,512]{1,0:T(8,128)(2,1)S(1)}, bf16[128,512]{1,0:T(8,128)(2,1)S(1)}, u32[]{:S(2)}, u32[]{:S(2)}) collective-permute-start(bf16[128,512]{1,0:T(8,128)(2,1)S(1)} %shard_map.122.refs_0_), channel_id=1, source_target_pairs={{0,8},{8,0},{16,24},{24,16},{1,9},{9,1},{17,25},{25,17},{2,10},{10... | collective-permute-start | bytes 393224 | tf_op jit(solution)/shard_map/ppermute | solution.py:86
  14.2 5.8 %collective-permute-start.5 = (f32[8,128]{1,0:T(8,128)S(1)}, f32[8,128]{1,0:T(8,128)S(1)}, u32[]{:S(2)}, u32[]{:S(2)}) collective-permute-start(f32[8,128]{1,0:T(8,128)S(1)} %get-tuple-element.53.after_ref.refs_0_), channel_id=1, source_target_pairs={{0,24},{8,16},{16,8},{24,0},{1,25},{9,17},{17,9},{25,1},{2,26},{10... | collective-permute-start | bytes 12296 | tf_op jit(solution)/shard_map/ppermute | solution.py:86
  16.5 3.6 %collective-permute-start.4 = (f32[8,128]{1,0:T(8,128)S(1)}, f32[8,128]{1,0:T(8,128)S(1)}, u32[]{:S(2)}, u32[]{:S(2)}) collective-permute-start(f32[8,128]{1,0:T(8,128)S(1)} %get-tuple-element.53.after_ref.refs_0_), channel_id=1, source_target_pairs={{0,16},{8,24},{16,0},{24,8},{1,17},{9,25},{17,1},{25,9},{2,18},{10... | collective-permute-start | bytes 12296 | tf_op jit(solution)/shard_map/ppermute | solution.py:86
  17.2 3.6 %collective-permute-start.3 = (f32[8,128]{1,0:T(8,128)S(1)}, f32[8,128]{1,0:T(8,128)S(1)}, u32[]{:S(2)}, u32[]{:S(2)}) collective-permute-start(f32[8,128]{1,0:T(8,128)S(1)} %get-tuple-element.53.after_ref.refs_0_), channel_id=1, source_target_pairs={{0,8},{8,0},{16,24},{24,16},{1,9},{9,1},{17,25},{25,17},{2,10},{10... | collective-permute-start | bytes 12296 | tf_op jit(solution)/shard_map/ppermute | solution.py:86
  21.1 2.3 %collective-permute-start.6 = (bf16[2064,128]{1,0:T(8,128)(2,1)S(1)}, bf16[2064,128]{1,0:T(8,128)(2,1)S(1)}, u32[]{:S(2)}, u32[]{:S(2)}) collective-permute-start(bf16[2064,128]{1,0:T(8,128)(2,1)S(1)} %get-tuple-element.57.refs_2_.refs_1_.refs_0_), channel_id=1, source_target_pairs={{0,1},{1,0},{2,3},{3,2},{4,5},{5,4},{6,7},{7,6},{8,9},{9,8},{10,11... | collective-permute-start | bytes 1585160 | tf_op jit(solution)/shard_map/ppermute | solution.py:86
  25.9 10.6 %collective-permute-start.10 = (bf16[512,256]{1,0:T(8,128)(2,1)S(1)}, bf16[512,256]{1,0:T(8,128)(2,1)S(1)}, u32[]{:S(2)}, u32[]{:S(2)}) collective-permute-start(bf16[512,256]{1,0:T(8,128)(2,1)S(1)} %get-tuple-element.68), channel_id=1, source_target_pairs={{0,24},{8,16},{16,8},{24,0},{1,25},{9,17},{17,9},{25,1},{2,26},{10... | collective-permute-start | bytes 786440 | tf_op jit(solution)/shard_map/ppermute | solution.py:86
  27.3 14.3 %collective-permute-start.11 = (bf16[512,256]{1,0:T(8,128)(2,1)S(1)}, bf16[512,256]{1,0:T(8,128)(2,1)S(1)}, u32[]{:S(2)}, u32[]{:S(2)}) collective-permute-start(bf16[512,256]{1,0:T(8,128)(2,1)S(1)} %get-tuple-element.69), channel_id=1, source_target_pairs={{0,16},{8,24},{16,0},{24,8},{1,17},{9,25},{17,1},{25,9},{2,18},{10... | collective-permute-start | bytes 786440 | tf_op jit(solution)/shard_map/ppermute | solution.py:86
  28.1 13.6 %collective-permute-start.12 = (bf16[512,256]{1,0:T(8,128)(2,1)S(1)}, bf16[512,256]{1,0:T(8,128)(2,1)S(1)}, u32[]{:S(2)}, u32[]{:S(2)}) collective-permute-start(bf16[512,256]{1,0:T(8,128)(2,1)S(1)} %get-tuple-element.70), channel_id=1, source_target_pairs={{0,8},{8,0},{16,24},{24,16},{1,9},{9,1},{17,25},{25,17},{2,10},{10... | collective-permute-start | bytes 786440 | tf_op jit(solution)/shard_map/ppermute | solution.py:86
  34.3 23.1 %copy-start.1 = (bf16[1,2048,256]{2,1,0:T(8,128)(2,1)S(1)}, bf16[1,2048,256]{2,1,0:T(8,128)(2,1)}, u32[]{:S(2)}) copy-start(bf16[1,2048,256]{2,1,0:T(8,128)(2,1)} %refs_0_.6) | copy-start | bytes 3145732
  34.3 24.1 %copy-start.6 = (s32[1,2]{1,0:T(1,128)S(1)}, s32[1,2]{1,0:T(1,128)}, u32[]{:S(2)}) copy-start(s32[1,2]{1,0:T(1,128)} %refs_0_.7) | copy-start | bytes 28
  34.3 13.0 %collective-permute-start.7 = (bf16[512,256]{1,0:T(8,128)(2,1)S(1)}, bf16[512,256]{1,0:T(8,128)(2,1)S(1)}, u32[]{:S(2)}, u32[]{:S(2)}) collective-permute-start(bf16[512,256]{1,0:T(8,128)(2,1)S(1)} %get-tuple-element.64), channel_id=1, source_target_pairs={{0,24},{8,16},{16,8},{24,0},{1,25},{9,17},{17,9},{25,1},{2,26},{10... | collective-permute-start | bytes 786440 | tf_op jit(solution)/shard_map/ppermute | solution.py:86
  35.8 16.6 %collective-permute-start.8 = (bf16[512,256]{1,0:T(8,128)(2,1)S(1)}, bf16[512,256]{1,0:T(8,128)(2,1)S(1)}, u32[]{:S(2)}, u32[]{:S(2)}) collective-permute-start(bf16[512,256]{1,0:T(8,128)(2,1)S(1)} %get-tuple-element.65), channel_id=1, source_target_pairs={{0,16},{8,24},{16,0},{24,8},{1,17},{9,25},{17,1},{25,9},{2,18},{10... | collective-permute-start | bytes 786440 | tf_op jit(solution)/shard_map/ppermute | solution.py:86
  36.5 15.9 %collective-permute-start.9 = (bf16[512,256]{1,0:T(8,128)(2,1)S(1)}, bf16[512,256]{1,0:T(8,128)(2,1)S(1)}, u32[]{:S(2)}, u32[]{:S(2)}) collective-permute-start(bf16[512,256]{1,0:T(8,128)(2,1)S(1)} %get-tuple-element.66), channel_id=1, source_target_pairs={{0,8},{8,0},{16,24},{24,16},{1,9},{9,1},{17,25},{25,17},{2,10},{10... | collective-permute-start | bytes 786440 | tf_op jit(solution)/shard_map/ppermute | solution.py:86
  42.1 14.4 %collective-permute-start.16 = (bf16[128,512]{1,0:T(8,128)(2,1)S(1)}, bf16[128,512]{1,0:T(8,128)(2,1)S(1)}, u32[]{:S(2)}, u32[]{:S(2)}) collective-permute-start(bf16[128,512]{1,0:T(8,128)(2,1)S(1)} %get-tuple-element.78), channel_id=1, source_target_pairs={{0,6},{1,7},{2,4},{3,5},{4,2},{5,3},{6,0},{7,1},{8,14},{9,15},{10,... | collective-permute-start | bytes 393224 | tf_op jit(solution)/shard_map/ppermute | solution.py:86
  45.8 11.5 %collective-permute-start.17 = (bf16[128,512]{1,0:T(8,128)(2,1)S(1)}, bf16[128,512]{1,0:T(8,128)(2,1)S(1)}, u32[]{:S(2)}, u32[]{:S(2)}) collective-permute-start(bf16[128,512]{1,0:T(8,128)(2,1)S(1)} %get-tuple-element.79), channel_id=1, source_target_pairs={{0,4},{1,5},{2,6},{3,7},{4,0},{5,1},{6,2},{7,3},{8,12},{9,13},{10,... | collective-permute-start | bytes 393224 | tf_op jit(solution)/shard_map/ppermute | solution.py:86
  47.3 10.0 %collective-permute-start.18 = (bf16[128,512]{1,0:T(8,128)(2,1)S(1)}, bf16[128,512]{1,0:T(8,128)(2,1)S(1)}, u32[]{:S(2)}, u32[]{:S(2)}) collective-permute-start(bf16[128,512]{1,0:T(8,128)(2,1)S(1)} %get-tuple-element.80), channel_id=1, source_target_pairs={{0,2},{1,3},{2,0},{3,1},{4,6},{5,7},{6,4},{7,5},{8,10},{9,11},{10,... | collective-permute-start | bytes 393224 | tf_op jit(solution)/shard_map/ppermute | solution.py:86
  52.8 8.3 %collective-permute-start.13 = (bf16[128,512]{1,0:T(8,128)(2,1)S(1)}, bf16[128,512]{1,0:T(8,128)(2,1)S(1)}, u32[]{:S(2)}, u32[]{:S(2)}) collective-permute-start(bf16[128,512]{1,0:T(8,128)(2,1)S(1)} %get-tuple-element.74), channel_id=1, source_target_pairs={{0,6},{1,7},{2,4},{3,5},{4,2},{5,3},{6,0},{7,1},{8,14},{9,15},{10,... | collective-permute-start | bytes 393224 | tf_op jit(solution)/shard_map/ppermute | solution.py:86
  56.5 11.6 %collective-permute-start.14 = (bf16[128,512]{1,0:T(8,128)(2,1)S(1)}, bf16[128,512]{1,0:T(8,128)(2,1)S(1)}, u32[]{:S(2)}, u32[]{:S(2)}) collective-permute-start(bf16[128,512]{1,0:T(8,128)(2,1)S(1)} %get-tuple-element.75), channel_id=1, source_target_pairs={{0,4},{1,5},{2,6},{3,7},{4,0},{5,1},{6,2},{7,3},{8,12},{9,13},{10,... | collective-permute-start | bytes 393224 | tf_op jit(solution)/shard_map/ppermute | solution.py:86
  56.5 11.6 %collective-permute-start.15 = (bf16[128,512]{1,0:T(8,128)(2,1)S(1)}, bf16[128,512]{1,0:T(8,128)(2,1)S(1)}, u32[]{:S(2)}, u32[]{:S(2)}) collective-permute-start(bf16[128,512]{1,0:T(8,128)(2,1)S(1)} %get-tuple-element.76), channel_id=1, source_target_pairs={{0,2},{1,3},{2,0},{3,1},{4,6},{5,7},{6,4},{7,5},{8,10},{9,11},{10,... | collective-permute-start | bytes 393224 | tf_op jit(solution)/shard_map/ppermute | solution.py:86
  57.3 10.9 %collective-permute-start.20 = (bf16[256,512]{1,0:T(8,128)(2,1)S(1)}, bf16[256,512]{1,0:T(8,128)(2,1)S(1)}, u32[]{:S(2)}, u32[]{:S(2)}) collective-permute-start(bf16[256,512]{1,0:T(8,128)(2,1)S(1)} %get-tuple-element.90), channel_id=1, source_target_pairs={{0,1},{1,0},{2,3},{3,2},{4,5},{5,4},{6,7},{7,6},{8,9},{9,8},{10,11... | collective-permute-start | bytes 786440 | tf_op jit(solution)/shard_map/ppermute | solution.py:86
  68.1 2.1 %collective-permute-start.19 = (bf16[256,512]{1,0:T(8,128)(2,1)S(1)}, bf16[256,512]{1,0:T(8,128)(2,1)S(1)}, u32[]{:S(2)}, u32[]{:S(2)}) collective-permute-start(bf16[256,512]{1,0:T(8,128)(2,1)S(1)} %get-tuple-element.88), channel_id=1, source_target_pairs={{0,1},{1,0},{2,3},{3,2},{4,5},{5,4},{6,7},{7,6},{8,9},{9,8},{10,11... | collective-permute-start | bytes 786440 | tf_op jit(solution)/shard_map/ppermute | solution.py:86
  (6 other events, 11.0 us)
